TPU v7x, 32 devices: a whole 2x2x4 slice. The times are simulated.
32 devices in a mesh: rep: 16 (over z, y, core), shard: 2 (over x).
Axes of the slice: x: 2, y: 2, z: 4, core: 2. Of those that a mesh axis runs over, the one named last changes fastest.
Arguments:
- prompt_in: bfloat16 [2, 16, 1024, 1024], P(None, 'rep', 'shard'), may hold values from -6 to 6
- cont_in: bfloat16 [2, 16, 2, 128, 1024], P(None, 'rep', 'shard'), may hold values from -6 to 6
- prompt_cot: bfloat16 [2, 16, 1024, 1024], P(None, 'rep', 'shard'), may hold values from -6 to 6
- cont_cot: bfloat16 [2, 16, 2, 128, 1024], P(None, 'rep', 'shard'), may hold values from -6 to 6
- ln1_gain: bfloat16 [1024], P('shard'), may hold values from 0.099609375 to 1.8984375
- ln1_bias: bfloat16 [1024], P('shard'), may hold values from -3 to 3
- ln2_gain: bfloat16 [1024], P('shard'), may hold values from 0.099609375 to 1.8984375
- ln2_bias: bfloat16 [1024], P('shard'), may hold values from -3 to 3
- qkv_weight: bfloat16 [1024, 3072], P('shard'), may hold values from -0.25 to 0.25
- qkv_bias: bfloat16 [3072], P('shard'), may hold values from -3 to 3
- out_weight: bfloat16 [1024, 1024], P('shard'), may hold values from -0.75 to 0.75
- out_bias: bfloat16 [1024], P('shard'), may hold values from -3 to 3
- up_weight: bfloat16 [1024, 4096], P('shard'), may hold values from -0.1875 to 0.1875
- up_bias: bfloat16 [4096], P('shard'), may hold values from -3 to 3
- down_weight: bfloat16 [4096, 1024], P('shard'), may hold values from -0.09375 to 0.09375
- down_bias: bfloat16 [1024], P('shard'), may hold values from -3 to 3
Outputs:
- prompt_out: bfloat16 [2, 16, 1024, 1024], P(None, 'rep', 'shard')
- cont_out: bfloat16 [2, 16, 2, 128, 1024], P(None, 'rep', 'shard')
- prompt_grad: float32 [2, 16, 1024, 1024], P(None, 'rep', 'shard')
- cont_grad: float32 [2, 16, 2, 128, 1024], P(None, 'rep', 'shard')
- ln1_gain_grad: float32 [1024], P('shard')
- ln1_bias_grad: float32 [1024], P('shard')
- ln2_gain_grad: float32 [1024], P('shard')
- ln2_bias_grad: float32 [1024], P('shard')
- qkv_weight_grad: float32 [1024, 3072], P('shard')
- qkv_bias_grad: float32 [3072], P('shard')
- out_weight_grad: float32 [1024, 1024], P('shard')
- out_bias_grad: float32 [1024], P('shard')
- up_weight_grad: float32 [1024, 4096], P('shard')
- up_bias_grad: float32 [4096], P('shard')
- down_weight_grad: float32 [4096, 1024], P('shard')
- down_bias_grad: float32 [1024], P('shard')
All inputs are finite; a program needn't handle non-finite values.
Results may differ from a plain program's by a relative error of at most 0.018.
Values may be sent and summed in bfloat16 or wider, within the bound.
No kernel may reach another device: no remote copies, remote signals or barrier semaphores. Data moves between devices by JAX's collectives and lax.ppermute only.
A program may use at most 448 MiB of HBM per device.

v0:
```python
import functools
import math

import jax
import jax.numpy as jnp
import numpy as np
from jax import lax
from jax.experimental import pallas as pl
from jax.experimental.pallas import tpu as pltpu
from jax.sharding import PartitionSpec as P

H = 16
HD = 64
ROT = 16
EPS = 1e-05
F32 = jnp.float32
BF = jnp.bfloat16
MIB = 1024 * 1024
SD = jax.ShapeDtypeStruct
SMALL = pl.CostEstimate(flops=1000000, bytes_accessed=100000, transcendentals=0)


def dnn(a, b):
    return lax.dot_general(a, b, (((1,), (0,)), ((), ())), preferred_element_type=F32)


def dnt(a, b):
    return lax.dot_general(a, b, (((1,), (1,)), ((), ())), preferred_element_type=F32)


def dtn(a, b):
    return lax.dot_general(a, b, (((0,), (0,)), ((), ())), preferred_element_type=F32)


def normed(rows):
    x = rows.astype(F32)
    c = x - jnp.mean(x, axis=-1, keepdims=True)
    inv = lax.rsqrt(jnp.mean(c * c, axis=-1, keepdims=True) + EPS)
    return c * inv, inv


def tile(i, n):
    return pl.ds(pl.multiple_of(i * n, n), n)


def rows_tile(n, most):
    t = most
    while n % t:
        t -= 8
    return t


def mlp_kernel(rt, x_ref, dy_ref, wu_ref, bu_ref, wd_ref, gb_ref, act_ref, dpre_ref, h_ref, bu_out, *back):
    f = pl.program_id(0)
    if back:
        yp_ref, g2_ref, ln_ref, yacc, dacc = back
    last = pl.num_programs(0) - 1
    rows = x_ref.shape[0]

    @pl.when(f == 0)
    def _():
        @pl.loop(0, rows // 128)
        def _(i):
            r = tile(i, 128)
            xh, _ = normed(x_ref[r, :])
            h_ref[r, :] = (xh * gb_ref[0:1, :] + gb_ref[1:2, :]).astype(BF)
            if back:
                yacc[r, :] = jnp.zeros((128, yacc.shape[1]), F32)
                dacc[r, :] = jnp.zeros((128, dacc.shape[1]), F32)

    def step(i, bsum):
        r = tile(i, rt)
        pre = dnn(h_ref[r, :], wu_ref[...]) + bu_ref[...]
        da = dnt(dy_ref[r, :], wd_ref[...])
        cdf = 0.5 * (1.0 + lax.erf(pre * 0.7071067811865476))
        act = (pre * cdf).astype(BF)
        dpre = (da * (cdf + pre * jnp.exp(-0.5 * pre * pre) * 0.3989422804014327)).astype(BF)
        act_ref[r, :] = act
        dpre_ref[r, :] = dpre
        if back:
            yacc[r, :] += dnn(act, wd_ref[...])
            dacc[r, :] += dnt(dpre, wu_ref[...])
        return bsum + jnp.sum(dpre.astype(F32), axis=0, keepdims=True)

    bu_out[...] = lax.fori_loop(0, rows // rt, step, jnp.zeros(bu_out.shape, F32))
    if not back:
        return

    @pl.when(f == last)
    def _():
        ln_ref[...] = jnp.zeros_like(ln_ref)

        @pl.loop(0, rows // 128)
        def _(i):
            r = tile(i, 128)
            xh, _ = normed(x_ref[r, :])
            dh = dacc[r, :]
            yp_ref[r, :] = yacc[r, :].astype(BF)
            g2_ref[r, :] = (dh * gb_ref[0:1, :]).astype(BF)
            ln_ref[0:1, :] += jnp.sum(dh * xh, axis=0, keepdims=True)
            ln_ref[1:2, :] += jnp.sum(dh, axis=0, keepdims=True)


def mlp_rows(x, dy, wu, bu, wd, gb, back):
    rows, width = x.shape
    hidden = wu.shape[1]
    fb = min(512, hidden)
    full = lambda s: pl.BlockSpec(s, lambda f: (0,) * len(s))
    return pl.pallas_call(
        functools.partial(mlp_kernel, rows_tile(rows, 640)),
        grid=(hidden // fb,),
        in_specs=[
            full((rows, width)),
            full((rows, width)),
            pl.BlockSpec((width, fb), lambda f: (0, f)),
            pl.BlockSpec((1, fb), lambda f: (0, f)),
            pl.BlockSpec((fb, width), lambda f: (f, 0)),
            full((2, width)),
        ],
        out_specs=[
            pl.BlockSpec((rows, fb), lambda f: (0, f)),
            pl.BlockSpec((rows, fb), lambda f: (0, f)),
            full((rows, width)),
            pl.BlockSpec((1, fb), lambda f: (0, f)),
        ]
        + [full((rows, width)), full((rows, width)), full((2, width))] * back,
        out_shape=[SD((rows, hidden), BF), SD((rows, hidden), BF), SD((rows, width), BF), SD((1, hidden), F32)]
        + [SD((rows, width), BF), SD((rows, width), BF), SD((2, width), F32)] * back,
        scratch_shapes=[pltpu.VMEM((rows, width), F32)] * (2 * back),
        compiler_params=pltpu.CompilerParams(vmem_limit_bytes=60 * MIB),
        cost_estimate=SMALL,
    )(x, dy, wu, bu, wd, gb)


def roll8(x, left):
    w = x.shape[-1]
    return pltpu.roll(x, (w - 8) if left else 8, 1)


def attn_kernel(S, PD, CL, QB, HG, adding, me_ref, *refs):
    it = iter(refs)
    take = lambda n: [next(it) for _ in range(n)]
    stacked = S > 2
    per = 1 if stacked else S
    xs = take(per)
    dys = take(per)
    far = 1 if stacked else S - 1
    yps = take(far * adding)
    g2s = take(far * adding)
    wq, wk, wv = take(3)
    bq, bk, bv = take(3)
    wo, gb = take(2)
    cr, s1r, s2r = take(3)
    ys = take(far)
    gs = take(far)
    dl, ctx, h1, ln, db = take(5)
    yacc, dacc, q_s, k_s, v_s, dc_s, kT, vT, dk_s, dv_s = take(10)
    g = pl.program_id(0)
    last = pl.num_programs(0) - 1
    me = me_ref[0]
    N = xs[0].shape[-2]
    T = N * S
    PR = PD * S
    CR = N - PD
    W = HG * HD

    def every_slot(fn, start=0):
        if stacked:

            @pl.loop(start, S)
            def _(j):
                fn(j, lambda refs: refs[0].at[j], lambda refs: refs[0].at[j - 1])

        else:
            for j in range(start, S):
                fn(j, lambda refs: refs[j], lambda refs: refs[j - 1])

    def slot_rows(start, n):
        if start < PR:
            s, off = start // PD, start % PD
        else:
            s, off = (start - PR) // CR, PD + (start - PR) % CR
        return pl.ds(pl.multiple_of(lax.rem(s - me + S, S) * N + off, 128), n)

    def pieces(start, n):
        step = min(n, PD if start < PR else CR)
        return [(i, step) for i in range(0, n, step)]

    @pl.when(g == 0)
    def _():
        def load(j, of, away):
            x = of(xs)

            @pl.loop(0, N // 128)
            def _(i):
                xh, _ = normed(x[tile(i, 128), :])
                h1[pl.ds(pl.multiple_of(j * N + i * 128, 128), 128), :] = (xh * gb[0:1, :] + gb[1:2, :]).astype(BF)

        every_slot(load)

    def rot(y, r, scale):
        c = cr[r, :]
        s1 = s1r[r, :]
        s2 = s2r[r, :]
        out = []
        for p in range(W // 128):
            z = y[:, p * 128 : (p + 1) * 128]
            z = (z * c + roll8(z, True) * s1 + roll8(z, False) * s2).astype(BF)
            out.append(z * jnp.asarray(scale, BF) if scale != 1.0 else z)
        return jnp.concatenate(out, axis=1) if len(out) > 1 else out[0]

    def proj(j, of, away):
        s = lax.rem(me + j, S)
        rp = pl.ds(pl.multiple_of(s * PD, 128), PD)
        rc = pl.ds(pl.multiple_of(PR + s * CR, 128), CR)
        hh = h1[pl.ds(pl.multiple_of(j * N, 128), N), :]
        y = dnn(hh, wq[...]) + bq[...]
        q_s[rp, :] = rot(y[:PD], rp, HD**-0.5)
        q_s[rc, :] = rot(y[PD:], rc, HD**-0.5)
        y = dnn(hh, wk[...]) + bk[...]
        k_s[rp, :] = rot(y[:PD], rp, 1.0)
        k_s[rc, :] = rot(y[PD:], rc, 1.0)
        y = (dnn(hh, wv[...]) + bv[...]).astype(BF)
        v_s[rp, :] = y[:PD]
        v_s[rc, :] = y[PD:]
        y = dnt(of(dys)[...], wo[...]).astype(BF)
        dc_s[rp, :] = y[:PD]
        dc_s[rc, :] = y[PD:]

    def bring(j, of, away):
        nb = away(yps).shape[0]
        r = pl.ds(pl.multiple_of(g * nb, 16), nb)
        away(ys)[r, :] = away(yps)[...]
        away(gs)[r, :] = away(g2s)[...]

    every_slot(proj)
    if adding:
        every_slot(bring, 1)
    lane = lax.broadcasted_iota(jnp.int32, (1, 128), 1)
    row_i = lax.broadcasted_iota(jnp.int32, (QB, QB), 0)
    col_i = lax.broadcasted_iota(jnp.int32, (QB, QB), 1)
    causal = row_i <= col_i
    cmask = causal & ((row_i // CL) == (col_i // CL))
    blocks = []
    for i in range(PR // QB):
        blocks.append((i * QB, [(0, i * QB, None)] * (i > 0) + [(i * QB, QB, causal)]))
    for c in range((T - PR) // QB):
        blocks.append((PR + c * QB, [(0, PR, None), (PR + c * QB, QB, cmask)]))

    @pl.loop(0, W // 128)
    def _(p):
        lanes = tile(p, 128)
        kT[...] = k_s[:, lanes].T
        vT[...] = v_s[:, lanes].T
        dk_s[...] = jnp.zeros_like(dk_s)
        dv_s[...] = jnp.zeros_like(dv_s)
        def begin(q0, parts):
            qb = q_s[pl.ds(q0, QB), lanes]
            dcb = dc_s[pl.ds(q0, QB), lanes]
            out = []
            for h in range(2):
                sel = (lane >= HD * h) & (lane < HD * h + HD)
                qm = jnp.where(sel, qb, jnp.zeros_like(qb))
                dm = jnp.where(sel, dcb, jnp.zeros_like(dcb))
                ss = []
                for k0, n, mask in parts:
                    s = dnt(k_s[k0 : k0 + n, lanes], qm)
                    ss.append(s if mask is None else jnp.where(mask, s, -1e30))
                out.append((qm, dm, ss, [dnt(v_s[k0 : k0 + n, lanes], dm) for k0, n, _ in parts]))
            return out

        ahead = begin(*blocks[0])
        for b, (q0, parts) in enumerate(blocks):
            now = ahead
            if b + 1 < len(blocks):
                ahead = begin(*blocks[b + 1])
            rq = pl.ds(q0, QB)
            P_, DS, cT, dqT = [], [], [], []
            qh = [t[0] for t in now]
            dch = [t[1] for t in now]
            for h in range(2):
                _, _, ss, dps = now[h]
                m = functools.reduce(jnp.maximum, [jnp.max(s, axis=0, keepdims=True) for s in ss])
                es = [jnp.exp(s - m) for s in ss]
                rl = 1.0 / sum(jnp.sum(e, axis=0, keepdims=True) for e in es)
                ps = [e * rl for e in es]
                delta = sum(jnp.sum(a * b, axis=0, keepdims=True) for a, b in zip(ps, dps))
                P_.append([a.astype(BF) for a in ps])
                DS.append([(a * (b - delta)).astype(BF) for a, b in zip(ps, dps)])
                hr = slice(HD * h, HD * h + HD)
                cT.append(sum(dnn(vT[hr, k0 : k0 + n], a) for (k0, n, _), a in zip(parts, P_[h])))
                dqT.append(sum(dnn(kT[hr, k0 : k0 + n], a) for (k0, n, _), a in zip(parts, DS[h])))
            q2 = jnp.concatenate(qh, axis=0)
            dc2 = jnp.concatenate(dch, axis=0)
            for i, (k0, n, _) in enumerate(parts):
                dv_s[k0 : k0 + n, :] += dnn(jnp.concatenate([P_[0][i], P_[1][i]], axis=1), dc2)
                dk_s[k0 : k0 + n, :] += dnn(jnp.concatenate([DS[0][i], DS[1][i]], axis=1), q2)
            co = jnp.concatenate(cT, axis=0).T.astype(BF)
            z = jnp.concatenate(dqT, axis=0).T * (HD**-0.5)
            z = (z * cr[rq, :] - roll8(z, True) * s1r[rq, :] - roll8(z, False) * s2r[rq, :]).astype(BF)
            for o, n in pieces(q0, QB):
                ctx[slot_rows(q0 + o, n), lanes] = co[o : o + n]
                dl[0, slot_rows(q0 + o, n), lanes] = z[o : o + n]

        @pl.loop(0, S)
        def _(s):
            to = lax.rem(s - me + S, S) * N
            for src, off, n in ((s * PD, 0, PD), (PR + s * CR, PD, CR)):
                r = pl.ds(pl.multiple_of(src, 128), n)
                w = pl.ds(pl.multiple_of(to + off, 128), n)
                z = dk_s[r, :]
                z = z * cr[r, :] - roll8(z, True) * s1r[r, :] - roll8(z, False) * s2r[r, :]
                dl[1, w, lanes] = z.astype(BF)
                dl[2, w, lanes] = dv_s[r, :].astype(BF)

    for c in range(3):
        db[c : c + 1, :] = jnp.sum(dl[c].astype(F32), axis=0, keepdims=True)

    @pl.loop(1, S)
    def _(j):
        r = pl.ds(pl.multiple_of(j * N, 128), N)
        w = pl.ds(pl.multiple_of((j - 1) * N, 128), N)
        y = dnn(ctx[r, :], wo[...])
        d = dnt(dl[0, r, :], wq[...]) + dnt(dl[1, r, :], wk[...]) + dnt(dl[2, r, :], wv[...])

        @pl.when(g == 0)
        def _():
            yacc[w, :] = y
            dacc[w, :] = d

        @pl.when(g > 0)
        def _():
            yacc[w, :] += y
            dacc[w, :] += d

    @pl.when(g == last)
    def _():
        ln[...] = jnp.zeros_like(ln)

        def store(j, of, away):
            x, yo, go = of(xs), away(ys), away(gs)

            @pl.loop(0, N // 128)
            def _(i):
                r = tile(i, 128)
                w = pl.ds(pl.multiple_of((j - 1) * N + i * 128, 128), 128)
                xh, _ = normed(x[r, :])
                d = dacc[w, :]
                y = yacc[w, :]
                gg = d * gb[0:1, :]
                if adding:
                    y = y + yo[r, :].astype(F32)
                    gg = gg + go[r, :].astype(F32)
                yo[r, :] = y.astype(BF)
                go[r, :] = gg.astype(BF)
                ln[0:1, :] += jnp.sum(d * xh, axis=0, keepdims=True)
                ln[1:2, :] += jnp.sum(d, axis=0, keepdims=True)

        every_slot(store, 1)


def attn_group(S, PD, CL, me, xs, dys, yps, g2s, wqkv, bqkv, wo, gb, tabs):
    N, D = xs[0].shape
    CW = wo.shape[0]
    T = N * S
    HG = 4 if CW % 256 == 0 else 2
    QB = 256
    W = HG * HD
    G = CW // W
    full = lambda s: pl.BlockSpec(s, lambda g, m: (0,) * len(s), pipeline_mode=pl.Buffered(1))
    keep = lambda s: pl.BlockSpec(s, lambda g, m: (0,) * len(s))
    tok, tok_out, per, far = full((N, D)), keep((N, D)), S, S - 1
    adding = int(T * D <= 1536 * 1024)
    others = (yps, g2s)
    if not adding:
        yps, g2s = [], []
    out_tok = SD((N, D), BF)
    part = pl.BlockSpec((N // G, D), lambda g, m: (g, 0))
    if S > 2:
        xs, dys, yps, g2s = [[jnp.stack(v, axis=0)] if v else v for v in (xs, dys, yps, g2s)]
        tok, tok_out, per, far = full((S, N, D)), keep((S - 1, N, D)), 1, 1
        out_tok = SD((S - 1, N, D), BF)
        part = pl.BlockSpec((S - 1, N // G, D), lambda g, m: (0, g, 0))
    wspec = lambda c: pl.BlockSpec((D, W), lambda g, m: (0, c * G + g))
    bspec = lambda c: pl.BlockSpec((1, W), lambda g, m: (0, c * G + g))
    outs = pl.pallas_call(
        functools.partial(attn_kernel, S, PD, CL, QB, HG, adding),
        grid_spec=pltpu.PrefetchScalarGridSpec(
            num_scalar_prefetch=1,
            grid=(G,),
            in_specs=[tok] * (2 * per)
            + [part] * (2 * adding * far)
            + [wspec(0), wspec(1), wspec(2), bspec(0), bspec(1), bspec(2)]
            + [pl.BlockSpec((W, D), lambda g, m: (g, 0)), full((2, D))]
            + [full((T, 128))] * 3,
            out_specs=[tok_out] * (2 * far)
            + [
                pl.BlockSpec((3, T, W), lambda g, m: (0, 0, g)),
                pl.BlockSpec((T, W), lambda g, m: (0, g)),
                keep((T, D)),
                keep((2, D)),
                pl.BlockSpec((3, W), lambda g, m: (0, g)),
            ],
            scratch_shapes=[pltpu.VMEM((T - N, D), F32)] * 2
            + [pltpu.VMEM((T, W), BF)] * 4
            + [pltpu.VMEM((128, T), BF)] * 2
            + [pltpu.VMEM((T, 128), F32)] * 2,
        ),
        out_shape=[out_tok] * (2 * far)
        + [SD((3, T, CW), BF), SD((T, CW), BF), SD((T, D), BF), SD((2, D), F32), SD((3, CW), F32)],
        compiler_params=pltpu.CompilerParams(vmem_limit_bytes=62 * MIB),
        cost_estimate=SMALL,
    )(me, *xs, *dys, *yps, *g2s, wqkv, wqkv, wqkv, bqkv, bqkv, bqkv, wo, gb, *tabs)
    ys, gs = outs[:far], outs[far : 2 * far]
    if S > 2:
        ys, gs = [[v[0][j] for j in range(S - 1)] for v in (ys, gs)]
    if not adding:
        ys, gs = [[a + b for a, b in zip(p, q)] for p, q in zip((ys, gs), others)]
    return ys, gs, outs[2 * far :]


def tn_kernel(n, wide, *refs):
    a = refs[:n]
    b = refs[n : 2 * n]
    o = refs[2 * n]
    if wide == 0:
        o[...] = sum(dtn(x[...], y[...]) for x, y in zip(a, b)).astype(BF)
    else:
        w = b[0].shape[2]
        for c in range(wide):
            o[:, c * w : (c + 1) * w] = sum(dtn(x[...], y[c]) for x, y in zip(a, b)).astype(BF)


def tn_sum(a, b, block):
    n = len(a)
    rows, da = a[0].shape
    block = min(block, da)
    wide = b[0].shape[0] if b[0].ndim == 3 else 0
    db = b[0].shape[-1] * max(wide, 1)
    keep = lambda s: pl.BlockSpec(s, lambda i: (0,) * len(s), pipeline_mode=pl.Buffered(1))
    return pl.pallas_call(
        functools.partial(tn_kernel, n, wide),
        grid=(da // block,),
        in_specs=[pl.BlockSpec((rows, block), lambda i: (0, i))] * n + [keep(b[0].shape)] * n,
        out_specs=pl.BlockSpec((block, db), lambda i: (i, 0)),
        out_shape=SD((da, db), BF),
        compiler_params=pltpu.CompilerParams(vmem_limit_bytes=60 * MIB),
        cost_estimate=SMALL,
    )(*a, *b)


def joined(refs):
    return jnp.concatenate([r[...] for r in refs], axis=0)


def down_kernel(n, more, *refs):
    o = refs[-1]
    t = dtn(joined(refs[:n]), joined(refs[n : 2 * n])).reshape(o.shape)
    o[...] = (t + refs[2 * n][...].astype(F32) if more else t).astype(BF)


def up_kernel(n, more, *refs):
    o = refs[-1]
    c, rows, w = o.shape
    t = dtn(joined(refs[:n]), joined(refs[n : 2 * n]))
    k = t.shape[1] // w
    for i in range(k):
        r = slice(i * (rows // k), (i + 1) * (rows // k))
        p = t[:, i * w : (i + 1) * w].reshape(c, rows // k, w)
        o[:, r, :] = (p + refs[2 * n][:, r, :].astype(F32) if more else p).astype(BF)


def mlp_grads(S, R, acts, dys, hs, dpres, g=None):
    n = len(acts)
    rows, FL = acts[0].shape
    D = dys[0].shape[1]
    DR = D // S
    blk = 256
    rd = FL // R
    ru = DR // R
    k = FL // D
    per = rd + S * ru * k
    keep = lambda s: pl.BlockSpec(s, lambda i: (0,) * len(s), pipeline_mode=pl.Buffered(1))
    steps = DR // blk
    more = g is not None
    hbm = pl.BlockSpec(memory_space=pl.ANY)

    def call(kernel, a, b, spec, g):
        width = b[0].shape[1]
        prior = [] if g is None else [g]
        return pl.pallas_call(
            functools.partial(kernel, n, more),
            grid=(a[0].shape[1] // blk,),
            in_specs=[pl.BlockSpec((rows, blk), lambda i: (0, i))] * n
            + [keep((rows, width))] * n
            + ([spec if more else hbm] if prior else []),
            out_specs=spec,
            out_shape=SD((R, per, D), BF),
            input_output_aliases={2 * n: 0} if prior else {},
            compiler_params=pltpu.CompilerParams(vmem_limit_bytes=60 * MIB),
            cost_estimate=SMALL,
        )(*a, *b, *prior)

    g = call(down_kernel, acts, dys, pl.BlockSpec((blk // rd, rd, D), lambda i: (i, 0, 0)), g)
    spec = pl.BlockSpec((blk // ru, ru * k, D), lambda i: (i % steps, rd // (ru * k) + i // steps, 0))
    return call(up_kernel, hs, dpres, spec, g)


def mlp_finish_kernel(S, rd, ru, g, down, up):
    n, per, D = g.shape
    k = (per - rd) // (S * ru)
    for c in range(n):
        down[c * rd : (c + 1) * rd, :] = g[c, :rd, :].astype(F32)
        for t in range(S * k):
            a = rd + t * ru
            up[c * ru : (c + 1) * ru, t * D : (t + 1) * D] = g[c, a : a + ru, :].astype(F32)


def mlp_finish(S, g, FL):
    R, per, D = g.shape
    rd = FL // R
    ru = D // S // R
    n = 4
    return pl.pallas_call(
        functools.partial(mlp_finish_kernel, S, rd, ru),
        grid=(R // n,),
        in_specs=[pl.BlockSpec((n, per, D), lambda c: (c, 0, 0))],
        out_specs=[pl.BlockSpec((n * rd, D), lambda c: (c, 0)), pl.BlockSpec((n * ru, S * FL), lambda c: (c, 0))],
        out_shape=[SD((FL, D), F32), SD((D // S, S * FL), F32)],
        compiler_params=pltpu.CompilerParams(vmem_limit_bytes=40 * MIB),
        cost_estimate=SMALL,
    )(g)


def attn_grads_kernel(n, S, R, q_ref, *refs):
    h = refs[:n]
    dl = refs[n : 2 * n]
    ctx = refs[2 * n : 3 * n]
    dy = refs[3 * n : -2]
    first, second = refs[-2:-1], refs[-1:]
    i = pl.program_id(0)
    q1 = q_ref[0]
    q2 = q_ref[1]
    blk = h[0].shape[1]
    D = dy[0].shape[1]
    DR = D // S
    CW = dl[0].shape[2]
    ru = DR // R
    k = D // CW
    steps = DR // blk
    s = i // steps
    base = (i % steps) * (blk // ru)

    def put(pair, pos, rows, v):
        pair[0][pos, rows, :] = v

    for p in range(3):
        t = dtn(joined(h), jnp.concatenate([y[p] for y in dl], axis=0)).astype(BF)
        for c in range(blk // ru):
            v = t[c * ru : (c + 1) * ru, :]
            if p < 2:
                put(first, (base + c) ^ q1, pl.ds(s * 2 * ru + p * ru, ru), v)
            else:
                put(second, (base + c) ^ q2, pl.ds(k * ru + s * ru, ru), v)
    t = dtn(joined(ctx), joined(dy)).astype(BF)
    m = ctx[0].shape[1] // ru
    for c in range(m):
        for j in range(k):
            put(second, (i * m + c) ^ q2, pl.ds(j * ru, ru), t[c * ru : (c + 1) * ru, j * CW : (j + 1) * CW])


def attn_grads(S, R, q, hs, dls, ctxs, dys):
    n = len(hs)
    T, D = hs[0].shape
    CW = ctxs[0].shape[1]
    DR = D // S
    ru = DR // R
    blk = 256
    G = D // blk
    keep = lambda s: pl.BlockSpec(s, lambda i, q: (0,) * len(s), pipeline_mode=pl.Buffered(1))
    shapes = [(R, S * 2 * ru, CW), (R, (D // CW + S) * ru, CW)]
    return pl.pallas_call(
        functools.partial(attn_grads_kernel, n, S, R),
        grid_spec=pltpu.PrefetchScalarGridSpec(
            num_scalar_prefetch=1,
            grid=(G,),
            in_specs=[pl.BlockSpec((T, blk), lambda i, q: (0, i))] * n
            + [keep((3, T, CW))] * n
            + [pl.BlockSpec((T, CW // G), lambda i, q: (0, i))] * n
            + [keep(dys[0].shape)] * len(dys),
            out_specs=[pl.BlockSpec(s, lambda i, q: (0, 0, 0)) for s in shapes],
        ),
        out_shape=[SD(s, BF) for s in shapes],
        compiler_params=pltpu.CompilerParams(vmem_limit_bytes=60 * MIB),
        cost_estimate=SMALL,
    )(q, *hs, *dls, *ctxs, *dys)


def attn_finish_kernel(S, ru, k, n, half, q_ref, *refs):
    out, qkv = refs[4 * n :]
    CW = refs[0].shape[2]
    D = out.shape[1]
    i = pl.program_id(0)

    def piece(which, c, a):
        low, high = refs[2 * which * n + c], refs[(2 * which + 1) * n + c]
        here = ((i * n + c) ^ q_ref[which]) < half
        rows = pl.ds(a, ru)
        return jnp.where(here, low[0, rows, :].astype(F32), high[0, rows, :].astype(F32))

    for c in range(n):
        r = slice(c * ru, (c + 1) * ru)
        for j in range(k):
            out[r, j * CW : (j + 1) * CW] = piece(1, c, j * ru)
        for t in range(S):
            for p in range(3):
                v = piece(0, c, (t * 2 + p) * ru) if p < 2 else piece(1, c, (k + t) * ru)
                qkv[r, p * D + t * CW : p * D + (t + 1) * CW] = v


def attn_finish(S, q, one, two):
    half, per1, CW = one[0].shape
    per2 = two[0].shape[1]
    R = 2 * half
    D = CW * S
    ru = D // S // R
    n = 4
    place_of = lambda i, q, k, c: (i * n + c) ^ q[k]
    low = lambda per, k, c: pl.BlockSpec((1, per, CW), lambda i, q: (jnp.minimum(place_of(i, q, k, c), half - 1), 0, 0))
    high = lambda per, k, c: pl.BlockSpec((1, per, CW), lambda i, q: (jnp.maximum(place_of(i, q, k, c) - half, 0), 0, 0))
    specs = [f(per, k, c) for k, per in ((0, per1), (1, per2)) for f in (low, high) for c in range(n)]
    return pl.pallas_call(
        functools.partial(attn_finish_kernel, S, ru, S, n, half),
        grid_spec=pltpu.PrefetchScalarGridSpec(
            num_scalar_prefetch=1,
            grid=(R // n,),
            in_specs=specs,
            out_specs=[pl.BlockSpec((n * ru, D), lambda c, q: (c, 0)), pl.BlockSpec((n * ru, 3 * D), lambda c, q: (c, 0))],
        ),
        out_shape=[SD((CW, D), F32), SD((D // S, 3 * D), F32)],
        compiler_params=pltpu.CompilerParams(vmem_limit_bytes=40 * MIB),
        cost_estimate=SMALL,
    )(q, *[a for pair in (one, two) for arr in pair for a in [arr] * n])


def own_kernel(dl, ctx, wqkv, wo, x, yp, g2, gb, y, g, ln, d1):
    N = x.shape[0]
    CW = ctx.shape[1]
    d1[...] = sum(dnt(dl[p], wqkv[:, p * CW : (p + 1) * CW]) for p in range(3))
    y[...] = (yp[...].astype(F32) + dnn(ctx[...], wo[...])).astype(BF)
    ln[...] = jnp.zeros_like(ln)

    @pl.loop(0, N // 128)
    def _(i):
        r = tile(i, 128)
        xh, _ = normed(x[r, :])
        a = d1[r, :]
        g[r, :] = (a * gb[0:1, :] + g2[r, :].astype(F32)).astype(BF)
        ln[0:1, :] += jnp.sum(a * xh, axis=0, keepdims=True)
        ln[1:2, :] += jnp.sum(a, axis=0, keepdims=True)


def own_rows(x, yp, g2, dl, ctx, wqkv, wo, gb):
    N, D = x.shape
    CW = wo.shape[0]
    full = lambda s: pl.BlockSpec(s, lambda f: (0,) * len(s))
    return pl.pallas_call(
        own_kernel,
        grid=(1,),
        in_specs=[full((3, N, CW)), full((N, CW)), full((D, 3 * CW)), full((CW, D))] + [full((N, D))] * 3 + [full((2, D))],
        out_specs=[full((N, D)), full((N, D)), full((2, D))],
        out_shape=[SD((N, D), BF), SD((N, D), BF), SD((2, D), F32)],
        scratch_shapes=[pltpu.VMEM((N, D), F32)],
        compiler_params=pltpu.CompilerParams(vmem_limit_bytes=60 * MIB),
        cost_estimate=SMALL,
    )(dl, ctx, wqkv, wo, x, yp, g2, gb)


def final_kernel(S, first, PT, *refs):
    it = iter(refs)
    take = lambda n: [next(it) for _ in range(n)]
    x, dy = take(2)
    ys = take(S)
    gs = take(S)
    (vb,) = take(1)
    if not first:
        take(4)
    po, co, pg, cg = take(4)
    i = pl.program_id(0)
    xv = x[...].astype(F32)
    xh, inv = normed(xv)
    y = xv + vb[0:1, :] + sum(r[...].astype(F32) for r in ys) + vb[1:2, :]
    gsum = sum(r[...].astype(F32) for r in gs)
    dx = (gsum - jnp.mean(gsum, axis=-1, keepdims=True) - xh * jnp.mean(gsum * xh, axis=-1, keepdims=True)) * inv
    out = y.astype(BF)
    grad = dy[...].astype(F32) + dx

    @pl.when(i < PT)
    def _():
        po[0] = out
        pg[0] = grad

    @pl.when(i >= PT)
    def _():
        co[0] = out
        cg[0] = grad


def final_rows(m, MB, PD, x, dy, ys, gs, vb, prior):
    S = len(ys)
    N, D = x.shape
    CR = N - PD
    RT = 128
    PT = PD // RT
    first = prior is None
    row = pl.BlockSpec((RT, D), lambda i: (i, 0))
    pspec = pl.BlockSpec((1, RT, D), lambda i: (m, jnp.minimum(i, PT - 1), 0))
    cspec = pl.BlockSpec((1, RT, D), lambda i: (m, jnp.maximum(i - PT, 0), 0))
    hbm = pl.BlockSpec(memory_space=pl.ANY)
    n_in = 2 * S + 3
    return pl.pallas_call(
        functools.partial(final_kernel, S, first, PT),
        grid=(N // RT,),
        in_specs=[row] * (2 * S + 2) + [pl.BlockSpec((2, D), lambda i: (0, 0))] + ([] if first else [hbm] * 4),
        out_specs=[pspec, cspec, pspec, cspec],
        out_shape=[SD((MB, PD, D), BF), SD((MB, CR, D), BF), SD((MB, PD, D), F32), SD((MB, CR, D), F32)],
        input_output_aliases={} if first else {n_in + k: k for k in range(4)},
        compiler_params=pltpu.CompilerParams(vmem_limit_bytes=32 * MIB),
        cost_estimate=SMALL,
    )(x, dy, *ys, *gs, vb, *(() if first else prior))


def shifted(value, S, j):
    return lax.ppermute(value, "shard", [(i, (i + j) % S) for i in range(S)])


def canonical(slots, me, S, back):
    if S == 1:
        return slots
    if S == 2:
        a, b = slots
        return [jnp.where(me == 0, a, b), jnp.where(me == 0, b, a)]
    stacked = jnp.stack(slots, axis=0)
    return [
        lax.dynamic_index_in_dim(stacked, lax.rem((me - s if back else s - me) + S, S), 0, keepdims=False) for s in range(S)
    ]


def exchanged(value, R, bit):
    return lax.ppermute(value, "rep", [(i, i ^ bit) for i in range(R)])


def columns_for(weight, me, S, j, parts, row=0, rows=None):
    cols = weight.shape[1] // parts
    rows = weight.shape[0] if rows is None else rows
    w = cols // S
    at = lax.rem(me + j, S) * w
    got = [lax.dynamic_slice(weight, (row, p * cols + at), (rows, w)) for p in range(parts)]
    return got[0] if parts == 1 else jnp.concatenate(got, axis=1)


def half_pieces(weight, me, S):
    n = weight.shape[0] // 2
    at = lax.axis_index("rep") % 2 * n
    return [columns_for(weight, me, S, j, 1, at, n) for j in range(1, S)]


def from_halves(weight, pieces, me, S, R):
    first = lax.axis_index("rep") % 2 == 0
    slots = [columns_for(weight, me, S, 0, 1)]
    for piece in pieces:
        other = exchanged(piece, R, 1)
        slots.append(jnp.concatenate([jnp.where(first, piece, other), jnp.where(first, other, piece)], axis=0))
    return jnp.concatenate(canonical(slots, me, S, True), axis=0)


def rep_pieces(weight, me, S, R, parts):
    n = weight.shape[0] // R
    rep = lax.axis_index("rep")
    return [columns_for(weight, me, S, j, parts, rep * n, n) for j in range(1, S)]


def from_rep(weight, pieces, me, S, parts):
    others = lax.all_gather(jnp.stack(pieces, axis=0), "rep", axis=1, tiled=True)
    slots = [columns_for(weight, me, S, 0, parts)] + [others[j] for j in range(S - 1)]
    return jnp.concatenate(canonical(slots, me, S, True), axis=0)


def add_low(a, b):
    return (a.astype(F32) + b.astype(F32)).astype(BF)


def orders(R):
    bits = [1 << i for i in range(R.bit_length() - 1)]
    return bits, bits[:1] + bits[2:] + bits[1:2]


def place(rep, order):
    q = jnp.zeros((), jnp.int32)
    for bit in order:
        q = 2 * q + (rep & bit) // bit
    return q


def beside_it(got, key, beside):
    if key in beside:
        got, beside[key] = lax.optimization_barrier((got, beside[key]))
    return got


def halving(pairs, R, beside):
    for i, bits in enumerate(zip(*orders(R))):
        got = beside_it([exchanged(p[1], R, bit) for p, bit in zip(pairs, bits)], i, beside)
        h = got[0].shape[0] // 2
        if h:
            pairs = [(add_low(p[0][:h], t[:h]), add_low(p[0][h:], t[h:])) for p, t in zip(pairs, got)]
        else:
            pairs = [add_low(p[0], t) for p, t in zip(pairs, got)]
    return [p[0] for p in pairs]


def doubling(parts, R, beside):
    pair = [p[None] for p in parts]
    for i, bits in reversed(list(enumerate(zip(*orders(R))))):
        got = beside_it([exchanged(g, R, bit) for g, bit in zip(pair, bits)], i, beside)
        if i:
            pair = [jnp.concatenate([g, t], axis=0) for g, t in zip(pair, got)]
    return list(zip(pair, got))


def hops(v, R):
    out = []
    for b in range(R.bit_length() - 1):
        v = v + exchanged(v, R, 1 << b)
        out.append(v)
    return out


def sum_all(v, S, R):
    bit = 1
    while bit < R:
        v = v + exchanged(v, R, bit)
        bit *= 2
    return v


def swap_shards(part, me, S, head):
    n = (part.shape[0] - head) // S
    slots = []
    for j in range(S):
        b = lax.dynamic_slice_in_dim(part, head + lax.rem(me + j, S) * n, n, 0)
        slots.append(shifted(b, S, j) if j else b)
    return jnp.concatenate(([part[:head]] if head else []) + canonical(slots, me, S, True), axis=0)


def reduce_rows(grad):
    part = lax.psum_scatter(grad, "rep", scatter_dimension=0, tiled=True)
    return lax.all_gather(part, "rep", axis=0, tiled=True).astype(F32)


def reduce_columns(grad, me, S, parts):
    rows, cols = grad.shape
    part = lax.psum_scatter(grad.reshape(S, rows // S, cols), "rep", scatter_dimension=1, tiled=True)
    slots = [lax.dynamic_index_in_dim(part, me, 0, keepdims=False)]
    for j in range(1, S):
        slots.append(shifted(lax.dynamic_index_in_dim(part, lax.rem(me + j, S), 0, keepdims=False), S, j))
    slots = [s.reshape(s.shape[0], parts, cols // parts) for s in slots]
    whole = jnp.stack(canonical(slots, me, S, True), axis=2).reshape(-1, S * cols)
    return lax.all_gather(whole, "rep", axis=0, tiled=True).astype(F32)


def rotary_tables(PR, CR, CL):
    pos = np.concatenate([np.arange(PR), PR + np.arange(CR) % CL]).astype(np.float32)
    half = ROT // 2
    freq = np.exp(np.arange(half, dtype=np.float32) * np.float32(-2.0 * math.log(10000.0) / ROT)).astype(np.float32)
    ang = (pos[:, None] * freq[None, :]).astype(np.float32)
    c = np.cos(ang)
    s = np.sin(ang)
    n = pos.shape[0]
    one = np.ones((n, HD - ROT), np.float32)
    zero = np.zeros((n, HD - ROT), np.float32)
    z8 = np.zeros((n, half), np.float32)
    tabs = ([c, c, one], [-s, z8, zero], [z8, s, zero])
    return [jnp.asarray(np.tile(np.concatenate(t, axis=1), (1, 128 // HD)), F32) for t in tabs]


def per_device(
    prompt_in,
    cont_in,
    prompt_cot,
    cont_cot,
    ln1_gain,
    ln1_bias,
    ln2_gain,
    ln2_bias,
    qkv_weight,
    qkv_bias,
    out_weight,
    out_bias,
    up_weight,
    up_bias,
    down_weight,
    down_bias,
):
    S = lax.axis_size("shard")
    R = lax.axis_size("rep")
    me = lax.axis_index("shard")
    MB, _, PD, D = prompt_in.shape
    CD, CL = cont_in.shape[2:4]
    CR = CD * CL
    N = PD + CR
    CW = D // S
    FL = up_weight.shape[1] // S
    me_arr = jnp.reshape(me, (1,)).astype(jnp.int32)

    X = [[jnp.concatenate([prompt_in[m, 0], cont_in[m, 0].reshape(CR, D)], axis=0)] for m in range(MB)]
    DY = [[jnp.concatenate([prompt_cot[m, 0], cont_cot[m, 0].reshape(CR, D)], axis=0)] for m in range(MB)]
    away = lambda values: [shifted(v, S, j + 1) for j, v in enumerate(values)]
    cut = half_pieces(up_weight, me, S)
    vectors_in = (ln1_gain, ln1_bias, ln2_gain, ln2_bias, out_bias, down_bias, qkv_bias)
    (vectors_in, qkv_weight), cut = lax.optimization_barrier(((vectors_in, qkv_weight), cut))
    small = jnp.concatenate([v.astype(F32).reshape(-1, CW) for v in vectors_in], axis=0)
    slots = [small] + away([small] * (S - 1))
    pieces_qkv = away(rep_pieces(qkv_weight, me, S, R, 3))
    pieces_up = away(cut)
    src = [(X[m][0], DY[m][0]) for m in range(MB)]
    src[1:], _ = lax.optimization_barrier((src[1:], pieces_up))
    pieces_up, _ = lax.optimization_barrier((pieces_up, (small, X, DY)))
    src[0], _ = lax.optimization_barrier((src[0], (slots[1:])))
    w_up = from_halves(up_weight, pieces_up, me, S, R)
    w_qkv = from_rep(qkv_weight, pieces_qkv, me, S, 3)

    whole = jnp.stack(canonical(slots, me, S, True), axis=0)
    vec = whole[:, :6].transpose(1, 0, 2).reshape(6, D)
    gb1 = vec[0:2]
    gb2 = vec[2:4]
    vb = vec[4:6]
    bqkv = whole[:, 6:].reshape(3, S, CW)
    bqkv = lax.dynamic_index_in_dim(bqkv, me, 1, keepdims=False).reshape(1, 3 * CW)
    bup = up_bias.astype(F32).reshape(1, FL)

    tabs = rotary_tables(PD * S, CR * S, CL)
    for m in range(MB):
        for j in range(1, S):
            X[m].append(shifted(src[m][0], S, S - j))
            DY[m].append(shifted(src[m][1], S, S - j))

    ff = [[None] * S for _ in range(MB)]

    def mlp(m, j):
        ff[m][j] = mlp_rows(X[m][j], DY[m][j], w_up, bup, down_weight, gb2, 1)

    for m in range(MB):
        mlp(m, 0)
    rest = []
    y_got, g_got = [], []

    def attend(m):
        ys, gs, more = attn_group(
            S, PD, CL, me_arr, X[m], DY[m], [f[4] for f in ff[m][1:]], [f[5] for f in ff[m][1:]], w_qkv, bqkv, out_weight, gb1, tabs
        )
        rest.append(list(more))
        y_got.append([shifted(ys[j - 1], S, j) for j in range(1, S)])
        g_got.append([shifted(gs[j - 1], S, j) for j in range(1, S)])

    def own(m):
        f = ff[m][0]
        return own_rows(X[m][0], f[4], f[5], rest[m][0], rest[m][1], w_qkv, out_weight, gb1)

    chunked = (D // S // R) % 16 == 0 and R & (R - 1) == 0
    rep = lax.axis_index("rep")
    late = [(MB - 1, j) for j in range(1, S)]
    early = [(m, j) for m in range(MB) for j in range(S) if (m, j) not in late]
    of = lambda set_, k: [ff[m][j][k] for m, j in set_]
    for m, j in early:
        if j:
            mlp(m, j)
    if chunked:
        gmlp = mlp_grads(S, R, of(early, 0), [DY[m][j] for m, j in early], of(early, 2), of(early, 1))
        w_up, gmlp, w_qkv = lax.optimization_barrier((w_up, gmlp, w_qkv))
    for m, j in late:
        mlp(m, j)
    if chunked:
        if late:
            gmlp = mlp_grads(S, R, of(late, 0), [DY[m][j] for m, j in late], of(late, 2), of(late, 1), gmlp)
        part = lax.psum_scatter(gmlp, "rep", scatter_dimension=0, tiled=True)[0]
        w_qkv, gmlp = lax.optimization_barrier((w_qkv, gmlp))
    for m in range(MB):
        attend(m)
        if m + 1 < MB:
            w_qkv, rest[m][3] = lax.optimization_barrier((w_qkv, rest[m][3]))
    every = early + late
    def vectors(mine_):
        ln1 = sum(r[3] for r in rest) + sum(o[2] for o in mine_)
        ln2 = sum(of(every, 6))
        db_out = sum(jnp.sum(DY[m][0].astype(F32), axis=0) for m in range(MB)).reshape(-1, CW)
        mine = (jnp.arange(S) == me).astype(F32)
        db_qkv = (sum(r[4] for r in rest)[:, None, :] * mine[None, :, None]).reshape(-1, CW)
        db_up = (sum(of(every, 3)) * mine[:, None]).reshape(-1, CW)
        return jnp.concatenate([ln1.reshape(-1, CW), ln2.reshape(-1, CW), db_out, db_qkv, db_up], axis=0)

    finals = lambda m, o, prior: final_rows(m, MB, PD, X[m][0], DY[m][0], [o[0]] + y_got[m], [o[1]] + g_got[m], vb, prior)
    hs, dls, ctxs = [[r[k] for r in rest] for k in (2, 0, 1)]
    if chunked:
        q = jnp.stack([place(rep, order) for order in orders(R)]).astype(jnp.int32)
        part = swap_shards(part, me, S, FL // R)
        hs, y_got[:-1], g_got[:-1], part = lax.optimization_barrier((hs, y_got[:-1], g_got[:-1], part))
        gmlp_all = lax.all_gather(part, "rep", axis=0, tiled=False)
        gatt = attn_grads(S, R, q, hs, dls, ctxs, [DY[m][j] for m in range(MB) for j in range(S)])
        dls_own, _ = lax.optimization_barrier(([r[0] for r in rest], gatt))
        for m in range(MB):
            rest[m][0] = dls_own[m]
        mine = [own(m) for m in range(MB)]
        beside = {1: mine}
        levels = R.bit_length() - 1
        path = hops(vectors(mine), R)
        late_hops = {}
        for n, v in enumerate(path):
            at = 2 + n
            (beside if at < levels else late_hops).setdefault(at if at < levels else max(2 * levels - 1 - at, 0), []).append(v)
        outs = None
        for m in range(MB - 1):
            outs = finals(m, mine[m], outs)
        whole_outs = finals(MB - 1, mine[-1], outs)
        beside[levels - 1] = beside.get(levels - 1, []) + [y_got[-1], g_got[-1]]
        half = halving([(g[: R // 2], g[R // 2 :]) for g in gatt], R, beside)
        k = D // CW * (D // S // R)
        finished = mlp_finish(S, gmlp_all, FL)
        after = {3: (outs, late_hops.get(3, [])), 2: (finished, late_hops.get(2, [])), 1: (whole_outs, late_hops.get(1, []))}
        g1, g2 = doubling([swap_shards(half[0], me, S, 0), swap_shards(half[1], me, S, k)], R, after)
        outs = after[1][0]
        g_down, g_up = after[2][0]
        vecs = path[-1]
        g_out, g_qkv = attn_finish(S, q, g1, g2)
    else:
        dls, ctxs, hs = [[r[k] for r in rest] for k in (0, 1, 2)]
        mine = [own(m) for m in range(MB)]
        g_down = reduce_rows(tn_sum(of(every, 0), [DY[m][j] for m, j in every], 256))
        g_up = reduce_columns(tn_sum(of(every, 2), of(every, 1), 256), me, S, 1)
        dycs = [jnp.concatenate(DY[m], axis=0) for m in range(MB)]
        g_out = reduce_rows(tn_sum(ctxs, dycs, 256))
        g_qkv = reduce_columns(tn_sum(hs, dls, 256), me, S, 3)
        vecs = sum_all(vectors(mine), S, R)
        outs = None
        for m in range(MB):
            outs = finals(m, mine[m], outs)
    tot = vecs + sum(shifted(vecs, S, j) for j in range(1, S))
    held = lambda a, n: lax.dynamic_slice_in_dim(tot, a + me * n, n, 0).reshape(-1)
    v_ln1g, v_ln1b, v_ln2g, v_ln2b, v_out = [held(k * S, 1) for k in range(5)]
    v_qkv = held(5 * S, 3)
    v_up = held(8 * S, FL // CW)

    po, co, pg, cg = outs
    return (
        po.reshape(MB, 1, PD, D),
        co.reshape(MB, 1, CD, CL, D),
        pg.reshape(MB, 1, PD, D),
        cg.reshape(MB, 1, CD, CL, D),
        v_ln1g,
        v_ln1b,
        v_ln2g,
        v_ln2b,
        g_qkv,
        v_qkv,
        g_out,
        v_out,
        g_up,
        v_up,
        g_down,
        v_out,
    )


def solution(mesh):
    tokens = (
        P(None, "rep", "shard", None),
        P(None, "rep", "shard", None, None),
        P(None, "rep", "shard", None),
        P(None, "rep", "shard", None, None),
    )
    vec = P("shard")
    mat = P("shard", None)
    params = (vec, vec, vec, vec, mat, vec, mat, vec, mat, vec, mat, vec)
    return jax.shard_map(
        per_device, mesh=mesh, in_specs=tokens + params, out_specs=tokens + params, check_vma=False
    )
```

profile of v0, /device:TPU:0, one launch (start us, length us, event | category | flops | bytes accessed | tf_op | source)
XLA Modules:
  0.0 494.0 jit_solution(5796252194059112333)
XLA Ops:
  7.3 2.5 dynamic_slice.79
  9.8 2.9 collective-permute-start.3
  16.4 21.8 %collective-permute-done.5 = bf16[32,1536]{1,0:T(8,128)(2,1)S(1)} collective-permute-done((bf16[32,1536]{1,0:T(8,128)(2,1)S(1)}, bf16[32,1536]{1,0:T(8,128)(2,1)S(1)}, u32[]{:S(2)}, u32[]{:S(2)}) %collective-permute-start.5) | collective-permute-done | bytes 98336 | tf_op jit(solution)/shard_map/ppermute | solution.py:734
  44.3 1.8 collective-permute-start
  46.1 2.5 constant_dynamic-slice_fusion.9
  53.9 1.7 broadcast_select_fusion.5
  56.7 2.6 pad_maximum_fusion.wu_ref
  59.3 20.4 %shard_map.308 = (bf16[640,2048]{1,0:T(8,128)(2,1)}, bf16[640,2048]{1,0:T(8,128)(2,1)}, bf16[640,1024]{1,0:T(8,128)(2,1)}, f32[1,2048]{1,0:T(1,128)}, bf16[640,1...) custom-call(bf16[640,1024]{1,0:T(8,128)(2,1)} %pad_maximum_fusion.6.x_ref.refs_0_.x, ...), custom_call_target="tpu_custom_call" | custom-call | flops 1000000 | bytes 100000 | tf_op jit(solution)/shard_map/pallas_call | solution.py:109
  79.7 20.2 %shard_map.307 = (bf16[640,2048]{1,0:T(8,128)(2,1)}, bf16[640,2048]{1,0:T(8,128)(2,1)}, bf16[640,1024]{1,0:T(8,128)(2,1)}, f32[1,2048]{1,0:T(1,128)}, bf16[640,1...) custom-call(bf16[640,1024]{1,0:T(8,128)(2,1)} %pad_maximum_fusion.4.x_ref.refs_0_.x, ...), custom_call_target="tpu_custom_call" | custom-call | flops 1000000 | bytes 100000 | tf_op jit(solution)/shard_map/pallas_call | solution.py:109
  99.9 9.3 %collective-permute-done.2.dy_ref.refs_4_.refs_3_.refs_7_ = bf16[640,1024]{1,0:T(8,128)(2,1)} collective-permute-done((bf16[640,1024]{1,0:T(8,128)(2,1)S(1)}, bf16[640,1024]{1,0:T(8,128)(2,1)}, u32[]{:S(2)}, u32[]{:S(2)}) %collective-permute-start.2) | collective-permute-done | bytes 1310752 | tf_op jit(solution)/shard_map/ppermute | solution.py:734
  109.3 20.2 %shard_map.306 = (bf16[640,2048]{1,0:T(8,128)(2,1)}, bf16[640,2048]{1,0:T(8,128)(2,1)}, bf16[640,1024]{1,0:T(8,128)(2,1)}, f32[1,2048]{1,0:T(1,128)}, bf16[640,1...) custom-call(bf16[640,1024]{1,0:T(8,128)(2,1)} %collective-permute-done.1.x_ref.refs_1_, ...), custom_call_target="tpu_custom_call" | custom-call | flops 1000000 | bytes 100000 | tf_op jit(solution)/shard_map/pallas_call | solution.py:109
  129.5 14.0 %shard_map.309.refs_6_ = bf16[16,256,1024]{2,1,0:T(8,128)(2,1)} custom-call(bf16[640,2048]{1,0:T(8,128)(2,1)} %get-tuple-element.142.refs_0_, bf16[640,2048]{1,0:T(8,128)(2,1)} %get-tuple-element.143.refs_1_, bf16[640,2048]{1,0:T(8,128)(2,1)} %get-tuple-element.144.refs_2_, bf16[640,1024]{1,0:T(8,128)(2,1)} %copy-done.2, ...), custom_call_target="tpu_custom_call" | custom-call | flops 1000000 | bytes 100000 | tf_op jit(solution)/shard_map/pallas_call | solution.py:491
  143.5 14.8 %shard_map.310.refs_2_ = bf16[16,256,1024]{2,1,0:T(8,128)(2,1)} custom-call(bf16[640,1024]{1,0:T(8,128)(2,1)} %get-tuple-element.136.refs_0_, bf16[640,1024]{1,0:T(8,128)(2,1)} %get-tuple-element.137.refs_1_, bf16[640,1024]{1,0:T(8,128)(2,1)} %get-tuple-element.138.refs_2_, ...), custom_call_target="tpu_custom_call", output_to_operand_aliasing={{}: (6, {})} | custom-call | flops 1000000 | bytes 100000 | tf_op jit(solution)/shard_map/pallas_call | solution.py:491
  158.4 2.1 broadcast_select_fusion.3
  160.5 1.9 pad_maximum_fusion.1.refs_6_.refs_7_.refs_8_.wqkv
  162.3 2.3 collective-permute-done.7.dy_ref.refs_1_.refs_3_.refs_9_
  164.7 20.1 %shard_map.311 = (bf16[640,2048]{1,0:T(8,128)(2,1)}, bf16[640,2048]{1,0:T(8,128)(2,1)}, bf16[640,1024]{1,0:T(8,128)(2,1)}, f32[1,2048]{1,0:T(1,128)}, bf16[640,1...) custom-call(bf16[640,1024]{1,0:T(8,128)(2,1)} %collective-permute-done.6.x_ref.refs_1_, ...), custom_call_target="tpu_custom_call" | custom-call | flops 1000000 | bytes 100000 | tf_op jit(solution)/shard_map/pallas_call | solution.py:109
  184.8 9.6 %shard_map.312.refs_2_ = bf16[16,256,1024]{2,1,0:T(8,128)(2,1)} custom-call(bf16[640,2048]{1,0:T(8,128)(2,1)} %get-tuple-element.152.refs_0_, bf16[640,1024]{1,0:T(8,128)(2,1)} %collective-permute-done.7.dy_ref.refs_1_.refs_3_.refs_9_, bf16[16,256,1024]{2,1,0:T(8,128)(2,1)} %shard_map.310.refs_2_), custom_call_target="tpu_custom_call", output_to_operand_aliasing={{}: (2, {})} | custom-call | flops 1000000 | bytes 100000 | tf_op jit(solution)/shard_map/pallas_call | solution.py:491
  194.4 8.1 %shard_map.313 = bf16[16,256,1024]{2,1,0:T(8,128)(2,1)} custom-call(bf16[640,1024]{1,0:T(8,128)(2,1)} %get-tuple-element.150.refs_0_, bf16[640,2048]{1,0:T(8,128)(2,1)} %get-tuple-element.151.refs_1_, bf16[16,256,1024]{2,1,0:T(8,128)(2,1)} %shard_map.312.refs_2_), custom_call_target="tpu_custom_call", output_to_operand_aliasing={{}: (2, {})} | custom-call | flops 1000000 | bytes 100000 | tf_op jit(solution)/shard_map/pallas_call | solution.py:491
  203.2 55.9 %shard_map.314 = (bf16[640,1024]{1,0:T(8,128)(2,1)}, bf16[640,1024]{1,0:T(8,128)(2,1)}, bf16[3,1280,512]{2,1,0:T(8,128)(2,1)}, bf16[1280,512]{1,0:T(8,128)(2,1)}...) custom-call(s32[1]{0:T(128)} %bitcast.2.me_ref, ...), custom_call_target="tpu_custom_call" | custom-call | flops 1000000 | bytes 100000 | tf_op jit(solution)/shard_map/pallas_call | solution.py:386
  259.5 1.7 collective-permute-start.9
  261.2 56.4 %shard_map.315 = (bf16[640,1024]{1,0:T(8,128)(2,1)}, bf16[640,1024]{1,0:T(8,128)(2,1)}, bf16[3,1280,512]{2,1,0:T(8,128)(2,1)}, bf16[1280,512]{1,0:T(8,128)(2,1)}...) custom-call(s32[1]{0:T(128)} %bitcast.2.me_ref, ...), custom_call_target="tpu_custom_call" | custom-call | flops 1000000 | bytes 100000 | tf_op jit(solution)/shard_map/pallas_call | solution.py:386
  319.8 3.8 collective-permute-done.10
  326.2 19.3 %shard_map.316 = (bf16[16,128,512]{2,1,0:T(8,128)(2,1)}, bf16[16,128,512]{2,1,0:T(8,128)(2,1)}) custom-call(s32[2]{0:T(128)} %pad_add_fusion.q_ref, bf16[1280,1024]{1,0:T(8,128)(2,1)} %get-tuple-element.163.refs_0_, bf16[1280,1024]{1,0:T(8,128)(2,1)} %get-tuple-element.164.refs_1_, bf16[3,1280,512]{2,1,0:T(8,128)(2,1)} %get-tuple-element.171.refs_2_.dl, ...), custom_call_target="tpu_custom_call" | custom-call | flops 1000000 | bytes 100000 | tf_op jit(solution)/shard_map/pallas_call | solution.py:582
  345.6 2.5 slice.167
  351.0 2.6 add_convert_fusion
  353.7 1.6 collective-permute-start.14
  355.3 2.3 add_convert_fusion.2
  361.5 9.8 %shard_map.318 = (bf16[640,1024]{1,0:T(8,128)(2,1)}, bf16[640,1024]{1,0:T(8,128)(2,1)}, f32[2,1024]{1,0:T(2,128)}) custom-call(bf16[3,1280,512]{2,1,0:T(8,128)(2,1)} %get-tuple-element.177.refs_3_.dl, bf16[1280,512]{1,0:T(8,128)(2,1)} %get-tuple-element.168.refs_5_.ctx, bf16[1024,1536]{1,0:T(8,128)(2,1)} %pad_maximum_fusion.1.refs_6_.refs_7_.refs_8_.wqkv, ...), custom_call_target="tpu_custom_call" | custom-call | flops 1000000 | bytes 100000 | tf_op jit(solution)/shard_map/pallas_call | solution.py:667
  371.4 9.8 %shard_map.317 = (bf16[640,1024]{1,0:T(8,128)(2,1)}, bf16[640,1024]{1,0:T(8,128)(2,1)}, f32[2,1024]{1,0:T(2,128)}) custom-call(bf16[3,1280,512]{2,1,0:T(8,128)(2,1)} %get-tuple-element.171.refs_2_.dl, bf16[1280,512]{1,0:T(8,128)(2,1)} %get-tuple-element.167.refs_4_.ctx, bf16[1024,1536]{1,0:T(8,128)(2,1)} %pad_maximum_fusion.1.refs_6_.refs_7_.refs_8_.wqkv, ...), custom_call_target="tpu_custom_call" | custom-call | flops 1000000 | bytes 100000 | tf_op jit(solution)/shard_map/pallas_call | solution.py:667
  381.2 2.1 collective-permute-done.14
  383.3 2.0 add_convert_fusion.4
  385.3 4.5 collective-permute-start.16
  390.6 2.4 collective-permute-start.15
  394.4 17.3 %collective-permute-done.16 = bf16[2,128,512]{2,1,0:T(8,128)(2,1)} collective-permute-done((bf16[2,128,512]{2,1,0:T(8,128)(2,1)}, bf16[2,128,512]{2,1,0:T(8,128)(2,1)}, u32[]{:S(2)}, u32[]{:S(2)}) %collective-permute-start.16) | collective-permute-done | bytes 262176 | tf_op jit(solution)/shard_map/ppermute | solution.py:750
  411.7 3.4 collective-permute-done.15
  416.5 2.1 collective-permute-start.20
  418.5 3.3 collective-permute-done.20
  424.9 2.1 collective-permute-start.23
  427.8 1.9 collective-permute-start.26
  436.1 6.3 %shard_map.319 = (bf16[2,512,1024]{2,1,0:T(8,128)(2,1)}, bf16[2,128,1024]{2,1,0:T(8,128)(2,1)}, f32[2,512,1024]{2,1,0:T(8,128)}, f32[2,128,1024]{2,1,0:T(8,128)}) custom-call(bf16[640,1024]{1,0:T(8,128)(2,1)S(1)} %copy-done.5, bf16[640,1024]{1,0:T(8,128)(2,1)S(1)} %copy-done.3, bf16[640,1024]{1,0:T(8,128)(2,1)S(1)} %copy-done.11, ...), custom_call_target="tpu_custom_call" | custom-call | flops 1000000 | bytes 100000 | tf_op jit(solution)/shard_map/pallas_call | solution.py:721
  443.1 2.1 collective-permute-start.28
  446.3 7.3 %collective-permute-done.30 = f32[24,512]{1,0:T(8,128)S(1)} collective-permute-done((f32[24,512]{1,0:T(8,128)S(1)}, f32[24,512]{1,0:T(8,128)S(1)}, u32[]{:S(2)}, u32[]{:S(2)}) %collective-permute-start.30) | collective-permute-done | bytes 49184 | tf_op jit(solution)/shard_map/ppermute | solution.py:750
  453.7 3.4 copy-done.6
  457.1 6.5 %shard_map.320 = (f32[2048,1024]{1,0:T(8,128)}, f32[512,4096]{1,0:T(8,128)}) custom-call(bf16[16,256,1024]{2,1,0:T(8,128)(2,1)S(1)} %bitcast.74), custom_call_target="tpu_custom_call" | custom-call | flops 1000000 | bytes 100000 | tf_op jit(solution)/shard_map/pallas_call | solution.py:524
  465.7 6.5 %shard_map.321 = (bf16[2,512,1024]{2,1,0:T(8,128)(2,1)}, bf16[2,128,1024]{2,1,0:T(8,128)(2,1)}, f32[2,512,1024]{2,1,0:T(8,128)}, f32[2,128,1024]{2,1,0:T(8,128)}) custom-call(bf16[640,1024]{1,0:T(8,128)(2,1)S(1)} %copy-done.4, bf16[640,1024]{1,0:T(8,128)(2,1)S(1)} %copy-done.1, ...), custom_call_target="tpu_custom_call", output_to_operand_aliasing={{0}: (7, {}), {1}: (8, {}), {2}: (9, {}), {3}: (10, {})} | custom-call | flops 1000000 | bytes 100000 | tf_op jit(solution)/shard_map/pallas_call | solution.py:721
  475.8 2.6 collective-permute-done.33
  480.3 6.3 %shard_map.322 = (f32[512,1024]{1,0:T(8,128)}, f32[512,3072]{1,0:T(8,128)}) custom-call(s32[2]{0:T(128)S(1)} %copy-done.13, bf16[8,128,512]{2,1,0:T(8,128)(2,1)S(1)} %pad_maximum_fusion.8.refs_0_.refs_1_.refs_2_.refs_3_, bf16[8,128,512]{2,1,0:T(8,128)(2,1)S(1)} %pad_maximum_fusion.8.refs_0_.refs_1_.refs_2_.refs_3_, ...), custom_call_target="tpu_custom_call" | custom-call | flops 1000000 | bytes 100000 | tf_op jit(solution)/shard_map/pallas_call | solution.py:632
  (254 shorter events, 52.2 us)
Async XLA Ops:
  7.3 151.1 %all-gather.5.cloned.1.call-start = ((), (), s32[]{:S(2)}) async-start(), calls=%async_computation.2 | async-start | bytes 1671168 | tf_op jit(solution)/shard_map/all_gather | solution.py:784
  9.8 34.5 %collective-permute-start.3 = (bf16[256,2048]{1,0:T(8,128)(2,1)}, bf16[256,2048]{1,0:T(8,128)(2,1)}, u32[]{:S(2)}, u32[]{:S(2)}) collective-permute-start(bf16[256,2048]{1,0:T(8,128)(2,1)} %dynamic_slice.79), channel_id=1, source_target_pairs={{0,1},{1,0},{2,3},{3,2},{4,5},{5,4},{6,7},{7,6},{8,9},{9,8},{10,11... | collective-permute-start | bytes 3145736 | tf_op jit(solution)/shard_map/ppermute | solution.py:734
  13.5 24.7 %collective-permute-start.5 = (bf16[32,1536]{1,0:T(8,128)(2,1)S(1)}, bf16[32,1536]{1,0:T(8,128)(2,1)S(1)}, u32[]{:S(2)}, u32[]{:S(2)}) collective-permute-start(bf16[32,1536]{1,0:T(8,128)(2,1)S(1)} %pad_maximum_fusion.15), channel_id=1, source_target_pairs={{0,1},{1,0},{2,3},{3,2},{4,5},{5,4},{6,7},{7,6},{8,9},{9,8},{10,11... | collective-permute-start | bytes 294920 | tf_op jit(solution)/shard_map/ppermute | solution.py:734
  16.3 33.7 %copy-start.2 = (bf16[640,1024]{1,0:T(8,128)(2,1)}, bf16[640,1024]{1,0:T(8,128)(2,1)S(1)}, u32[]{:S(2)}) copy-start(bf16[640,1024]{1,0:T(8,128)(2,1)S(1)} %pad_maximum_fusion.5.dy_ref.refs_3_.refs_2_.refs_6_.refs_1_) | copy-start | bytes 3932164
  38.9 278.8 %reduce-scatter.2.cloned.1.call-start = ((), (), s32[]{:S(2)}) async-start(), calls=%async_computation.1 | async-start | bytes 8912896 | tf_op jit(solution)/shard_map/reduce_scatter | solution.py:986
  44.3 9.7 %collective-permute-start.4 = (bf16[256,2048]{1,0:T(8,128)(2,1)}, bf16[256,2048]{1,0:T(8,128)(2,1)}, u32[]{:S(2)}, u32[]{:S(2)}) collective-permute-start(bf16[256,2048]{1,0:T(8,128)(2,1)} %collective-permute-done.3), channel_id=1, source_target_pairs={{0,2},{2,0},{4,6},{6,4},{8,10},{10,8},{12,14},{14,12},{16,18},{18,... | collective-permute-start | bytes 3145736 | tf_op jit(solution)/shard_map/ppermute | solution.py:750
  44.3 5.0 %collective-permute-start = (f32[9,512]{1,0:T(8,128)S(1)}, f32[9,512]{1,0:T(8,128)S(1)}, u32[]{:S(2)}, u32[]{:S(2)}) collective-permute-start(f32[9,512]{1,0:T(8,128)S(1)} %concatenate.70), channel_id=1, source_target_pairs={{0,1},{1,0},{2,3},{3,2},{4,5},{5,4},{6,7},{7,6},{8,9},{9,8},{10,11... | collective-permute-start | bytes 55304 | tf_op jit(solution)/shard_map/ppermute | solution.py:734
  49.2 50.7 %collective-permute-start.1 = (bf16[640,1024]{1,0:T(8,128)(2,1)}, bf16[640,1024]{1,0:T(8,128)(2,1)}, u32[]{:S(2)}, u32[]{:S(2)}) collective-permute-start(bf16[640,1024]{1,0:T(8,128)(2,1)} %pad_maximum_fusion.4.x_ref.refs_0_.x), channel_id=1, source_target_pairs={{0,1},{1,0},{2,3},{3,2},{4,5},{5,4},{6,7},{7,6},{8,9},{9,8},{10,11... | collective-permute-start | bytes 3932168 | tf_op jit(solution)/shard_map/ppermute | solution.py:734
  50.0 59.3 %collective-permute-start.2 = (bf16[640,1024]{1,0:T(8,128)(2,1)S(1)}, bf16[640,1024]{1,0:T(8,128)(2,1)}, u32[]{:S(2)}, u32[]{:S(2)}) collective-permute-start(bf16[640,1024]{1,0:T(8,128)(2,1)S(1)} %pad_maximum_fusion.5.dy_ref.refs_3_.refs_2_.refs_6_.refs_1_), channel_id=1, source_target_pairs={{0,1},{1,0},{2,3},{3,2},{4,5},{5,4},{6,7},{7,6},{8,9},{9,8},{10,11... | collective-permute-start | bytes 3932168 | tf_op jit(solution)/shard_map/ppermute | solution.py:734
  51.9 110.4 %collective-permute-start.6 = (bf16[640,1024]{1,0:T(8,128)(2,1)}, bf16[640,1024]{1,0:T(8,128)(2,1)}, u32[]{:S(2)}, u32[]{:S(2)}) collective-permute-start(bf16[640,1024]{1,0:T(8,128)(2,1)} %pad_maximum_fusion.6.x_ref.refs_0_.x), channel_id=1, source_target_pairs={{0,1},{1,0},{2,3},{3,2},{4,5},{5,4},{6,7},{7,6},{8,9},{9,8},{10,11... | collective-permute-start | bytes 3932168 | tf_op jit(solution)/shard_map/ppermute | solution.py:734
  52.7 112.0 %collective-permute-start.7 = (bf16[640,1024]{1,0:T(8,128)(2,1)S(1)}, bf16[640,1024]{1,0:T(8,128)(2,1)}, u32[]{:S(2)}, u32[]{:S(2)}) collective-permute-start(bf16[640,1024]{1,0:T(8,128)(2,1)S(1)} %pad_maximum_fusion.7.dy_ref.refs_5_.refs_2_.refs_8_.refs_1_), channel_id=1, source_target_pairs={{0,1},{1,0},{2,3},{3,2},{4,5},{5,4},{6,7},{7,6},{8,9},{9,8},{10,11... | collective-permute-start | bytes 3932168 | tf_op jit(solution)/shard_map/ppermute | solution.py:734
  143.5 14.9 %copy-start.18 = (bf16[512,512]{1,0:T(8,128)(2,1)S(1)}, bf16[512,512]{1,0:T(8,128)(2,1)}, u32[]{:S(2)}) copy-start(bf16[512,512]{1,0:T(8,128)(2,1)} %get-tuple-element.270) | copy-start | bytes 1572868
  143.5 14.9 %copy-start.19 = (bf16[512,512]{1,0:T(8,128)(2,1)S(1)}, bf16[512,512]{1,0:T(8,128)(2,1)}, u32[]{:S(2)}) copy-start(bf16[512,512]{1,0:T(8,128)(2,1)} %get-tuple-element.271) | copy-start | bytes 1572868
  202.5 251.2 %all-gather.7.cloned.1.call-start = ((), (), s32[]{:S(2)}) async-start(), calls=%async_computation.3 | async-start | bytes 8912896 | tf_op jit(solution)/shard_map/all_gather | solution.py:1008
  259.1 66.3 %collective-permute-start.8 = (bf16[640,1024]{1,0:T(8,128)(2,1)}, bf16[640,1024]{1,0:T(8,128)(2,1)S(1)}, u32[]{:S(2)}, u32[]{:S(2)}) collective-permute-start(bf16[640,1024]{1,0:T(8,128)(2,1)} %get-tuple-element.161), channel_id=1, source_target_pairs={{0,1},{1,0},{2,3},{3,2},{4,5},{5,4},{6,7},{7,6},{8,9},{9,8},{10,11... | collective-permute-start | bytes 3932168 | tf_op jit(solution)/shard_map/ppermute | solution.py:734
  259.5 65.9 %collective-permute-start.9 = (bf16[640,1024]{1,0:T(8,128)(2,1)}, bf16[640,1024]{1,0:T(8,128)(2,1)}, u32[]{:S(2)}, u32[]{:S(2)}) collective-permute-start(bf16[640,1024]{1,0:T(8,128)(2,1)} %get-tuple-element.162), channel_id=1, source_target_pairs={{0,1},{1,0},{2,3},{3,2},{4,5},{5,4},{6,7},{7,6},{8,9},{9,8},{10,11... | collective-permute-start | bytes 3932168 | tf_op jit(solution)/shard_map/ppermute | solution.py:734
  318.6 5.0 %collective-permute-start.10 = (bf16[64,1024]{1,0:T(8,128)(2,1)S(1)}, bf16[64,1024]{1,0:T(8,128)(2,1)S(1)}, u32[]{:S(2)}, u32[]{:S(2)}) collective-permute-start(bf16[64,1024]{1,0:T(8,128)(2,1)S(1)} %dynamic-slice_bitcast_fusion), channel_id=1, source_target_pairs={{0,1},{1,0},{2,3},{3,2},{4,5},{5,4},{6,7},{7,6},{8,9},{9,8},{10,11... | collective-permute-start | bytes 393224 | tf_op jit(solution)/shard_map/ppermute | solution.py:734
  325.4 20.1 %copy-start.9 = (bf16[640,1024]{1,0:T(8,128)(2,1)}, bf16[640,1024]{1,0:T(8,128)(2,1)S(1)}, u32[]{:S(2)}) copy-start(bf16[640,1024]{1,0:T(8,128)(2,1)S(1)} %collective-permute-done.8.refs_3_) | copy-start | bytes 3932164
  348.0 3.0 collective-permute-start.13
  349.2 6.1 %collective-permute-start.11 = (bf16[8,128,512]{2,1,0:T(8,128)(2,1)}, bf16[8,128,512]{2,1,0:T(8,128)(2,1)}, u32[]{:S(2)}, u32[]{:S(2)}) collective-permute-start(bf16[8,128,512]{2,1,0:T(8,128)(2,1)} %slice.161), channel_id=1, source_target_pairs={{0,2},{2,0},{4,6},{6,4},{8,10},{10,8},{12,14},{14,12},{16,18},{18,... | collective-permute-start | bytes 3145736 | tf_op jit(solution)/shard_map/ppermute | solution.py:750
  353.7 29.6 %collective-permute-start.14 = (bf16[4,128,512]{2,1,0:T(8,128)(2,1)}, bf16[4,128,512]{2,1,0:T(8,128)(2,1)}, u32[]{:S(2)}, u32[]{:S(2)}) collective-permute-start(bf16[4,128,512]{2,1,0:T(8,128)(2,1)} %get-tuple-element.265), channel_id=1, source_target_pairs={{0,8},{2,10},{4,12},{6,14},{8,0},{10,2},{12,4},{14,6},{16,24},{18,... | collective-permute-start | bytes 1572872 | tf_op jit(solution)/shard_map/ppermute | solution.py:750
  357.6 25.7 %collective-permute-start.12 = (bf16[4,128,512]{2,1,0:T(8,128)(2,1)}, bf16[4,128,512]{2,1,0:T(8,128)(2,1)S(1)}, u32[]{:S(2)}, u32[]{:S(2)}) collective-permute-start(bf16[4,128,512]{2,1,0:T(8,128)(2,1)} %get-tuple-element.266), channel_id=1, source_target_pairs={{0,4},{2,6},{4,0},{6,2},{8,12},{10,14},{12,8},{14,10},{16,20},{18,... | collective-permute-start | bytes 1572872 | tf_op jit(solution)/shard_map/ppermute | solution.py:750
  359.3 62.5 %collective-permute-start.21 = (bf16[640,1024]{1,0:T(8,128)(2,1)}, bf16[640,1024]{1,0:T(8,128)(2,1)}, u32[]{:S(2)}, u32[]{:S(2)}) collective-permute-start(bf16[640,1024]{1,0:T(8,128)(2,1)} %get-tuple-element.199), channel_id=1, source_target_pairs={{0,1},{1,0},{2,3},{3,2},{4,5},{5,4},{6,7},{7,6},{8,9},{9,8},{10,11... | collective-permute-start | bytes 3932168 | tf_op jit(solution)/shard_map/ppermute | solution.py:734
  359.9 61.9 %collective-permute-start.22 = (bf16[640,1024]{1,0:T(8,128)(2,1)}, bf16[640,1024]{1,0:T(8,128)(2,1)}, u32[]{:S(2)}, u32[]{:S(2)}) collective-permute-start(bf16[640,1024]{1,0:T(8,128)(2,1)} %get-tuple-element.200), channel_id=1, source_target_pairs={{0,1},{1,0},{2,3},{3,2},{4,5},{5,4},{6,7},{7,6},{8,9},{9,8},{10,11... | collective-permute-start | bytes 3932168 | tf_op jit(solution)/shard_map/ppermute | solution.py:734
  381.2 11.9 %copy-start.34 = (f32[2,1024]{1,0:T(2,128)S(1)}, f32[2,1024]{1,0:T(2,128)}, u32[]{:S(2)}) copy-start(f32[2,1024]{1,0:T(2,128)} %get-tuple-element.185) | copy-start | bytes 24580
  381.2 11.9 %copy-start.38 = (f32[2,1024]{1,0:T(2,128)S(1)}, f32[2,1024]{1,0:T(2,128)}, u32[]{:S(2)}) copy-start(f32[2,1024]{1,0:T(2,128)} %get-tuple-element.186) | copy-start | bytes 24580
  381.2 11.9 %copy-start.44 = (f32[2,1024]{1,0:T(2,128)S(1)}, f32[2,1024]{1,0:T(2,128)}, u32[]{:S(2)}) copy-start(f32[2,1024]{1,0:T(2,128)} %get-tuple-element.182) | copy-start | bytes 24580
  385.3 26.5 %collective-permute-start.16 = (bf16[2,128,512]{2,1,0:T(8,128)(2,1)}, bf16[2,128,512]{2,1,0:T(8,128)(2,1)}, u32[]{:S(2)}, u32[]{:S(2)}) collective-permute-start(bf16[2,128,512]{2,1,0:T(8,128)(2,1)} %get-tuple-element.283), channel_id=1, source_target_pairs={{0,16},{2,18},{4,20},{6,22},{8,24},{10,26},{12,28},{14,30},{16,0},... | collective-permute-start | bytes 786440 | tf_op jit(solution)/shard_map/ppermute | solution.py:750
  390.6 41.5 %copy-start.3 = (bf16[640,1024]{1,0:T(8,128)(2,1)S(1)}, bf16[640,1024]{1,0:T(8,128)(2,1)}, u32[]{:S(2)}) copy-start(bf16[640,1024]{1,0:T(8,128)(2,1)} %copy-done.2) | copy-start | bytes 3932164
  390.6 41.5 %copy-start.5 = (bf16[640,1024]{1,0:T(8,128)(2,1)S(1)}, bf16[640,1024]{1,0:T(8,128)(2,1)}, u32[]{:S(2)}) copy-start(bf16[640,1024]{1,0:T(8,128)(2,1)} %pad_maximum_fusion.4.x_ref.refs_0_.x) | copy-start | bytes 3932164
  390.6 24.6 %collective-permute-start.15 = (bf16[2,128,512]{2,1,0:T(8,128)(2,1)}, bf16[2,128,512]{2,1,0:T(8,128)(2,1)S(1)}, u32[]{:S(2)}, u32[]{:S(2)}) collective-permute-start(bf16[2,128,512]{2,1,0:T(8,128)(2,1)} %get-tuple-element.284), channel_id=1, source_target_pairs={{0,8},{2,10},{4,12},{6,14},{8,0},{10,2},{12,4},{14,6},{16,24},{18,... | collective-permute-start | bytes 786440 | tf_op jit(solution)/shard_map/ppermute | solution.py:750
  393.1 1.3 collective-permute-start.17
  416.3 5.6 %collective-permute-start.19 = (bf16[1,128,512]{2,1,0:T(8,128)(2,1)S(1)}, bf16[1,128,512]{2,1,0:T(8,128)(2,1)}, u32[]{:S(2)}, u32[]{:S(2)}) collective-permute-start(bf16[1,128,512]{2,1,0:T(8,128)(2,1)S(1)} %add_convert_fusion.11), channel_id=1, source_target_pairs={{0,4},{2,6},{4,0},{6,2},{8,12},{10,14},{12,8},{14,10},{16,20},{18,... | collective-permute-start | bytes 393224 | tf_op jit(solution)/shard_map/ppermute | solution.py:750
  416.4 6.3 %collective-permute-start.18 = (bf16[1,128,512]{2,1,0:T(8,128)(2,1)S(1)}, bf16[1,128,512]{2,1,0:T(8,128)(2,1)}, u32[]{:S(2)}, u32[]{:S(2)}) collective-permute-start(bf16[1,128,512]{2,1,0:T(8,128)(2,1)S(1)} %add_convert_fusion.12), channel_id=1, source_target_pairs={{0,16},{2,18},{4,20},{6,22},{8,24},{10,26},{12,28},{14,30},{16,0},... | collective-permute-start | bytes 393224 | tf_op jit(solution)/shard_map/ppermute | solution.py:750
  416.5 5.4 %collective-permute-start.20 = (f32[24,512]{1,0:T(8,128)S(1)}, f32[24,512]{1,0:T(8,128)S(1)}, u32[]{:S(2)}, u32[]{:S(2)}) collective-permute-start(f32[24,512]{1,0:T(8,128)S(1)} %add.306), channel_id=1, source_target_pairs={{0,4},{2,6},{4,0},{6,2},{8,12},{10,14},{12,8},{14,10},{16,20},{18,... | collective-permute-start | bytes 147464 | tf_op jit(solution)/shard_map/ppermute | solution.py:750
  423.8 4.0 collective-permute-start.25
  424.9 4.7 collective-permute-start.23
  427.8 14.7 %collective-permute-start.26 = (bf16[1,128,512]{2,1,0:T(8,128)(2,1)S(1)}, bf16[1,128,512]{2,1,0:T(8,128)(2,1)S(1)}, u32[]{:S(2)}, u32[]{:S(2)}) collective-permute-start(bf16[1,128,512]{2,1,0:T(8,128)(2,1)S(1)} %maximum_bitcast_fusion.1), channel_id=1, source_target_pairs={{0,4},{2,6},{4,0},{6,2},{8,12},{10,14},{12,8},{14,10},{16,20},{18,... | collective-permute-start | bytes 393224 | tf_op jit(solution)/shard_map/ppermute | solution.py:750
  429.7 12.8 %collective-permute-start.24 = (bf16[1,128,512]{2,1,0:T(8,128)(2,1)S(1)}, bf16[1,128,512]{2,1,0:T(8,128)(2,1)S(1)}, u32[]{:S(2)}, u32[]{:S(2)}) collective-permute-start(bf16[1,128,512]{2,1,0:T(8,128)(2,1)S(1)} %maximum_bitcast_fusion), channel_id=1, source_target_pairs={{0,16},{2,18},{4,20},{6,22},{8,24},{10,26},{12,28},{14,30},{16,0},... | collective-permute-start | bytes 393224 | tf_op jit(solution)/shard_map/ppermute | solution.py:750
  430.9 11.5 %collective-permute-start.27 = (f32[24,512]{1,0:T(8,128)S(1)}, f32[24,512]{1,0:T(8,128)S(1)}, u32[]{:S(2)}, u32[]{:S(2)}) collective-permute-start(f32[24,512]{1,0:T(8,128)S(1)} %add.311), channel_id=1, source_target_pairs={{0,8},{2,10},{4,12},{6,14},{8,0},{10,2},{12,4},{14,6},{16,24},{18,... | collective-permute-start | bytes 147464 | tf_op jit(solution)/shard_map/ppermute | solution.py:750
  442.5 21.2 %collective-permute-start.29 = (bf16[2,128,512]{2,1,0:T(8,128)(2,1)S(1)}, bf16[2,128,512]{2,1,0:T(8,128)(2,1)S(1)}, u32[]{:S(2)}, u32[]{:S(2)}) collective-permute-start(bf16[2,128,512]{2,1,0:T(8,128)(2,1)S(1)} %pad_maximum_fusion.14), channel_id=1, source_target_pairs={{0,16},{2,18},{4,20},{6,22},{8,24},{10,26},{12,28},{14,30},{16,0},... | collective-permute-start | bytes 786440 | tf_op jit(solution)/shard_map/ppermute | solution.py:750
  443.1 20.5 %collective-permute-start.28 = (bf16[2,128,512]{2,1,0:T(8,128)(2,1)S(1)}, bf16[2,128,512]{2,1,0:T(8,128)(2,1)S(1)}, u32[]{:S(2)}, u32[]{:S(2)}) collective-permute-start(bf16[2,128,512]{2,1,0:T(8,128)(2,1)S(1)} %pad_maximum_fusion.13), channel_id=1, source_target_pairs={{0,8},{2,10},{4,12},{6,14},{8,0},{10,2},{12,4},{14,6},{16,24},{18,... | collective-permute-start | bytes 786440 | tf_op jit(solution)/shard_map/ppermute | solution.py:750
  445.2 8.4 %collective-permute-start.30 = (f32[24,512]{1,0:T(8,128)S(1)}, f32[24,512]{1,0:T(8,128)S(1)}, u32[]{:S(2)}, u32[]{:S(2)}) collective-permute-start(f32[24,512]{1,0:T(8,128)S(1)} %add.319), channel_id=1, source_target_pairs={{0,16},{2,18},{4,20},{6,22},{8,24},{10,26},{12,28},{14,30},{16,0},... | collective-permute-start | bytes 147464 | tf_op jit(solution)/shard_map/ppermute | solution.py:750
  463.7 9.2 %collective-permute-start.32 = (bf16[4,128,512]{2,1,0:T(8,128)(2,1)S(1)}, bf16[4,128,512]{2,1,0:T(8,128)(2,1)S(1)}, u32[]{:S(2)}, u32[]{:S(2)}) collective-permute-start(bf16[4,128,512]{2,1,0:T(8,128)(2,1)S(1)} %pad_maximum_fusion.12), channel_id=1, source_target_pairs={{0,8},{2,10},{4,12},{6,14},{8,0},{10,2},{12,4},{14,6},{16,24},{18,... | collective-permute-start | bytes 1572872 | tf_op jit(solution)/shard_map/ppermute | solution.py:750
  464.2 9.2 %collective-permute-start.31 = (bf16[4,128,512]{2,1,0:T(8,128)(2,1)S(1)}, bf16[4,128,512]{2,1,0:T(8,128)(2,1)S(1)}, u32[]{:S(2)}, u32[]{:S(2)}) collective-permute-start(bf16[4,128,512]{2,1,0:T(8,128)(2,1)S(1)} %pad_maximum_fusion.11), channel_id=1, source_target_pairs={{0,4},{2,6},{4,0},{6,2},{8,12},{10,14},{12,8},{14,10},{16,20},{18,... | collective-permute-start | bytes 1572872 | tf_op jit(solution)/shard_map/ppermute | solution.py:750
  473.6 6.7 %collective-permute-start.35 = (bf16[8,128,512]{2,1,0:T(8,128)(2,1)S(1)}, bf16[8,128,512]{2,1,0:T(8,128)(2,1)S(1)}, u32[]{:S(2)}, u32[]{:S(2)}) collective-permute-start(bf16[8,128,512]{2,1,0:T(8,128)(2,1)S(1)} %pad_maximum_fusion.9.refs_8_.refs_9_.refs_10_.refs_11_), channel_id=1, source_target_pairs={{0,2},{2,0},{4,6},{6,4},{8,10},{10,8},{12,14},{14,12},{16,18},{18,... | collective-permute-start | bytes 3145736 | tf_op jit(solution)/shard_map/ppermute | solution.py:750
  474.0 6.3 %collective-permute-start.34 = (bf16[8,128,512]{2,1,0:T(8,128)(2,1)S(1)}, bf16[8,128,512]{2,1,0:T(8,128)(2,1)}, u32[]{:S(2)}, u32[]{:S(2)}) collective-permute-start(bf16[8,128,512]{2,1,0:T(8,128)(2,1)S(1)} %pad_maximum_fusion.8.refs_0_.refs_1_.refs_2_.refs_3_), channel_id=1, source_target_pairs={{0,2},{2,0},{4,6},{6,4},{8,10},{10,8},{12,14},{14,12},{16,18},{18,... | collective-permute-start | bytes 3145736 | tf_op jit(solution)/shard_map/ppermute | solution.py:750
  474.4 4.1 collective-permute-start.33
  (46 other events, 216.7 us)
Sparse Core Ops, SparseCore 0:
  39.0 41.1 all-gather.4
  202.7 104.9 reduce-scatter.1
  325.6 91.9 all-gather.6
where the time goes:
time: 499 us; the launch traced here: 494 us
  Pallas kernels  304 us (61%)
  waiting for transfers between devices  78.2 us (16%)
  starting transfers between devices  40.3 us (8%)
  other arithmetic  28.5 us (6%)
  local copies, waits for them, and re-layouts  27.6 us (6%)
  between operations  15 us (3%)
    pallas_call x2, Pallas kernels, attn_group(): pl.pallas_call(functools.partial(attn_kernel, S, PD, CL, QB, HG, adding),...  112 us
    pallas_call x4, Pallas kernels, mlp_rows(): pl.pallas_call(functools.partial(mlp_kernel, rows_tile(rows, 640)), grid=...  80.9 us
    pallas_call x4, Pallas kernels, call(): pl.pallas_call(functools.partial(kernel, n, more), grid=(a[0].shape[1] //...  46.5 us
    ppermute x15, waiting for transfers between devices, shifted(): return lax.ppermute(value, 'shard', [(i, (i + j) % S) for i in range(S)])  40.7 us
    ppermute x21, waiting for transfers between devices, exchanged(): return lax.ppermute(value, 'rep', [(i, i ^ bit) for i in range(R)])  37.4 us
    ppermute x21, starting transfers between devices, exchanged(): return lax.ppermute(value, 'rep', [(i, i ^ bit) for i in range(R)])  23.3 us
    pallas_call x2, Pallas kernels, own_rows(): pl.pallas_call(own_kernel, grid=(1,), in_specs=[full((3, N, CW)), full((N...  19.6 us
    pallas_call x1, Pallas kernels, attn_grads(): pl.pallas_call(functools.partial(attn_grads_kernel, n, S, R), grid_spec=p...  19.3 us
  transfers between devices with their start and end apart: 39, of which 16 were waited for; matrix products, arithmetic and copies ran while one was open for 9% of the time, Pallas kernels for 53%

commit v1 on v0

--- a/solution.py
+++ b/solution.py
@@ -128,7 +128,7 @@
         + [SD((rows, width), BF), SD((rows, width), BF), SD((2, width), F32)] * back,
         scratch_shapes=[pltpu.VMEM((rows, width), F32)] * (2 * back),
         compiler_params=pltpu.CompilerParams(vmem_limit_bytes=60 * MIB),
-        cost_estimate=SMALL,
+        cost_estimate=pl.CostEstimate(flops=4 * rows * width * hidden, bytes_accessed=4 * (width * hidden + rows * hidden) + 6 * rows * width, transcendentals=2 * rows * hidden),
     )(x, dy, wu, bu, wd, gb)
 
 
@@ -759,25 +759,24 @@
     return got[0] if parts == 1 else jnp.concatenate(got, axis=1)
 
 
-def half_pieces(weight, me, S):
-    n = weight.shape[0] // 2
-    at = lax.axis_index("rep") % 2 * n
+def quarter_pieces(weight, me, S):
+    n = weight.shape[0] // 4
+    rep = lax.axis_index("rep")
+    at = (2 * (rep % 2) + (rep // 2) % 2) * n
     return [columns_for(weight, me, S, j, 1, at, n) for j in range(1, S)]
 
 
-def from_halves(weight, pieces, me, S, R):
-    first = lax.axis_index("rep") % 2 == 0
+def from_quarters(weight, pieces, me, S, R):
+    rep = lax.axis_index("rep")
+
+    def both(piece, other, first):
+        return jnp.concatenate([jnp.where(first, piece, other), jnp.where(first, other, piece)], axis=0)
+
     slots = [columns_for(weight, me, S, 0, 1)]
     for piece in pieces:
-        other = exchanged(piece, R, 1)
-        slots.append(jnp.concatenate([jnp.where(first, piece, other), jnp.where(first, other, piece)], axis=0))
+        pair = both(piece, exchanged(piece, R, 2), (rep // 2) % 2 == 0)
+        slots.append(both(pair, exchanged(pair, R, 1), rep % 2 == 0))
     return jnp.concatenate(canonical(slots, me, S, True), axis=0)
-
-
-def rep_pieces(weight, me, S, R, parts):
-    n = weight.shape[0] // R
-    rep = lax.axis_index("rep")
-    return [columns_for(weight, me, S, j, parts, rep * n, n) for j in range(1, S)]
 
 
 def from_rep(weight, pieces, me, S, parts):
@@ -916,18 +915,22 @@
     X = [[jnp.concatenate([prompt_in[m, 0], cont_in[m, 0].reshape(CR, D)], axis=0)] for m in range(MB)]
     DY = [[jnp.concatenate([prompt_cot[m, 0], cont_cot[m, 0].reshape(CR, D)], axis=0)] for m in range(MB)]
     away = lambda values: [shifted(v, S, j + 1) for j, v in enumerate(values)]
-    cut = half_pieces(up_weight, me, S)
+    cut = quarter_pieces(up_weight, me, S)
     vectors_in = (ln1_gain, ln1_bias, ln2_gain, ln2_bias, out_bias, down_bias, qkv_bias)
     (vectors_in, qkv_weight), cut = lax.optimization_barrier(((vectors_in, qkv_weight), cut))
-    small = jnp.concatenate([v.astype(F32).reshape(-1, CW) for v in vectors_in], axis=0)
-    slots = [small] + away([small] * (S - 1))
-    pieces_qkv = away(rep_pieces(qkv_weight, me, S, R, 3))
+    small = jnp.concatenate([v.reshape(-1, CW) for v in vectors_in], axis=0)
+    n = D // S // R
+    rep = lax.axis_index("rep")
+    at = lambda j, p: (rep * n, p * D + lax.rem(me + j, S) * CW)
+    pack = lambda j: jnp.concatenate([lax.dynamic_slice(qkv_weight, at(j, p), (n, CW)) for p in range(3)] + [small], axis=0)
+    packs = away([pack(j) for j in range(1, S)])
+    slots = [small.astype(F32)] + [g[3 * n :].astype(F32) for g in packs]
+    pieces_qkv = [jnp.concatenate([g[p * n : (p + 1) * n] for p in range(3)], axis=1) for g in packs]
     pieces_up = away(cut)
     src = [(X[m][0], DY[m][0]) for m in range(MB)]
     src[1:], _ = lax.optimization_barrier((src[1:], pieces_up))
-    pieces_up, _ = lax.optimization_barrier((pieces_up, (small, X, DY)))
-    src[0], _ = lax.optimization_barrier((src[0], (slots[1:])))
-    w_up = from_halves(up_weight, pieces_up, me, S, R)
+    pieces_up, _ = lax.optimization_barrier((pieces_up, (packs, X[0], DY[0])))
+    w_up = from_quarters(up_weight, pieces_up, me, S, R)
     w_qkv = from_rep(qkv_weight, pieces_qkv, me, S, 3)
 
     whole = jnp.stack(canonical(slots, me, S, True), axis=0)

time: 499 us -> 489 us (0.980)
  waiting for transfers between devices: 78.2 us -> 52.9 us
  starting transfers between devices: 40.3 us -> 46.7 us
    ppermute x15 -> x14, waiting for transfers between devices: 40.7 us -> 11.6 us  [shifted(): return lax.ppermute(value, 'shard', [(i, (i + j) % S) for i in range(S)])]
    ppermute x21 -> x22, starting transfers between devices: 23.3 us -> 30.9 us  [exchanged(): return lax.ppermute(value, 'rep', [(i, i ^ bit) for i in range(R)])]
    ppermute x21 -> x22, waiting for transfers between devices: 37.4 us -> 41.1 us  [exchanged(): return lax.ppermute(value, 'rep', [(i, i ^ bit) for i in range(R)])]
    unnamed x113 -> x101, local copies, waits for them, and re-layouts: 11.2 us -> 8.38 us
    ppermute x15 -> x14, starting transfers between devices: 16.9 us -> 15.6 us  [shifted(): return lax.ppermute(value, 'shard', [(i, (i + j) % S) for i in range(S)])]
  transfers between devices with their start and end apart: 39 -> 39, of which waited for: 16 -> 13; matrix products, arithmetic and copies ran while one was open for 9% -> 11% of each run, Pallas kernels for 53% -> 54%
where the time goes in v1:
time: 489 us; the launch traced here: 484 us
  Pallas kernels  304 us (62%)
  waiting for transfers between devices  52.9 us (11%)
  starting transfers between devices  46.7 us (10%)
  other arithmetic  33.1 us (7%)
  local copies, waits for them, and re-layouts  32 us (7%)
  between operations  15 us (3%)
    pallas_call x2, Pallas kernels, attn_group(): pl.pallas_call(functools.partial(attn_kernel, S, PD, CL, QB, HG, adding),...  112 us
    pallas_call x4, Pallas kernels, mlp_rows(): pl.pallas_call(functools.partial(mlp_kernel, rows_tile(rows, 640)), grid=...  80.9 us
    pallas_call x4, Pallas kernels, call(): pl.pallas_call(functools.partial(kernel, n, more), grid=(a[0].shape[1] //...  46.6 us
    ppermute x22, waiting for transfers between devices, exchanged(): return lax.ppermute(value, 'rep', [(i, i ^ bit) for i in range(R)])  41.1 us
    ppermute x22, starting transfers between devices, exchanged(): return lax.ppermute(value, 'rep', [(i, i ^ bit) for i in range(R)])  30.9 us
    pallas_call x2, Pallas kernels, own_rows(): pl.pallas_call(own_kernel, grid=(1,), in_specs=[full((3, N, CW)), full((N...  19.7 us
    pallas_call x1, Pallas kernels, attn_grads(): pl.pallas_call(functools.partial(attn_grads_kernel, n, S, R), grid_spec=p...  19.3 us
    ppermute x14, starting transfers between devices, shifted(): return lax.ppermute(value, 'shard', [(i, (i + j) % S) for i in range(S)])  15.6 us
  transfers between devices with their start and end apart: 39, of which 13 were waited for; matrix products, arithmetic and copies ran while one was open for 11% of the time, Pallas kernels for 54%

profile of v1, /device:TPU:0, one launch (start us, length us, event | category | flops | bytes accessed | tf_op | source)
XLA Modules:
  0.0 484.0 jit_solution(678712813838754911)
XLA Ops:
  7.3 1.9 dynamic_slice.80
  9.2 2.9 collective-permute-start.2
  19.0 1.8 slice_bitcast_fusion.1
  24.3 2.4 collective-permute-done.3
  26.7 1.8 collective-permute-start.4
  31.7 2.5 constant_dynamic-slice_fusion.9
  34.2 5.9 %collective-permute-done.4 = bf16[128,2048]{1,0:T(8,128)(2,1)} collective-permute-done((bf16[128,2048]{1,0:T(8,128)(2,1)}, bf16[128,2048]{1,0:T(8,128)(2,1)}, u32[]{:S(2)}, u32[]{:S(2)}) %collective-permute-start.4) | collective-permute-done | bytes 524320 | tf_op jit(solution)/shard_map/ppermute | solution.py:750
  49.0 1.8 broadcast_select_fusion.5
  52.0 2.6 pad_maximum_fusion.wu_ref
  54.6 20.3 %shard_map.307 = (bf16[640,2048]{1,0:T(8,128)(2,1)}, bf16[640,2048]{1,0:T(8,128)(2,1)}, bf16[640,1024]{1,0:T(8,128)(2,1)}, f32[1,2048]{1,0:T(1,128)}, bf16[640,1...) custom-call(bf16[640,1024]{1,0:T(8,128)(2,1)} %pad_maximum_fusion.4.x_ref.refs_0_.x, ...), custom_call_target="tpu_custom_call" | custom-call | flops 5368709120 | bytes 17563648 | tf_op jit(solution)/shard_map/pallas_call | solution.py:109
  74.9 20.2 %shard_map.308 = (bf16[640,2048]{1,0:T(8,128)(2,1)}, bf16[640,2048]{1,0:T(8,128)(2,1)}, bf16[640,1024]{1,0:T(8,128)(2,1)}, f32[1,2048]{1,0:T(1,128)}, bf16[640,1...) custom-call(bf16[640,1024]{1,0:T(8,128)(2,1)} %pad_maximum_fusion.6.x_ref.refs_0_.x, ...), custom_call_target="tpu_custom_call" | custom-call | flops 5368709120 | bytes 17563648 | tf_op jit(solution)/shard_map/pallas_call | solution.py:109
  95.2 20.2 %shard_map.306 = (bf16[640,2048]{1,0:T(8,128)(2,1)}, bf16[640,2048]{1,0:T(8,128)(2,1)}, bf16[640,1024]{1,0:T(8,128)(2,1)}, f32[1,2048]{1,0:T(1,128)}, bf16[640,1...) custom-call(bf16[640,1024]{1,0:T(8,128)(2,1)} %collective-permute-done.x_ref.refs_1_, ...), custom_call_target="tpu_custom_call" | custom-call | flops 5368709120 | bytes 17563648 | tf_op jit(solution)/shard_map/pallas_call | solution.py:109
  115.3 14.0 %shard_map.309.refs_6_ = bf16[16,256,1024]{2,1,0:T(8,128)(2,1)} custom-call(bf16[640,2048]{1,0:T(8,128)(2,1)} %get-tuple-element.139.refs_0_, bf16[640,2048]{1,0:T(8,128)(2,1)} %get-tuple-element.140.refs_1_, bf16[640,2048]{1,0:T(8,128)(2,1)} %get-tuple-element.141.refs_2_, bf16[640,1024]{1,0:T(8,128)(2,1)} %copy-done.2, ...), custom_call_target="tpu_custom_call" | custom-call | flops 1000000 | bytes 100000 | tf_op jit(solution)/shard_map/pallas_call | solution.py:491
  129.3 14.9 %shard_map.310.refs_2_ = bf16[16,256,1024]{2,1,0:T(8,128)(2,1)} custom-call(bf16[640,1024]{1,0:T(8,128)(2,1)} %get-tuple-element.133.refs_0_, bf16[640,1024]{1,0:T(8,128)(2,1)} %get-tuple-element.134.refs_1_, bf16[640,1024]{1,0:T(8,128)(2,1)} %get-tuple-element.135.refs_2_, ...), custom_call_target="tpu_custom_call", output_to_operand_aliasing={{}: (6, {})} | custom-call | flops 1000000 | bytes 100000 | tf_op jit(solution)/shard_map/pallas_call | solution.py:491
  144.2 2.0 broadcast_select_fusion.3
  146.2 1.9 pad_maximum_fusion.1.refs_6_.refs_7_.refs_8_.wqkv
  148.1 20.2 %shard_map.311 = (bf16[640,2048]{1,0:T(8,128)(2,1)}, bf16[640,2048]{1,0:T(8,128)(2,1)}, bf16[640,1024]{1,0:T(8,128)(2,1)}, f32[1,2048]{1,0:T(1,128)}, bf16[640,1...) custom-call(bf16[640,1024]{1,0:T(8,128)(2,1)} %collective-permute-done.6.x_ref.refs_1_, ...), custom_call_target="tpu_custom_call" | custom-call | flops 5368709120 | bytes 17563648 | tf_op jit(solution)/shard_map/pallas_call | solution.py:109
  168.3 9.6 %shard_map.312.refs_2_ = bf16[16,256,1024]{2,1,0:T(8,128)(2,1)} custom-call(bf16[640,2048]{1,0:T(8,128)(2,1)} %get-tuple-element.148.refs_0_, bf16[640,1024]{1,0:T(8,128)(2,1)} %collective-permute-done.7.dy_ref.refs_1_.refs_3_.refs_9_, bf16[16,256,1024]{2,1,0:T(8,128)(2,1)} %shard_map.310.refs_2_), custom_call_target="tpu_custom_call", output_to_operand_aliasing={{}: (2, {})} | custom-call | flops 1000000 | bytes 100000 | tf_op jit(solution)/shard_map/pallas_call | solution.py:491
  177.9 8.1 %shard_map.313 = bf16[16,256,1024]{2,1,0:T(8,128)(2,1)} custom-call(bf16[640,1024]{1,0:T(8,128)(2,1)} %get-tuple-element.146.refs_0_, bf16[640,2048]{1,0:T(8,128)(2,1)} %get-tuple-element.147.refs_1_, bf16[16,256,1024]{2,1,0:T(8,128)(2,1)} %shard_map.312.refs_2_), custom_call_target="tpu_custom_call", output_to_operand_aliasing={{}: (2, {})} | custom-call | flops 1000000 | bytes 100000 | tf_op jit(solution)/shard_map/pallas_call | solution.py:491
  186.7 55.9 %shard_map.314 = (bf16[640,1024]{1,0:T(8,128)(2,1)}, bf16[640,1024]{1,0:T(8,128)(2,1)}, bf16[3,1280,512]{2,1,0:T(8,128)(2,1)}, bf16[1280,512]{1,0:T(8,128)(2,1)}...) custom-call(s32[1]{0:T(128)} %bitcast.2.me_ref, ...), custom_call_target="tpu_custom_call" | custom-call | flops 1000000 | bytes 100000 | tf_op jit(solution)/shard_map/pallas_call | solution.py:386
  244.7 56.4 %shard_map.315 = (bf16[640,1024]{1,0:T(8,128)(2,1)}, bf16[640,1024]{1,0:T(8,128)(2,1)}, bf16[3,1280,512]{2,1,0:T(8,128)(2,1)}, bf16[1280,512]{1,0:T(8,128)(2,1)}...) custom-call(s32[1]{0:T(128)} %bitcast.2.me_ref, ...), custom_call_target="tpu_custom_call" | custom-call | flops 1000000 | bytes 100000 | tf_op jit(solution)/shard_map/pallas_call | solution.py:386
  302.1 1.6 collective-permute-start.10
  304.6 2.5 collective-permute-done.10
  309.7 19.3 %shard_map.316 = (bf16[16,128,512]{2,1,0:T(8,128)(2,1)}, bf16[16,128,512]{2,1,0:T(8,128)(2,1)}) custom-call(s32[2]{0:T(128)} %pad_add_fusion.q_ref, bf16[1280,1024]{1,0:T(8,128)(2,1)} %get-tuple-element.159.refs_0_, bf16[1280,1024]{1,0:T(8,128)(2,1)} %get-tuple-element.160.refs_1_, bf16[3,1280,512]{2,1,0:T(8,128)(2,1)} %get-tuple-element.167.refs_2_.dl, ...), custom_call_target="tpu_custom_call" | custom-call | flops 1000000 | bytes 100000 | tf_op jit(solution)/shard_map/pallas_call | solution.py:582
  330.6 2.3 slice.183
  334.3 2.8 add_convert_fusion.2
  337.1 1.6 collective-permute-start.12
  338.8 2.3 add_convert_fusion
  344.9 9.8 %shard_map.317 = (bf16[640,1024]{1,0:T(8,128)(2,1)}, bf16[640,1024]{1,0:T(8,128)(2,1)}, f32[2,1024]{1,0:T(2,128)}) custom-call(bf16[3,1280,512]{2,1,0:T(8,128)(2,1)} %get-tuple-element.167.refs_2_.dl, bf16[1280,512]{1,0:T(8,128)(2,1)} %get-tuple-element.163.refs_4_.ctx, bf16[1024,1536]{1,0:T(8,128)(2,1)} %pad_maximum_fusion.1.refs_6_.refs_7_.refs_8_.wqkv, ...), custom_call_target="tpu_custom_call" | custom-call | flops 1000000 | bytes 100000 | tf_op jit(solution)/shard_map/pallas_call | solution.py:667
  354.7 9.9 %shard_map.318 = (bf16[640,1024]{1,0:T(8,128)(2,1)}, bf16[640,1024]{1,0:T(8,128)(2,1)}, f32[2,1024]{1,0:T(2,128)}) custom-call(bf16[3,1280,512]{2,1,0:T(8,128)(2,1)} %get-tuple-element.173.refs_3_.dl, bf16[1280,512]{1,0:T(8,128)(2,1)} %get-tuple-element.164.refs_5_.ctx, bf16[1024,1536]{1,0:T(8,128)(2,1)} %pad_maximum_fusion.1.refs_6_.refs_7_.refs_8_.wqkv, ...), custom_call_target="tpu_custom_call" | custom-call | flops 1000000 | bytes 100000 | tf_op jit(solution)/shard_map/pallas_call | solution.py:667
  364.6 11.4 %collective-permute-done.14 = bf16[4,128,512]{2,1,0:T(8,128)(2,1)S(1)} collective-permute-done((bf16[4,128,512]{2,1,0:T(8,128)(2,1)}, bf16[4,128,512]{2,1,0:T(8,128)(2,1)S(1)}, u32[]{:S(2)}, u32[]{:S(2)}) %collective-permute-start.14) | collective-permute-done | bytes 524320 | tf_op jit(solution)/shard_map/ppermute | solution.py:750
  376.1 1.9 add_convert_fusion.6
  378.9 12.0 %collective-permute-start.16 = (bf16[2,128,512]{2,1,0:T(8,128)(2,1)}, bf16[2,128,512]{2,1,0:T(8,128)(2,1)S(1)}, u32[]{:S(2)}, u32[]{:S(2)}) collective-permute-start(bf16[2,128,512]{2,1,0:T(8,128)(2,1)} %get-tuple-element.279), channel_id=1, source_target_pairs={{0,16},{2,18},{4,20},{6,22},{8,24},{10,26},{12,28},{14,30},{16,0},... | collective-permute-start | bytes 786440 | tf_op jit(solution)/shard_map/ppermute | solution.py:750
  392.3 7.6 %collective-permute-done.15 = bf16[2,128,512]{2,1,0:T(8,128)(2,1)} collective-permute-done((bf16[2,128,512]{2,1,0:T(8,128)(2,1)}, bf16[2,128,512]{2,1,0:T(8,128)(2,1)}, u32[]{:S(2)}, u32[]{:S(2)}) %collective-permute-start.15) | collective-permute-done | bytes 262176 | tf_op jit(solution)/shard_map/ppermute | solution.py:750
  400.9 2.4 collective-permute-start.18
  403.2 1.6 add_convert_fusion.11
  404.9 2.0 collective-permute-start.20
  406.9 3.7 collective-permute-done.20
  416.2 2.5 collective-permute-done.23
  419.3 2.5 collective-permute-start.27
  424.5 6.7 %shard_map.319 = (bf16[2,512,1024]{2,1,0:T(8,128)(2,1)}, bf16[2,128,1024]{2,1,0:T(8,128)(2,1)}, f32[2,512,1024]{2,1,0:T(8,128)}, f32[2,128,1024]{2,1,0:T(8,128)}) custom-call(bf16[640,1024]{1,0:T(8,128)(2,1)} %pad_maximum_fusion.4.x_ref.refs_0_.x, bf16[640,1024]{1,0:T(8,128)(2,1)S(1)} %copy-done.3, bf16[640,1024]{1,0:T(8,128)(2,1)S(1)} %copy-done.10, ...), custom_call_target="tpu_custom_call" | custom-call | flops 1000000 | bytes 100000 | tf_op jit(solution)/shard_map/pallas_call | solution.py:721
  431.4 1.9 collective-permute-start.29
  434.4 8.3 %collective-permute-done.30 = f32[24,512]{1,0:T(8,128)S(1)} collective-permute-done((f32[24,512]{1,0:T(8,128)S(1)}, f32[24,512]{1,0:T(8,128)S(1)}, u32[]{:S(2)}, u32[]{:S(2)}) %collective-permute-start.30) | collective-permute-done | bytes 49184 | tf_op jit(solution)/shard_map/ppermute | solution.py:750
  442.7 3.4 copy-done.5
  446.0 6.5 %shard_map.320 = (f32[2048,1024]{1,0:T(8,128)}, f32[512,4096]{1,0:T(8,128)}) custom-call(bf16[16,256,1024]{2,1,0:T(8,128)(2,1)S(1)} %bitcast.74), custom_call_target="tpu_custom_call" | custom-call | flops 1000000 | bytes 100000 | tf_op jit(solution)/shard_map/pallas_call | solution.py:524
  454.3 6.1 %shard_map.321 = (bf16[2,512,1024]{2,1,0:T(8,128)(2,1)}, bf16[2,128,1024]{2,1,0:T(8,128)(2,1)}, f32[2,512,1024]{2,1,0:T(8,128)}, f32[2,128,1024]{2,1,0:T(8,128)}) custom-call(bf16[640,1024]{1,0:T(8,128)(2,1)S(1)} %copy-done.4, bf16[640,1024]{1,0:T(8,128)(2,1)S(1)} %copy-done.1, ...), custom_call_target="tpu_custom_call", output_to_operand_aliasing={{0}: (7, {}), {1}: (8, {}), {2}: (9, {}), {3}: (10, {})} | custom-call | flops 1000000 | bytes 100000 | tf_op jit(solution)/shard_map/pallas_call | solution.py:721
  464.9 3.5 collective-permute-done.33
  470.3 6.3 %shard_map.322 = (f32[512,1024]{1,0:T(8,128)}, f32[512,3072]{1,0:T(8,128)}) custom-call(s32[2]{0:T(128)S(1)} %copy-done.12, bf16[8,128,512]{2,1,0:T(8,128)(2,1)S(1)} %pad_maximum_fusion.9.refs_0_.refs_1_.refs_2_.refs_3_, bf16[8,128,512]{2,1,0:T(8,128)(2,1)S(1)} %pad_maximum_fusion.9.refs_0_.refs_1_.refs_2_.refs_3_, ...), custom_call_target="tpu_custom_call" | custom-call | flops 1000000 | bytes 100000 | tf_op jit(solution)/shard_map/pallas_call | solution.py:632
  (245 shorter events, 59.5 us)
Async XLA Ops:
  7.2 137.0 %all-gather.5.cloned.1.call-start = ((), (), s32[]{:S(2)}) async-start(), calls=%async_computation.2 | async-start | bytes 1671168 | tf_op jit(solution)/shard_map/all_gather | solution.py:783
  9.2 17.5 %collective-permute-start.2 = (bf16[128,2048]{1,0:T(8,128)(2,1)}, bf16[128,2048]{1,0:T(8,128)(2,1)}, u32[]{:S(2)}, u32[]{:S(2)}) collective-permute-start(bf16[128,2048]{1,0:T(8,128)(2,1)} %dynamic_slice.80), channel_id=1, source_target_pairs={{0,1},{1,0},{2,3},{3,2},{4,5},{5,4},{6,7},{7,6},{8,9},{9,8},{10,11... | collective-permute-start | bytes 1572872 | tf_op jit(solution)/shard_map/ppermute | solution.py:734
  17.9 8.8 %collective-permute-start.3 = (bf16[105,512]{1,0:T(8,128)(2,1)S(1)}, bf16[105,512]{1,0:T(8,128)(2,1)S(1)}, u32[]{:S(2)}, u32[]{:S(2)}) collective-permute-start(bf16[105,512]{1,0:T(8,128)(2,1)S(1)} %concatenate.73), channel_id=1, source_target_pairs={{0,1},{1,0},{2,3},{3,2},{4,5},{5,4},{6,7},{7,6},{8,9},{9,8},{10,11... | collective-permute-start | bytes 322568 | tf_op jit(solution)/shard_map/ppermute | solution.py:734
  26.7 13.4 %collective-permute-start.4 = (bf16[128,2048]{1,0:T(8,128)(2,1)}, bf16[128,2048]{1,0:T(8,128)(2,1)}, u32[]{:S(2)}, u32[]{:S(2)}) collective-permute-start(bf16[128,2048]{1,0:T(8,128)(2,1)} %collective-permute-done.2), channel_id=1, source_target_pairs={{0,4},{2,6},{4,0},{6,2},{8,12},{10,14},{12,8},{14,10},{16,20},{18,... | collective-permute-start | bytes 1572872 | tf_op jit(solution)/shard_map/ppermute | solution.py:750
  28.5 66.7 %collective-permute-start = (bf16[640,1024]{1,0:T(8,128)(2,1)}, bf16[640,1024]{1,0:T(8,128)(2,1)}, u32[]{:S(2)}, u32[]{:S(2)}) collective-permute-start(bf16[640,1024]{1,0:T(8,128)(2,1)} %pad_maximum_fusion.4.x_ref.refs_0_.x), channel_id=1, source_target_pairs={{0,1},{1,0},{2,3},{3,2},{4,5},{5,4},{6,7},{7,6},{8,9},{9,8},{10,11... | collective-permute-start | bytes 3932168 | tf_op jit(solution)/shard_map/ppermute | solution.py:734
  30.0 65.2 %collective-permute-start.1 = (bf16[640,1024]{1,0:T(8,128)(2,1)S(1)}, bf16[640,1024]{1,0:T(8,128)(2,1)}, u32[]{:S(2)}, u32[]{:S(2)}) collective-permute-start(bf16[640,1024]{1,0:T(8,128)(2,1)S(1)} %pad_maximum_fusion.5.dy_ref.refs_3_.refs_2_.refs_6_.refs_1_), channel_id=1, source_target_pairs={{0,1},{1,0},{2,3},{3,2},{4,5},{5,4},{6,7},{7,6},{8,9},{9,8},{10,11... | collective-permute-start | bytes 3932168 | tf_op jit(solution)/shard_map/ppermute | solution.py:734
  42.5 6.6 %collective-permute-start.5 = (bf16[256,2048]{1,0:T(8,128)(2,1)}, bf16[256,2048]{1,0:T(8,128)(2,1)}, u32[]{:S(2)}, u32[]{:S(2)}) collective-permute-start(bf16[256,2048]{1,0:T(8,128)(2,1)} %pad_maximum_fusion.8), channel_id=1, source_target_pairs={{0,2},{2,0},{4,6},{6,4},{8,10},{10,8},{12,14},{14,12},{16,18},{18,... | collective-permute-start | bytes 3145736 | tf_op jit(solution)/shard_map/ppermute | solution.py:750
  45.6 255.5 %reduce-scatter.2.cloned.1.call-start = ((), (), s32[]{:S(2)}) async-start(), calls=%async_computation.1 | async-start | bytes 8912896 | tf_op jit(solution)/shard_map/reduce_scatter | solution.py:989
  47.0 101.1 %collective-permute-start.6 = (bf16[640,1024]{1,0:T(8,128)(2,1)}, bf16[640,1024]{1,0:T(8,128)(2,1)}, u32[]{:S(2)}, u32[]{:S(2)}) collective-permute-start(bf16[640,1024]{1,0:T(8,128)(2,1)} %pad_maximum_fusion.6.x_ref.refs_0_.x), channel_id=1, source_target_pairs={{0,1},{1,0},{2,3},{3,2},{4,5},{5,4},{6,7},{7,6},{8,9},{9,8},{10,11... | collective-permute-start | bytes 3932168 | tf_op jit(solution)/shard_map/ppermute | solution.py:734
  48.4 99.7 %collective-permute-start.7 = (bf16[640,1024]{1,0:T(8,128)(2,1)S(1)}, bf16[640,1024]{1,0:T(8,128)(2,1)}, u32[]{:S(2)}, u32[]{:S(2)}) collective-permute-start(bf16[640,1024]{1,0:T(8,128)(2,1)S(1)} %pad_maximum_fusion.7.dy_ref.refs_5_.refs_2_.refs_8_.refs_1_), channel_id=1, source_target_pairs={{0,1},{1,0},{2,3},{3,2},{4,5},{5,4},{6,7},{7,6},{8,9},{9,8},{10,11... | collective-permute-start | bytes 3932168 | tf_op jit(solution)/shard_map/ppermute | solution.py:734
  129.3 14.9 %copy-start.21 = (bf16[512,512]{1,0:T(8,128)(2,1)S(1)}, bf16[512,512]{1,0:T(8,128)(2,1)}, u32[]{:S(2)}) copy-start(bf16[512,512]{1,0:T(8,128)(2,1)} %get-tuple-element.267) | copy-start | bytes 1572868
  129.3 14.9 %copy-start.22 = (bf16[512,512]{1,0:T(8,128)(2,1)S(1)}, bf16[512,512]{1,0:T(8,128)(2,1)}, u32[]{:S(2)}) copy-start(bf16[512,512]{1,0:T(8,128)(2,1)} %get-tuple-element.268) | copy-start | bytes 1572868
  186.0 256.6 %all-gather.7.cloned.1.call-start = ((), (), s32[]{:S(2)}) async-start(), calls=%async_computation.3 | async-start | bytes 8912896 | tf_op jit(solution)/shard_map/all_gather | solution.py:1011
  242.6 66.3 %collective-permute-start.8 = (bf16[640,1024]{1,0:T(8,128)(2,1)}, bf16[640,1024]{1,0:T(8,128)(2,1)S(1)}, u32[]{:S(2)}, u32[]{:S(2)}) collective-permute-start(bf16[640,1024]{1,0:T(8,128)(2,1)} %get-tuple-element.157), channel_id=1, source_target_pairs={{0,1},{1,0},{2,3},{3,2},{4,5},{5,4},{6,7},{7,6},{8,9},{9,8},{10,11... | collective-permute-start | bytes 3932168 | tf_op jit(solution)/shard_map/ppermute | solution.py:734
  244.2 64.7 %collective-permute-start.9 = (bf16[640,1024]{1,0:T(8,128)(2,1)}, bf16[640,1024]{1,0:T(8,128)(2,1)}, u32[]{:S(2)}, u32[]{:S(2)}) collective-permute-start(bf16[640,1024]{1,0:T(8,128)(2,1)} %get-tuple-element.158), channel_id=1, source_target_pairs={{0,1},{1,0},{2,3},{3,2},{4,5},{5,4},{6,7},{7,6},{8,9},{9,8},{10,11... | collective-permute-start | bytes 3932168 | tf_op jit(solution)/shard_map/ppermute | solution.py:734
  302.1 5.0 %collective-permute-start.10 = (bf16[64,1024]{1,0:T(8,128)(2,1)S(1)}, bf16[64,1024]{1,0:T(8,128)(2,1)S(1)}, u32[]{:S(2)}, u32[]{:S(2)}) collective-permute-start(bf16[64,1024]{1,0:T(8,128)(2,1)S(1)} %dynamic-slice_bitcast_fusion), channel_id=1, source_target_pairs={{0,1},{1,0},{2,3},{3,2},{4,5},{5,4},{6,7},{7,6},{8,9},{9,8},{10,11... | collective-permute-start | bytes 393224 | tf_op jit(solution)/shard_map/ppermute | solution.py:734
  308.9 20.1 %copy-start.8 = (bf16[640,1024]{1,0:T(8,128)(2,1)}, bf16[640,1024]{1,0:T(8,128)(2,1)S(1)}, u32[]{:S(2)}) copy-start(bf16[640,1024]{1,0:T(8,128)(2,1)S(1)} %collective-permute-done.8.refs_3_) | copy-start | bytes 3932164
  330.5 3.8 collective-permute-start.11
  332.9 5.8 %collective-permute-start.13 = (bf16[8,128,512]{2,1,0:T(8,128)(2,1)}, bf16[8,128,512]{2,1,0:T(8,128)(2,1)}, u32[]{:S(2)}, u32[]{:S(2)}) collective-permute-start(bf16[8,128,512]{2,1,0:T(8,128)(2,1)} %slice.183), channel_id=1, source_target_pairs={{0,2},{2,0},{4,6},{6,4},{8,10},{10,8},{12,14},{14,12},{16,18},{18,... | collective-permute-start | bytes 3145736 | tf_op jit(solution)/shard_map/ppermute | solution.py:750
  337.1 27.5 %collective-permute-start.12 = (bf16[4,128,512]{2,1,0:T(8,128)(2,1)}, bf16[4,128,512]{2,1,0:T(8,128)(2,1)}, u32[]{:S(2)}, u32[]{:S(2)}) collective-permute-start(bf16[4,128,512]{2,1,0:T(8,128)(2,1)} %get-tuple-element.262), channel_id=1, source_target_pairs={{0,4},{2,6},{4,0},{6,2},{8,12},{10,14},{12,8},{14,10},{16,20},{18,... | collective-permute-start | bytes 1572872 | tf_op jit(solution)/shard_map/ppermute | solution.py:750
  341.0 35.0 %collective-permute-start.14 = (bf16[4,128,512]{2,1,0:T(8,128)(2,1)}, bf16[4,128,512]{2,1,0:T(8,128)(2,1)S(1)}, u32[]{:S(2)}, u32[]{:S(2)}) collective-permute-start(bf16[4,128,512]{2,1,0:T(8,128)(2,1)} %get-tuple-element.261), channel_id=1, source_target_pairs={{0,8},{2,10},{4,12},{6,14},{8,0},{10,2},{12,4},{14,6},{16,24},{18,... | collective-permute-start | bytes 1572872 | tf_op jit(solution)/shard_map/ppermute | solution.py:750
  342.7 67.9 %collective-permute-start.21 = (bf16[640,1024]{1,0:T(8,128)(2,1)}, bf16[640,1024]{1,0:T(8,128)(2,1)S(1)}, u32[]{:S(2)}, u32[]{:S(2)}) collective-permute-start(bf16[640,1024]{1,0:T(8,128)(2,1)} %get-tuple-element.195), channel_id=1, source_target_pairs={{0,1},{1,0},{2,3},{3,2},{4,5},{5,4},{6,7},{7,6},{8,9},{9,8},{10,11... | collective-permute-start | bytes 3932168 | tf_op jit(solution)/shard_map/ppermute | solution.py:734
  344.2 66.3 %collective-permute-start.22 = (bf16[640,1024]{1,0:T(8,128)(2,1)}, bf16[640,1024]{1,0:T(8,128)(2,1)}, u32[]{:S(2)}, u32[]{:S(2)}) collective-permute-start(bf16[640,1024]{1,0:T(8,128)(2,1)} %get-tuple-element.196), channel_id=1, source_target_pairs={{0,1},{1,0},{2,3},{3,2},{4,5},{5,4},{6,7},{7,6},{8,9},{9,8},{10,11... | collective-permute-start | bytes 3932168 | tf_op jit(solution)/shard_map/ppermute | solution.py:734
  364.6 26.3 %copy-start.37 = (f32[2,1024]{1,0:T(2,128)S(1)}, f32[2,1024]{1,0:T(2,128)}, u32[]{:S(2)}) copy-start(f32[2,1024]{1,0:T(2,128)} %get-tuple-element.181) | copy-start | bytes 24580
  364.6 26.3 %copy-start.40 = (f32[2,1024]{1,0:T(2,128)S(1)}, f32[2,1024]{1,0:T(2,128)}, u32[]{:S(2)}) copy-start(f32[2,1024]{1,0:T(2,128)} %get-tuple-element.182) | copy-start | bytes 24580
  364.6 26.3 %copy-start.46 = (f32[2,1024]{1,0:T(2,128)S(1)}, f32[2,1024]{1,0:T(2,128)}, u32[]{:S(2)}) copy-start(f32[2,1024]{1,0:T(2,128)} %get-tuple-element.172) | copy-start | bytes 24580
  364.6 26.3 %copy-start.47 = (f32[2,1024]{1,0:T(2,128)S(1)}, f32[2,1024]{1,0:T(2,128)}, u32[]{:S(2)}) copy-start(f32[2,1024]{1,0:T(2,128)} %get-tuple-element.178) | copy-start | bytes 24580
  377.9 21.9 %collective-permute-start.15 = (bf16[2,128,512]{2,1,0:T(8,128)(2,1)}, bf16[2,128,512]{2,1,0:T(8,128)(2,1)}, u32[]{:S(2)}, u32[]{:S(2)}) collective-permute-start(bf16[2,128,512]{2,1,0:T(8,128)(2,1)} %get-tuple-element.280), channel_id=1, source_target_pairs={{0,8},{2,10},{4,12},{6,14},{8,0},{10,2},{12,4},{14,6},{16,24},{18,... | collective-permute-start | bytes 786440 | tf_op jit(solution)/shard_map/ppermute | solution.py:750
  378.9 43.0 %copy-start.3 = (bf16[640,1024]{1,0:T(8,128)(2,1)S(1)}, bf16[640,1024]{1,0:T(8,128)(2,1)}, u32[]{:S(2)}) copy-start(bf16[640,1024]{1,0:T(8,128)(2,1)} %copy-done.2) | copy-start | bytes 3932164
  378.9 21.0 %collective-permute-start.16 = (bf16[2,128,512]{2,1,0:T(8,128)(2,1)}, bf16[2,128,512]{2,1,0:T(8,128)(2,1)S(1)}, u32[]{:S(2)}, u32[]{:S(2)}) collective-permute-start(bf16[2,128,512]{2,1,0:T(8,128)(2,1)} %get-tuple-element.279), channel_id=1, source_target_pairs={{0,16},{2,18},{4,20},{6,22},{8,24},{10,26},{12,28},{14,30},{16,0},... | collective-permute-start | bytes 786440 | tf_op jit(solution)/shard_map/ppermute | solution.py:750
  391.0 1.3 collective-permute-start.17
  400.9 9.7 %collective-permute-start.18 = (bf16[1,128,512]{2,1,0:T(8,128)(2,1)S(1)}, bf16[1,128,512]{2,1,0:T(8,128)(2,1)}, u32[]{:S(2)}, u32[]{:S(2)}) collective-permute-start(bf16[1,128,512]{2,1,0:T(8,128)(2,1)S(1)} %add_convert_fusion.12), channel_id=1, source_target_pairs={{0,16},{2,18},{4,20},{6,22},{8,24},{10,26},{12,28},{14,30},{16,0},... | collective-permute-start | bytes 393224 | tf_op jit(solution)/shard_map/ppermute | solution.py:750
  404.8 5.8 %collective-permute-start.19 = (bf16[1,128,512]{2,1,0:T(8,128)(2,1)}, bf16[1,128,512]{2,1,0:T(8,128)(2,1)}, u32[]{:S(2)}, u32[]{:S(2)}) collective-permute-start(bf16[1,128,512]{2,1,0:T(8,128)(2,1)} %add_convert_fusion.11), channel_id=1, source_target_pairs={{0,4},{2,6},{4,0},{6,2},{8,12},{10,14},{12,8},{14,10},{16,20},{18,... | collective-permute-start | bytes 393224 | tf_op jit(solution)/shard_map/ppermute | solution.py:750
  404.9 5.7 %collective-permute-start.20 = (f32[24,512]{1,0:T(8,128)S(1)}, f32[24,512]{1,0:T(8,128)S(1)}, u32[]{:S(2)}, u32[]{:S(2)}) collective-permute-start(f32[24,512]{1,0:T(8,128)S(1)} %add.318), channel_id=1, source_target_pairs={{0,4},{2,6},{4,0},{6,2},{8,12},{10,14},{12,8},{14,10},{16,20},{18,... | collective-permute-start | bytes 147464 | tf_op jit(solution)/shard_map/ppermute | solution.py:750
  406.9 15.0 %copy-start.9 = (bf16[640,1024]{1,0:T(8,128)(2,1)S(1)}, bf16[640,1024]{1,0:T(8,128)(2,1)}, u32[]{:S(2)}) copy-start(bf16[640,1024]{1,0:T(8,128)(2,1)} %copy-done.8) | copy-start | bytes 3932164
  411.7 4.0 collective-permute-start.25
  414.3 4.3 collective-permute-start.23
  415.7 15.5 %collective-permute-start.26 = (bf16[1,128,512]{2,1,0:T(8,128)(2,1)S(1)}, bf16[1,128,512]{2,1,0:T(8,128)(2,1)S(1)}, u32[]{:S(2)}, u32[]{:S(2)}) collective-permute-start(bf16[1,128,512]{2,1,0:T(8,128)(2,1)S(1)} %maximum_bitcast_fusion.1), channel_id=1, source_target_pairs={{0,4},{2,6},{4,0},{6,2},{8,12},{10,14},{12,8},{14,10},{16,20},{18,... | collective-permute-start | bytes 393224 | tf_op jit(solution)/shard_map/ppermute | solution.py:750
  418.7 12.6 %collective-permute-start.24 = (bf16[1,128,512]{2,1,0:T(8,128)(2,1)S(1)}, bf16[1,128,512]{2,1,0:T(8,128)(2,1)S(1)}, u32[]{:S(2)}, u32[]{:S(2)}) collective-permute-start(bf16[1,128,512]{2,1,0:T(8,128)(2,1)S(1)} %maximum_bitcast_fusion), channel_id=1, source_target_pairs={{0,16},{2,18},{4,20},{6,22},{8,24},{10,26},{12,28},{14,30},{16,0},... | collective-permute-start | bytes 393224 | tf_op jit(solution)/shard_map/ppermute | solution.py:750
  419.3 11.9 %collective-permute-start.27 = (f32[24,512]{1,0:T(8,128)S(1)}, f32[24,512]{1,0:T(8,128)S(1)}, u32[]{:S(2)}, u32[]{:S(2)}) collective-permute-start(f32[24,512]{1,0:T(8,128)S(1)} %add.323), channel_id=1, source_target_pairs={{0,8},{2,10},{4,12},{6,14},{8,0},{10,2},{12,4},{14,6},{16,24},{18,... | collective-permute-start | bytes 147464 | tf_op jit(solution)/shard_map/ppermute | solution.py:750
  431.3 21.3 %collective-permute-start.28 = (bf16[2,128,512]{2,1,0:T(8,128)(2,1)S(1)}, bf16[2,128,512]{2,1,0:T(8,128)(2,1)S(1)}, u32[]{:S(2)}, u32[]{:S(2)}) collective-permute-start(bf16[2,128,512]{2,1,0:T(8,128)(2,1)S(1)} %pad_maximum_fusion.14), channel_id=1, source_target_pairs={{0,8},{2,10},{4,12},{6,14},{8,0},{10,2},{12,4},{14,6},{16,24},{18,... | collective-permute-start | bytes 786440 | tf_op jit(solution)/shard_map/ppermute | solution.py:750
  431.4 21.2 %collective-permute-start.29 = (bf16[2,128,512]{2,1,0:T(8,128)(2,1)S(1)}, bf16[2,128,512]{2,1,0:T(8,128)(2,1)S(1)}, u32[]{:S(2)}, u32[]{:S(2)}) collective-permute-start(bf16[2,128,512]{2,1,0:T(8,128)(2,1)S(1)} %pad_maximum_fusion.15), channel_id=1, source_target_pairs={{0,16},{2,18},{4,20},{6,22},{8,24},{10,26},{12,28},{14,30},{16,0},... | collective-permute-start | bytes 786440 | tf_op jit(solution)/shard_map/ppermute | solution.py:750
  433.2 9.4 %collective-permute-start.30 = (f32[24,512]{1,0:T(8,128)S(1)}, f32[24,512]{1,0:T(8,128)S(1)}, u32[]{:S(2)}, u32[]{:S(2)}) collective-permute-start(f32[24,512]{1,0:T(8,128)S(1)} %add.331), channel_id=1, source_target_pairs={{0,16},{2,18},{4,20},{6,22},{8,24},{10,26},{12,28},{14,30},{16,0},... | collective-permute-start | bytes 147464 | tf_op jit(solution)/shard_map/ppermute | solution.py:750
  452.7 9.2 %collective-permute-start.31 = (bf16[4,128,512]{2,1,0:T(8,128)(2,1)S(1)}, bf16[4,128,512]{2,1,0:T(8,128)(2,1)S(1)}, u32[]{:S(2)}, u32[]{:S(2)}) collective-permute-start(bf16[4,128,512]{2,1,0:T(8,128)(2,1)S(1)} %pad_maximum_fusion.12), channel_id=1, source_target_pairs={{0,4},{2,6},{4,0},{6,2},{8,12},{10,14},{12,8},{14,10},{16,20},{18,... | collective-permute-start | bytes 1572872 | tf_op jit(solution)/shard_map/ppermute | solution.py:750
  453.8 9.6 %collective-permute-start.32 = (bf16[4,128,512]{2,1,0:T(8,128)(2,1)S(1)}, bf16[4,128,512]{2,1,0:T(8,128)(2,1)S(1)}, u32[]{:S(2)}, u32[]{:S(2)}) collective-permute-start(bf16[4,128,512]{2,1,0:T(8,128)(2,1)S(1)} %pad_maximum_fusion.13), channel_id=1, source_target_pairs={{0,8},{2,10},{4,12},{6,14},{8,0},{10,2},{12,4},{14,6},{16,24},{18,... | collective-permute-start | bytes 1572872 | tf_op jit(solution)/shard_map/ppermute | solution.py:750
  463.5 6.7 %collective-permute-start.34 = (bf16[8,128,512]{2,1,0:T(8,128)(2,1)S(1)}, bf16[8,128,512]{2,1,0:T(8,128)(2,1)S(1)}, u32[]{:S(2)}, u32[]{:S(2)}) collective-permute-start(bf16[8,128,512]{2,1,0:T(8,128)(2,1)S(1)} %pad_maximum_fusion.9.refs_0_.refs_1_.refs_2_.refs_3_), channel_id=1, source_target_pairs={{0,2},{2,0},{4,6},{6,4},{8,10},{10,8},{12,14},{14,12},{16,18},{18,... | collective-permute-start | bytes 3145736 | tf_op jit(solution)/shard_map/ppermute | solution.py:750
  463.7 6.5 %collective-permute-start.35 = (bf16[8,128,512]{2,1,0:T(8,128)(2,1)S(1)}, bf16[8,128,512]{2,1,0:T(8,128)(2,1)}, u32[]{:S(2)}, u32[]{:S(2)}) collective-permute-start(bf16[8,128,512]{2,1,0:T(8,128)(2,1)S(1)} %pad_maximum_fusion.10.refs_8_.refs_9_.refs_10_.refs_11_), channel_id=1, source_target_pairs={{0,2},{2,0},{4,6},{6,4},{8,10},{10,8},{12,14},{14,12},{16,18},{18,... | collective-permute-start | bytes 3145736 | tf_op jit(solution)/shard_map/ppermute | solution.py:750
  464.3 4.1 collective-permute-start.33
  (40 other events, 197.4 us)
Sparse Core Ops, SparseCore 0:
  45.7 40.8 all-gather.4
  186.1 105.7 reduce-scatter.1
  309.1 92.2 all-gather.6

commit v2 on v1

--- a/solution.py
+++ b/solution.py
@@ -676,6 +676,60 @@
     )(dl, ctx, wqkv, wo, x, yp, g2, gb)
 
 
+def own_both_kernel(act, dpre, wu, wd, dl, ctx, wqkv, wo, x, gb, y, g, ln, yacc, d1, d2):
+    f = pl.program_id(0)
+    last = pl.num_programs(0) - 1
+    N = x.shape[0]
+    CW = ctx.shape[1]
+
+    @pl.when(f == 0)
+    def _():
+        yacc[...] = dnn(ctx[...], wo[...])
+        d1[...] = sum(dnt(dl[p], wqkv[:, p * CW : (p + 1) * CW]) for p in range(3))
+        d2[...] = jnp.zeros_like(d2)
+
+    yacc[...] += dnn(act[...], wd[...])
+    d2[...] += dnt(dpre[...], wu[...])
+
+    @pl.when(f == last)
+    def _():
+        ln[...] = jnp.zeros_like(ln)
+
+        @pl.loop(0, N // 128)
+        def _(i):
+            r = tile(i, 128)
+            xh, _ = normed(x[r, :])
+            a = d1[r, :]
+            b = d2[r, :]
+            y[r, :] = yacc[r, :].astype(BF)
+            g[r, :] = (a * gb[0:1, :] + b * gb[2:3, :]).astype(BF)
+            ln[0:1, :] += jnp.sum(a * xh, axis=0, keepdims=True)
+            ln[1:2, :] += jnp.sum(a, axis=0, keepdims=True)
+            ln[2:3, :] += jnp.sum(b * xh, axis=0, keepdims=True)
+            ln[3:4, :] += jnp.sum(b, axis=0, keepdims=True)
+
+
+def own_both_rows(x, act, dpre, wu, wd, dl, ctx, wqkv, wo, gb):
+    N, D = x.shape
+    FL = wu.shape[1]
+    CW = wo.shape[0]
+    fb = min(512, FL)
+    full = lambda s: pl.BlockSpec(s, lambda f: (0,) * len(s), pipeline_mode=pl.Buffered(1))
+    keep = lambda s: pl.BlockSpec(s, lambda f: (0,) * len(s))
+    rows = pl.BlockSpec((N, fb), lambda f: (0, f))
+    return pl.pallas_call(
+        own_both_kernel,
+        grid=(FL // fb,),
+        in_specs=[rows, rows, pl.BlockSpec((D, fb), lambda f: (0, f)), pl.BlockSpec((fb, D), lambda f: (f, 0))]
+        + [full((3, N, CW)), full((N, CW)), full((D, 3 * CW)), full((CW, D)), full((N, D)), full((4, D))],
+        out_specs=[keep((N, D)), keep((N, D)), keep((4, D))],
+        out_shape=[SD((N, D), BF), SD((N, D), BF), SD((4, D), F32)],
+        scratch_shapes=[pltpu.VMEM((N, D), F32)] * 3,
+        compiler_params=pltpu.CompilerParams(vmem_limit_bytes=60 * MIB),
+        cost_estimate=SMALL,
+    )(act, dpre, wu, wd, dl, ctx, wqkv, wo, x, gb)
+
+
 def final_kernel(S, first, PT, *refs):
     it = iter(refs)
     take = lambda n: [next(it) for _ in range(n)]
@@ -917,7 +971,7 @@
     away = lambda values: [shifted(v, S, j + 1) for j, v in enumerate(values)]
     cut = quarter_pieces(up_weight, me, S)
     vectors_in = (ln1_gain, ln1_bias, ln2_gain, ln2_bias, out_bias, down_bias, qkv_bias)
-    (vectors_in, qkv_weight), cut = lax.optimization_barrier(((vectors_in, qkv_weight), cut))
+    (vectors_in, qkv_weight), _ = lax.optimization_barrier(((vectors_in, qkv_weight), (cut, X[0], DY[0])))
     small = jnp.concatenate([v.reshape(-1, CW) for v in vectors_in], axis=0)
     n = D // S // R
     rep = lax.axis_index("rep")
@@ -935,6 +989,7 @@
 
     whole = jnp.stack(canonical(slots, me, S, True), axis=0)
     vec = whole[:, :6].transpose(1, 0, 2).reshape(6, D)
+    gb = vec[0:4]
     gb1 = vec[0:2]
     gb2 = vec[2:4]
     vb = vec[4:6]
@@ -951,7 +1006,7 @@
     ff = [[None] * S for _ in range(MB)]
 
     def mlp(m, j):
-        ff[m][j] = mlp_rows(X[m][j], DY[m][j], w_up, bup, down_weight, gb2, 1)
+        ff[m][j] = mlp_rows(X[m][j], DY[m][j], w_up, bup, down_weight, gb2, int((m, j) != (MB - 1, 0)))
 
     for m in range(MB):
         mlp(m, 0)
@@ -968,6 +1023,8 @@
 
     def own(m):
         f = ff[m][0]
+        if len(f) == 4:
+            return own_both_rows(X[m][0], f[0], f[1], w_up, down_weight, rest[m][0], rest[m][1], w_qkv, out_weight, gb)
         return own_rows(X[m][0], f[4], f[5], rest[m][0], rest[m][1], w_qkv, out_weight, gb1)
 
     chunked = (D // S // R) % 16 == 0 and R & (R - 1) == 0
@@ -994,8 +1051,8 @@
             w_qkv, rest[m][3] = lax.optimization_barrier((w_qkv, rest[m][3]))
     every = early + late
     def vectors(mine_):
-        ln1 = sum(r[3] for r in rest) + sum(o[2] for o in mine_)
-        ln2 = sum(of(every, 6))
+        ln1 = sum(r[3] for r in rest) + sum(o[2][0:2] for o in mine_)
+        ln2 = sum(f[6] for f in (ff[m][j] for m, j in every) if len(f) > 4) + sum(o[2][2:4] for o in mine_ if o[2].shape[0] > 2)
         db_out = sum(jnp.sum(DY[m][0].astype(F32), axis=0) for m in range(MB)).reshape(-1, CW)
         mine = (jnp.arange(S) == me).astype(F32)
         db_qkv = (sum(r[4] for r in rest)[:, None, :] * mine[None, :, None]).reshape(-1, CW)
@@ -1014,12 +1071,13 @@
         for m in range(MB):
             rest[m][0] = dls_own[m]
         mine = [own(m) for m in range(MB)]
-        beside = {1: mine}
+        beside = {1: mine[:-1]}
+        beside[2] = mine[-1:]
         levels = R.bit_length() - 1
         path = hops(vectors(mine), R)
         late_hops = {}
         for n, v in enumerate(path):
-            at = 2 + n
+            at = 3 + n
             (beside if at < levels else late_hops).setdefault(at if at < levels else max(2 * levels - 1 - at, 0), []).append(v)
         outs = None
         for m in range(MB - 1):

time: 489 us -> 479 us (0.980)
  starting transfers between devices: 46.7 us -> 39.7 us
  local copies, waits for them, and re-layouts: 32 us -> 26.7 us
    pallas_call x0 -> x1, Pallas kernels: none -> 18 us  [own_both_rows(): pl.pallas_call(own_both_kernel, grid=(FL // fb,), in_specs=[rows, rows, p...]
    pallas_call x2 -> x1, Pallas kernels: 19.7 us -> 10.9 us  [own_rows(): pl.pallas_call(own_kernel, grid=(1,), in_specs=[full((3, N, CW)), full((N...]
    pallas_call x4, Pallas kernels: 80.9 us -> 72.5 us  [mlp_rows(): pl.pallas_call(functools.partial(mlp_kernel, rows_tile(rows, 640)), grid=...]
    ppermute x22, starting transfers between devices: 30.9 us -> 24 us  [exchanged(): return lax.ppermute(value, 'rep', [(i, i ^ bit) for i in range(R)])]
    ppermute x14, waiting for transfers between devices: 11.6 us -> 18.3 us  [shifted(): return lax.ppermute(value, 'shard', [(i, (i + j) % S) for i in range(S)])]
  transfers between devices with their start and end apart: 39 -> 39, of which waited for: 13 -> 16; matrix products, arithmetic and copies ran while one was open for 11% -> 10% of each run, Pallas kernels for 54% -> 55%
where the time goes in v2:
time: 479 us; the launch traced here: 474 us
  Pallas kernels  305 us (64%)
  waiting for transfers between devices  54.6 us (11%)
  starting transfers between devices  39.7 us (8%)
  other arithmetic  33 us (7%)
  local copies, waits for them, and re-layouts  26.7 us (6%)
  between operations  15.1 us (3%)
    pallas_call x2, Pallas kernels, attn_group(): pl.pallas_call(functools.partial(attn_kernel, S, PD, CL, QB, HG, adding),...  112 us
    pallas_call x4, Pallas kernels, mlp_rows(): pl.pallas_call(functools.partial(mlp_kernel, rows_tile(rows, 640)), grid=...  72.5 us
    pallas_call x4, Pallas kernels, call(): pl.pallas_call(functools.partial(kernel, n, more), grid=(a[0].shape[1] //...  46.2 us
    ppermute x22, waiting for transfers between devices, exchanged(): return lax.ppermute(value, 'rep', [(i, i ^ bit) for i in range(R)])  36.3 us
    ppermute x22, starting transfers between devices, exchanged(): return lax.ppermute(value, 'rep', [(i, i ^ bit) for i in range(R)])  24 us
    pallas_call x1, Pallas kernels, attn_grads(): pl.pallas_call(functools.partial(attn_grads_kernel, n, S, R), grid_spec=p...  19.4 us
    ppermute x14, waiting for transfers between devices, shifted(): return lax.ppermute(value, 'shard', [(i, (i + j) % S) for i in range(S)])  18.3 us
    pallas_call x1, Pallas kernels, own_both_rows(): pl.pallas_call(own_both_kernel, grid=(FL // fb,), in_specs=[rows, rows, p...  18 us
  transfers between devices with their start and end apart: 39, of which 16 were waited for; matrix products, arithmetic and copies ran while one was open for 10% of the time, Pallas kernels for 55%

profile of v2, /device:TPU:0, one launch (start us, length us, event | category | flops | bytes accessed | tf_op | source)
XLA Modules:
  0.0 474.0 jit_solution(2700027092467523951)
XLA Ops:
  7.3 2.0 dynamic_slice.80
  9.3 2.9 collective-permute-start.2
  12.3 1.8 slice_bitcast_fusion.6
  20.4 6.4 %collective-permute-done.3 = bf16[105,512]{1,0:T(8,128)(2,1)S(1)} collective-permute-done((bf16[105,512]{1,0:T(8,128)(2,1)S(1)}, bf16[105,512]{1,0:T(8,128)(2,1)S(1)}, u32[]{:S(2)}, u32[]{:S(2)}) %collective-permute-start.3) | collective-permute-done | bytes 107552 | tf_op jit(solution)/shard_map/ppermute | solution.py:788
  26.9 1.8 collective-permute-start.4
  30.7 2.2 pad_maximum_fusion.6.x_ref.refs_0_.x
  32.8 2.6 constant_dynamic-slice_fusion.9
  35.4 4.7 collective-permute-done.4
  49.0 1.8 broadcast_select_fusion.5
  52.0 2.6 pad_maximum_fusion.wu_ref.wu
  54.6 11.6 %shard_map.308 = (bf16[640,2048]{1,0:T(8,128)(2,1)}, bf16[640,2048]{1,0:T(8,128)(2,1)}, bf16[640,1024]{1,0:T(8,128)(2,1)}, f32[1,2048]{1,0:T(1,128)}) custom-call(bf16[640,1024]{1,0:T(8,128)(2,1)} %pad_maximum_fusion.6.x_ref.refs_0_.x, bf16[640,1024]{1,0:T(8,128)(2,1)} %copy-done, bf16[1024,2048]{1,0:T(8,128)(2,1)} %pad_maximum_fusion.wu_ref.wu, ...), custom_call_target="tpu_custom_call" | custom-call | flops 5368709120 | bytes 17563648 | tf_op jit(solution)/shard_map/pallas_call | solution.py:109
  66.2 20.1 %shard_map.307 = (bf16[640,2048]{1,0:T(8,128)(2,1)}, bf16[640,2048]{1,0:T(8,128)(2,1)}, bf16[640,1024]{1,0:T(8,128)(2,1)}, f32[1,2048]{1,0:T(1,128)}, bf16[640,1...) custom-call(bf16[640,1024]{1,0:T(8,128)(2,1)} %pad_maximum_fusion.4.x_ref.refs_0_.x, ...), custom_call_target="tpu_custom_call" | custom-call | flops 5368709120 | bytes 17563648 | tf_op jit(solution)/shard_map/pallas_call | solution.py:109
  86.3 2.4 collective-permute-done.1.dy_ref.refs_4_.refs_3_.refs_7_
  88.7 20.2 %shard_map.306 = (bf16[640,2048]{1,0:T(8,128)(2,1)}, bf16[640,2048]{1,0:T(8,128)(2,1)}, bf16[640,1024]{1,0:T(8,128)(2,1)}, f32[1,2048]{1,0:T(1,128)}, bf16[640,1...) custom-call(bf16[640,1024]{1,0:T(8,128)(2,1)} %collective-permute-done.x_ref.refs_1_, ...), custom_call_target="tpu_custom_call" | custom-call | flops 5368709120 | bytes 17563648 | tf_op jit(solution)/shard_map/pallas_call | solution.py:109
  108.9 14.0 %shard_map.309.refs_6_ = bf16[16,256,1024]{2,1,0:T(8,128)(2,1)} custom-call(bf16[640,2048]{1,0:T(8,128)(2,1)} %get-tuple-element.134.refs_0_, bf16[640,2048]{1,0:T(8,128)(2,1)} %get-tuple-element.135.refs_1_, bf16[640,2048]{1,0:T(8,128)(2,1)} %get-tuple-element.136.refs_2_.act, bf16[640,1024]{1,0:T(8,128)(2,1)} %copy-done.2, ...), custom_call_target="tpu_custom_call" | custom-call | flops 1000000 | bytes 100000 | tf_op jit(solution)/shard_map/pallas_call | solution.py:491
  122.9 14.5 %shard_map.310.refs_2_ = bf16[16,256,1024]{2,1,0:T(8,128)(2,1)} custom-call(bf16[640,1024]{1,0:T(8,128)(2,1)} %get-tuple-element.128.refs_0_, bf16[640,1024]{1,0:T(8,128)(2,1)} %get-tuple-element.129.refs_1_, bf16[640,1024]{1,0:T(8,128)(2,1)} %get-tuple-element.130.refs_2_, ...), custom_call_target="tpu_custom_call", output_to_operand_aliasing={{}: (6, {})} | custom-call | flops 1000000 | bytes 100000 | tf_op jit(solution)/shard_map/pallas_call | solution.py:491
  137.4 2.0 broadcast_select_fusion.3
  139.4 2.0 pad_maximum_fusion.1.refs_6_.refs_7_.refs_8_.wqkv
  142.6 20.5 %shard_map.311 = (bf16[640,2048]{1,0:T(8,128)(2,1)}, bf16[640,2048]{1,0:T(8,128)(2,1)}, bf16[640,1024]{1,0:T(8,128)(2,1)}, f32[1,2048]{1,0:T(1,128)}, bf16[640,1...) custom-call(bf16[640,1024]{1,0:T(8,128)(2,1)} %collective-permute-done.6.x_ref.refs_1_, ...), custom_call_target="tpu_custom_call" | custom-call | flops 5368709120 | bytes 17563648 | tf_op jit(solution)/shard_map/pallas_call | solution.py:109
  163.1 9.6 %shard_map.312.refs_2_ = bf16[16,256,1024]{2,1,0:T(8,128)(2,1)} custom-call(bf16[640,2048]{1,0:T(8,128)(2,1)} %get-tuple-element.143.refs_0_, bf16[640,1024]{1,0:T(8,128)(2,1)} %collective-permute-done.7.dy_ref.refs_1_.refs_3_.refs_9_, bf16[16,256,1024]{2,1,0:T(8,128)(2,1)} %shard_map.310.refs_2_), custom_call_target="tpu_custom_call", output_to_operand_aliasing={{}: (2, {})} | custom-call | flops 1000000 | bytes 100000 | tf_op jit(solution)/shard_map/pallas_call | solution.py:491
  172.8 8.1 %shard_map.313 = bf16[16,256,1024]{2,1,0:T(8,128)(2,1)} custom-call(bf16[640,1024]{1,0:T(8,128)(2,1)} %get-tuple-element.141.refs_0_, bf16[640,2048]{1,0:T(8,128)(2,1)} %get-tuple-element.142.refs_1_, bf16[16,256,1024]{2,1,0:T(8,128)(2,1)} %shard_map.312.refs_2_), custom_call_target="tpu_custom_call", output_to_operand_aliasing={{}: (2, {})} | custom-call | flops 1000000 | bytes 100000 | tf_op jit(solution)/shard_map/pallas_call | solution.py:491
  181.6 55.9 %shard_map.314 = (bf16[640,1024]{1,0:T(8,128)(2,1)}, bf16[640,1024]{1,0:T(8,128)(2,1)}, bf16[3,1280,512]{2,1,0:T(8,128)(2,1)}, bf16[1280,512]{1,0:T(8,128)(2,1)}...) custom-call(s32[1]{0:T(128)} %bitcast.2.me_ref, ...), custom_call_target="tpu_custom_call" | custom-call | flops 1000000 | bytes 100000 | tf_op jit(solution)/shard_map/pallas_call | solution.py:386
  239.6 56.5 %shard_map.315 = (bf16[640,1024]{1,0:T(8,128)(2,1)}, bf16[640,1024]{1,0:T(8,128)(2,1)}, bf16[3,1280,512]{2,1,0:T(8,128)(2,1)}, bf16[1280,512]{1,0:T(8,128)(2,1)}...) custom-call(s32[1]{0:T(128)} %bitcast.2.me_ref, ...), custom_call_target="tpu_custom_call" | custom-call | flops 1000000 | bytes 100000 | tf_op jit(solution)/shard_map/pallas_call | solution.py:386
  299.6 2.5 collective-permute-done.10
  304.7 19.4 %shard_map.316 = (bf16[16,128,512]{2,1,0:T(8,128)(2,1)}, bf16[16,128,512]{2,1,0:T(8,128)(2,1)}) custom-call(s32[2]{0:T(128)} %pad_add_fusion.q_ref, bf16[1280,1024]{1,0:T(8,128)(2,1)} %get-tuple-element.154.refs_0_, bf16[1280,1024]{1,0:T(8,128)(2,1)} %get-tuple-element.155.refs_1_, bf16[3,1280,512]{2,1,0:T(8,128)(2,1)} %get-tuple-element.162.refs_2_.dl, ...), custom_call_target="tpu_custom_call" | custom-call | flops 1000000 | bytes 100000 | tf_op jit(solution)/shard_map/pallas_call | solution.py:582
  326.3 2.0 collective-permute-done.13
  329.5 1.6 collective-permute-start.14
  336.5 10.9 %shard_map.317 = (bf16[640,1024]{1,0:T(8,128)(2,1)}, bf16[640,1024]{1,0:T(8,128)(2,1)}, f32[2,1024]{1,0:T(2,128)}) custom-call(bf16[3,1280,512]{2,1,0:T(8,128)(2,1)} %get-tuple-element.162.refs_2_.dl, bf16[1280,512]{1,0:T(8,128)(2,1)} %get-tuple-element.158.refs_4_.ctx, bf16[1024,1536]{1,0:T(8,128)(2,1)} %pad_maximum_fusion.1.refs_6_.refs_7_.refs_8_.wqkv, ...), custom_call_target="tpu_custom_call" | custom-call | flops 1000000 | bytes 100000 | tf_op jit(solution)/shard_map/pallas_call | solution.py:667
  347.3 7.3 %collective-permute-done.14 = bf16[4,128,512]{2,1,0:T(8,128)(2,1)} collective-permute-done((bf16[4,128,512]{2,1,0:T(8,128)(2,1)}, bf16[4,128,512]{2,1,0:T(8,128)(2,1)}, u32[]{:S(2)}, u32[]{:S(2)}) %collective-permute-start.14) | collective-permute-done | bytes 524320 | tf_op jit(solution)/shard_map/ppermute | solution.py:804
  354.6 1.9 add_convert_fusion.4
  356.5 4.3 collective-permute-start.16
  360.8 1.9 add_convert_fusion.6
  362.7 2.5 collective-permute-start.15
  365.4 18.0 %shard_map.318 = (bf16[640,1024]{1,0:T(8,128)(2,1)}, bf16[640,1024]{1,0:T(8,128)(2,1)}, f32[4,1024]{1,0:T(4,128)}) custom-call(bf16[640,2048]{1,0:T(8,128)(2,1)} %get-tuple-element.136.refs_2_.act, bf16[640,2048]{1,0:T(8,128)(2,1)} %get-tuple-element.133.refs_5_.dpre, bf16[1024,2048]{1,0:T(8,128)(2,1)} %pad_maximum_fusion.wu_ref.wu, bf16[2048,1024]{1,0:T(8,128)(2,1)} %wd.1, ...), custom_call_target="tpu_custom_call" | custom-call | flops 1000000 | bytes 100000 | tf_op jit(solution)/shard_map/pallas_call | solution.py:720
  383.4 4.8 %collective-permute-done.15 = bf16[2,128,512]{2,1,0:T(8,128)(2,1)S(1)} collective-permute-done((bf16[2,128,512]{2,1,0:T(8,128)(2,1)}, bf16[2,128,512]{2,1,0:T(8,128)(2,1)S(1)}, u32[]{:S(2)}, u32[]{:S(2)}) %collective-permute-start.15) | collective-permute-done | bytes 262176 | tf_op jit(solution)/shard_map/ppermute | solution.py:804
  388.2 1.6 add_convert_fusion.11
  395.1 2.5 collective-permute-done.17
  409.6 6.7 %shard_map.319 = (bf16[2,512,1024]{2,1,0:T(8,128)(2,1)}, bf16[2,128,1024]{2,1,0:T(8,128)(2,1)}, f32[2,512,1024]{2,1,0:T(8,128)}, f32[2,128,1024]{2,1,0:T(8,128)}) custom-call(bf16[640,1024]{1,0:T(8,128)(2,1)} %pad_maximum_fusion.4.x_ref.refs_0_.x, bf16[640,1024]{1,0:T(8,128)(2,1)S(1)} %copy-done.3, bf16[640,1024]{1,0:T(8,128)(2,1)S(1)} %copy-done.10, ...), custom_call_target="tpu_custom_call" | custom-call | flops 1000000 | bytes 100000 | tf_op jit(solution)/shard_map/pallas_call | solution.py:775
  416.4 2.9 collective-permute-start.28
  419.3 2.0 collective-permute-start.29
  421.4 7.3 %collective-permute-done.29 = f32[24,512]{1,0:T(8,128)S(1)} collective-permute-done((f32[24,512]{1,0:T(8,128)S(1)}, f32[24,512]{1,0:T(8,128)S(1)}, u32[]{:S(2)}, u32[]{:S(2)}) %collective-permute-start.29) | collective-permute-done | bytes 49184 | tf_op jit(solution)/shard_map/ppermute | solution.py:804
  428.7 3.4 copy-done.5
  432.1 6.5 %shard_map.320 = (f32[2048,1024]{1,0:T(8,128)}, f32[512,4096]{1,0:T(8,128)}) custom-call(bf16[16,256,1024]{2,1,0:T(8,128)(2,1)S(1)} %bitcast.75), custom_call_target="tpu_custom_call" | custom-call | flops 1000000 | bytes 100000 | tf_op jit(solution)/shard_map/pallas_call | solution.py:524
  440.1 2.3 collective-permute-start.32
  442.4 5.0 %collective-permute-done.32 = f32[24,512]{1,0:T(8,128)S(1)} collective-permute-done((f32[24,512]{1,0:T(8,128)S(1)}, f32[24,512]{1,0:T(8,128)S(1)}, u32[]{:S(2)}, u32[]{:S(2)}) %collective-permute-start.32) | collective-permute-done | bytes 49184 | tf_op jit(solution)/shard_map/ppermute | solution.py:804
  447.4 6.1 %shard_map.321 = (bf16[2,512,1024]{2,1,0:T(8,128)(2,1)}, bf16[2,128,1024]{2,1,0:T(8,128)(2,1)}, f32[2,512,1024]{2,1,0:T(8,128)}, f32[2,128,1024]{2,1,0:T(8,128)}) custom-call(bf16[640,1024]{1,0:T(8,128)(2,1)S(1)} %copy-done.4, bf16[640,1024]{1,0:T(8,128)(2,1)S(1)} %copy-done.1, ...), custom_call_target="tpu_custom_call", output_to_operand_aliasing={{0}: (7, {}), {1}: (8, {}), {2}: (9, {}), {3}: (10, {})} | custom-call | flops 1000000 | bytes 100000 | tf_op jit(solution)/shard_map/pallas_call | solution.py:775
  454.9 3.5 collective-permute-done.33
  460.3 6.3 %shard_map.322 = (f32[512,1024]{1,0:T(8,128)}, f32[512,3072]{1,0:T(8,128)}) custom-call(s32[2]{0:T(128)S(1)} %copy-done.12, bf16[8,128,512]{2,1,0:T(8,128)(2,1)S(1)} %pad_maximum_fusion.9.refs_0_.refs_1_.refs_2_.refs_3_, bf16[8,128,512]{2,1,0:T(8,128)(2,1)S(1)} %pad_maximum_fusion.9.refs_0_.refs_1_.refs_2_.refs_3_, ...), custom_call_target="tpu_custom_call" | custom-call | flops 1000000 | bytes 100000 | tf_op jit(solution)/shard_map/pallas_call | solution.py:632
  (257 shorter events, 59.4 us)
Async XLA Ops:
  7.2 130.2 %all-gather.5.cloned.1.call-start = ((), (), s32[]{:S(2)}) async-start(), calls=%async_computation.2 | async-start | bytes 1671168 | tf_op jit(solution)/shard_map/all_gather | solution.py:837
  9.3 17.5 %collective-permute-start.2 = (bf16[128,2048]{1,0:T(8,128)(2,1)}, bf16[128,2048]{1,0:T(8,128)(2,1)}, u32[]{:S(2)}, u32[]{:S(2)}) collective-permute-start(bf16[128,2048]{1,0:T(8,128)(2,1)} %dynamic_slice.80), channel_id=1, source_target_pairs={{0,1},{1,0},{2,3},{3,2},{4,5},{5,4},{6,7},{7,6},{8,9},{9,8},{10,11... | collective-permute-start | bytes 1572872 | tf_op jit(solution)/shard_map/ppermute | solution.py:788
  20.4 6.5 %collective-permute-start.3 = (bf16[105,512]{1,0:T(8,128)(2,1)S(1)}, bf16[105,512]{1,0:T(8,128)(2,1)S(1)}, u32[]{:S(2)}, u32[]{:S(2)}) collective-permute-start(bf16[105,512]{1,0:T(8,128)(2,1)S(1)} %concatenate.73), channel_id=1, source_target_pairs={{0,1},{1,0},{2,3},{3,2},{4,5},{5,4},{6,7},{7,6},{8,9},{9,8},{10,11... | collective-permute-start | bytes 322568 | tf_op jit(solution)/shard_map/ppermute | solution.py:788
  26.9 13.3 %collective-permute-start.4 = (bf16[128,2048]{1,0:T(8,128)(2,1)}, bf16[128,2048]{1,0:T(8,128)(2,1)S(1)}, u32[]{:S(2)}, u32[]{:S(2)}) collective-permute-start(bf16[128,2048]{1,0:T(8,128)(2,1)} %collective-permute-done.2), channel_id=1, source_target_pairs={{0,4},{2,6},{4,0},{6,2},{8,12},{10,14},{12,8},{14,10},{16,20},{18,... | collective-permute-start | bytes 1572872 | tf_op jit(solution)/shard_map/ppermute | solution.py:804
  28.6 57.7 %collective-permute-start = (bf16[640,1024]{1,0:T(8,128)(2,1)}, bf16[640,1024]{1,0:T(8,128)(2,1)}, u32[]{:S(2)}, u32[]{:S(2)}) collective-permute-start(bf16[640,1024]{1,0:T(8,128)(2,1)} %pad_maximum_fusion.4.x_ref.refs_0_.x), channel_id=1, source_target_pairs={{0,1},{1,0},{2,3},{3,2},{4,5},{5,4},{6,7},{7,6},{8,9},{9,8},{10,11... | collective-permute-start | bytes 3932168 | tf_op jit(solution)/shard_map/ppermute | solution.py:788
  30.1 58.6 %collective-permute-start.1 = (bf16[640,1024]{1,0:T(8,128)(2,1)S(1)}, bf16[640,1024]{1,0:T(8,128)(2,1)}, u32[]{:S(2)}, u32[]{:S(2)}) collective-permute-start(bf16[640,1024]{1,0:T(8,128)(2,1)S(1)} %pad_maximum_fusion.5.dy_ref.refs_3_.refs_2_.refs_6_.refs_1_), channel_id=1, source_target_pairs={{0,1},{1,0},{2,3},{3,2},{4,5},{5,4},{6,7},{7,6},{8,9},{9,8},{10,11... | collective-permute-start | bytes 3932168 | tf_op jit(solution)/shard_map/ppermute | solution.py:788
  42.5 6.5 %collective-permute-start.5 = (bf16[256,2048]{1,0:T(8,128)(2,1)}, bf16[256,2048]{1,0:T(8,128)(2,1)}, u32[]{:S(2)}, u32[]{:S(2)}) collective-permute-start(bf16[256,2048]{1,0:T(8,128)(2,1)} %pad_maximum_fusion.8), channel_id=1, source_target_pairs={{0,2},{2,0},{4,6},{6,4},{8,10},{10,8},{12,14},{14,12},{16,18},{18,... | collective-permute-start | bytes 3145736 | tf_op jit(solution)/shard_map/ppermute | solution.py:804
  45.5 250.5 %reduce-scatter.2.cloned.1.call-start = ((), (), s32[]{:S(2)}) async-start(), calls=%async_computation.1 | async-start | bytes 8912896 | tf_op jit(solution)/shard_map/reduce_scatter | solution.py:1046
  46.9 94.4 %collective-permute-start.6 = (bf16[640,1024]{1,0:T(8,128)(2,1)}, bf16[640,1024]{1,0:T(8,128)(2,1)}, u32[]{:S(2)}, u32[]{:S(2)}) collective-permute-start(bf16[640,1024]{1,0:T(8,128)(2,1)} %pad_maximum_fusion.6.x_ref.refs_0_.x), channel_id=1, source_target_pairs={{0,1},{1,0},{2,3},{3,2},{4,5},{5,4},{6,7},{7,6},{8,9},{9,8},{10,11... | collective-permute-start | bytes 3932168 | tf_op jit(solution)/shard_map/ppermute | solution.py:788
  48.4 94.2 %collective-permute-start.7 = (bf16[640,1024]{1,0:T(8,128)(2,1)S(1)}, bf16[640,1024]{1,0:T(8,128)(2,1)}, u32[]{:S(2)}, u32[]{:S(2)}) collective-permute-start(bf16[640,1024]{1,0:T(8,128)(2,1)S(1)} %pad_maximum_fusion.7.dy_ref.refs_5_.refs_2_.refs_8_.refs_1_), channel_id=1, source_target_pairs={{0,1},{1,0},{2,3},{3,2},{4,5},{5,4},{6,7},{7,6},{8,9},{9,8},{10,11... | collective-permute-start | bytes 3932168 | tf_op jit(solution)/shard_map/ppermute | solution.py:788
  180.9 247.8 %all-gather.7.cloned.1.call-start = ((), (), s32[]{:S(2)}) async-start(), calls=%async_computation.3 | async-start | bytes 8912896 | tf_op jit(solution)/shard_map/all_gather | solution.py:1068
  237.5 66.4 %collective-permute-start.8 = (bf16[640,1024]{1,0:T(8,128)(2,1)}, bf16[640,1024]{1,0:T(8,128)(2,1)S(1)}, u32[]{:S(2)}, u32[]{:S(2)}) collective-permute-start(bf16[640,1024]{1,0:T(8,128)(2,1)} %get-tuple-element.152), channel_id=1, source_target_pairs={{0,1},{1,0},{2,3},{3,2},{4,5},{5,4},{6,7},{7,6},{8,9},{9,8},{10,11... | collective-permute-start | bytes 3932168 | tf_op jit(solution)/shard_map/ppermute | solution.py:788
  239.0 64.8 %collective-permute-start.9 = (bf16[640,1024]{1,0:T(8,128)(2,1)}, bf16[640,1024]{1,0:T(8,128)(2,1)}, u32[]{:S(2)}, u32[]{:S(2)}) collective-permute-start(bf16[640,1024]{1,0:T(8,128)(2,1)} %get-tuple-element.153), channel_id=1, source_target_pairs={{0,1},{1,0},{2,3},{3,2},{4,5},{5,4},{6,7},{7,6},{8,9},{9,8},{10,11... | collective-permute-start | bytes 3932168 | tf_op jit(solution)/shard_map/ppermute | solution.py:788
  297.0 5.0 %collective-permute-start.10 = (bf16[64,1024]{1,0:T(8,128)(2,1)S(1)}, bf16[64,1024]{1,0:T(8,128)(2,1)S(1)}, u32[]{:S(2)}, u32[]{:S(2)}) collective-permute-start(bf16[64,1024]{1,0:T(8,128)(2,1)S(1)} %dynamic-slice_bitcast_fusion), channel_id=1, source_target_pairs={{0,1},{1,0},{2,3},{3,2},{4,5},{5,4},{6,7},{7,6},{8,9},{9,8},{10,11... | collective-permute-start | bytes 393224 | tf_op jit(solution)/shard_map/ppermute | solution.py:788
  303.9 20.2 %copy-start.8 = (bf16[640,1024]{1,0:T(8,128)(2,1)}, bf16[640,1024]{1,0:T(8,128)(2,1)S(1)}, u32[]{:S(2)}) copy-start(bf16[640,1024]{1,0:T(8,128)(2,1)S(1)} %collective-permute-done.8.refs_3_) | copy-start | bytes 3932164
  325.6 2.7 collective-permute-start.13
  326.1 5.0 %collective-permute-start.11 = (bf16[8,128,512]{2,1,0:T(8,128)(2,1)S(1)}, bf16[8,128,512]{2,1,0:T(8,128)(2,1)S(1)}, u32[]{:S(2)}, u32[]{:S(2)}) collective-permute-start(bf16[8,128,512]{2,1,0:T(8,128)(2,1)S(1)} %slice.189), channel_id=1, source_target_pairs={{0,2},{2,0},{4,6},{6,4},{8,10},{10,8},{12,14},{14,12},{16,18},{18,... | collective-permute-start | bytes 3145736 | tf_op jit(solution)/shard_map/ppermute | solution.py:804
  329.5 25.2 %collective-permute-start.14 = (bf16[4,128,512]{2,1,0:T(8,128)(2,1)}, bf16[4,128,512]{2,1,0:T(8,128)(2,1)}, u32[]{:S(2)}, u32[]{:S(2)}) collective-permute-start(bf16[4,128,512]{2,1,0:T(8,128)(2,1)} %get-tuple-element.253), channel_id=1, source_target_pairs={{0,8},{2,10},{4,12},{6,14},{8,0},{10,2},{12,4},{14,6},{16,24},{18,... | collective-permute-start | bytes 1572872 | tf_op jit(solution)/shard_map/ppermute | solution.py:804
  332.4 22.2 %collective-permute-start.12 = (bf16[4,128,512]{2,1,0:T(8,128)(2,1)}, bf16[4,128,512]{2,1,0:T(8,128)(2,1)}, u32[]{:S(2)}, u32[]{:S(2)}) collective-permute-start(bf16[4,128,512]{2,1,0:T(8,128)(2,1)} %get-tuple-element.254), channel_id=1, source_target_pairs={{0,4},{2,6},{4,0},{6,2},{8,12},{10,14},{12,8},{14,10},{16,20},{18,... | collective-permute-start | bytes 1572872 | tf_op jit(solution)/shard_map/ppermute | solution.py:804
  334.4 59.4 %collective-permute-start.20 = (bf16[640,1024]{1,0:T(8,128)(2,1)}, bf16[640,1024]{1,0:T(8,128)(2,1)S(1)}, u32[]{:S(2)}, u32[]{:S(2)}) collective-permute-start(bf16[640,1024]{1,0:T(8,128)(2,1)} %get-tuple-element.187), channel_id=1, source_target_pairs={{0,1},{1,0},{2,3},{3,2},{4,5},{5,4},{6,7},{7,6},{8,9},{9,8},{10,11... | collective-permute-start | bytes 3932168 | tf_op jit(solution)/shard_map/ppermute | solution.py:788
  335.9 57.8 %collective-permute-start.21 = (bf16[640,1024]{1,0:T(8,128)(2,1)}, bf16[640,1024]{1,0:T(8,128)(2,1)}, u32[]{:S(2)}, u32[]{:S(2)}) collective-permute-start(bf16[640,1024]{1,0:T(8,128)(2,1)} %get-tuple-element.188), channel_id=1, source_target_pairs={{0,1},{1,0},{2,3},{3,2},{4,5},{5,4},{6,7},{7,6},{8,9},{9,8},{10,11... | collective-permute-start | bytes 3932168 | tf_op jit(solution)/shard_map/ppermute | solution.py:788
  336.4 24.4 %copy-start.28 = (bf16[4,128,512]{2,1,0:T(8,128)(2,1)S(1)}, bf16[4,128,512]{2,1,0:T(8,128)(2,1)}, u32[]{:S(2)}) copy-start(bf16[4,128,512]{2,1,0:T(8,128)(2,1)} %get-tuple-element.255) | copy-start | bytes 1572868
  356.5 26.9 %collective-permute-start.16 = (bf16[2,128,512]{2,1,0:T(8,128)(2,1)}, bf16[2,128,512]{2,1,0:T(8,128)(2,1)}, u32[]{:S(2)}, u32[]{:S(2)}) collective-permute-start(bf16[2,128,512]{2,1,0:T(8,128)(2,1)} %get-tuple-element.271), channel_id=1, source_target_pairs={{0,16},{2,18},{4,20},{6,22},{8,24},{10,26},{12,28},{14,30},{16,0},... | collective-permute-start | bytes 786440 | tf_op jit(solution)/shard_map/ppermute | solution.py:804
  362.7 25.5 %collective-permute-start.15 = (bf16[2,128,512]{2,1,0:T(8,128)(2,1)}, bf16[2,128,512]{2,1,0:T(8,128)(2,1)S(1)}, u32[]{:S(2)}, u32[]{:S(2)}) collective-permute-start(bf16[2,128,512]{2,1,0:T(8,128)(2,1)} %get-tuple-element.272), channel_id=1, source_target_pairs={{0,8},{2,10},{4,12},{6,14},{8,0},{10,2},{12,4},{14,6},{16,24},{18,... | collective-permute-start | bytes 786440 | tf_op jit(solution)/shard_map/ppermute | solution.py:804
  365.4 26.1 %copy-start.35 = (f32[2,1024]{1,0:T(2,128)S(1)}, f32[2,1024]{1,0:T(2,128)}, u32[]{:S(2)}) copy-start(f32[2,1024]{1,0:T(2,128)} %get-tuple-element.178) | copy-start | bytes 24580
  365.4 26.1 %copy-start.36 = (f32[2,1024]{1,0:T(2,128)S(1)}, f32[2,1024]{1,0:T(2,128)}, u32[]{:S(2)}) copy-start(f32[2,1024]{1,0:T(2,128)} %get-tuple-element.179) | copy-start | bytes 24580
  365.4 26.1 %copy-start.37 = (f32[2,1024]{1,0:T(2,128)S(1)}, f32[2,1024]{1,0:T(2,128)}, u32[]{:S(2)}) copy-start(f32[2,1024]{1,0:T(2,128)} %get-tuple-element.180) | copy-start | bytes 24580
  365.4 26.1 %copy-start.38 = (f32[2,1024]{1,0:T(2,128)S(1)}, f32[2,1024]{1,0:T(2,128)}, u32[]{:S(2)}) copy-start(f32[2,1024]{1,0:T(2,128)} %get-tuple-element.176) | copy-start | bytes 24580
  365.4 26.1 %copy-start.42 = (f32[2,1024]{1,0:T(2,128)S(1)}, f32[2,1024]{1,0:T(2,128)}, u32[]{:S(2)}) copy-start(f32[2,1024]{1,0:T(2,128)} %get-tuple-element.177) | copy-start | bytes 24580
  365.4 26.1 %copy-start.46 = (f32[2,1024]{1,0:T(2,128)S(1)}, f32[2,1024]{1,0:T(2,128)}, u32[]{:S(2)}) copy-start(f32[2,1024]{1,0:T(2,128)} %get-tuple-element.167) | copy-start | bytes 24580
  383.4 23.6 %copy-start.3 = (bf16[640,1024]{1,0:T(8,128)(2,1)S(1)}, bf16[640,1024]{1,0:T(8,128)(2,1)}, u32[]{:S(2)}) copy-start(bf16[640,1024]{1,0:T(8,128)(2,1)} %copy-done.2) | copy-start | bytes 3932164
  389.8 5.3 %collective-permute-start.18 = (bf16[1,128,512]{2,1,0:T(8,128)(2,1)}, bf16[1,128,512]{2,1,0:T(8,128)(2,1)}, u32[]{:S(2)}, u32[]{:S(2)}) collective-permute-start(bf16[1,128,512]{2,1,0:T(8,128)(2,1)} %add_convert_fusion.11), channel_id=1, source_target_pairs={{0,4},{2,6},{4,0},{6,2},{8,12},{10,14},{12,8},{14,10},{16,20},{18,... | collective-permute-start | bytes 393224 | tf_op jit(solution)/shard_map/ppermute | solution.py:804
  391.5 6.2 %collective-permute-start.17 = (bf16[1,128,512]{2,1,0:T(8,128)(2,1)}, bf16[1,128,512]{2,1,0:T(8,128)(2,1)}, u32[]{:S(2)}, u32[]{:S(2)}) collective-permute-start(bf16[1,128,512]{2,1,0:T(8,128)(2,1)} %add_convert_fusion.12), channel_id=1, source_target_pairs={{0,16},{2,18},{4,20},{6,22},{8,24},{10,26},{12,28},{14,30},{16,0},... | collective-permute-start | bytes 393224 | tf_op jit(solution)/shard_map/ppermute | solution.py:804
  392.4 1.3 collective-permute-start.19
  398.7 4.0 collective-permute-start.24
  401.2 4.3 collective-permute-start.22
  402.7 13.6 %collective-permute-start.25 = (bf16[1,128,512]{2,1,0:T(8,128)(2,1)S(1)}, bf16[1,128,512]{2,1,0:T(8,128)(2,1)S(1)}, u32[]{:S(2)}, u32[]{:S(2)}) collective-permute-start(bf16[1,128,512]{2,1,0:T(8,128)(2,1)S(1)} %maximum_bitcast_fusion.1), channel_id=1, source_target_pairs={{0,4},{2,6},{4,0},{6,2},{8,12},{10,14},{12,8},{14,10},{16,20},{18,... | collective-permute-start | bytes 393224 | tf_op jit(solution)/shard_map/ppermute | solution.py:804
  405.6 10.7 %collective-permute-start.23 = (bf16[1,128,512]{2,1,0:T(8,128)(2,1)S(1)}, bf16[1,128,512]{2,1,0:T(8,128)(2,1)S(1)}, u32[]{:S(2)}, u32[]{:S(2)}) collective-permute-start(bf16[1,128,512]{2,1,0:T(8,128)(2,1)S(1)} %maximum_bitcast_fusion), channel_id=1, source_target_pairs={{0,16},{2,18},{4,20},{6,22},{8,24},{10,26},{12,28},{14,30},{16,0},... | collective-permute-start | bytes 393224 | tf_op jit(solution)/shard_map/ppermute | solution.py:804
  405.8 10.5 %collective-permute-start.26 = (f32[24,512]{1,0:T(8,128)S(1)}, f32[24,512]{1,0:T(8,128)S(1)}, u32[]{:S(2)}, u32[]{:S(2)}) collective-permute-start(f32[24,512]{1,0:T(8,128)S(1)} %add.322), channel_id=1, source_target_pairs={{0,4},{2,6},{4,0},{6,2},{8,12},{10,14},{12,8},{14,10},{16,20},{18,... | collective-permute-start | bytes 147464 | tf_op jit(solution)/shard_map/ppermute | solution.py:804
  416.4 22.2 %collective-permute-start.28 = (bf16[2,128,512]{2,1,0:T(8,128)(2,1)S(1)}, bf16[2,128,512]{2,1,0:T(8,128)(2,1)S(1)}, u32[]{:S(2)}, u32[]{:S(2)}) collective-permute-start(bf16[2,128,512]{2,1,0:T(8,128)(2,1)S(1)} %pad_maximum_fusion.15), channel_id=1, source_target_pairs={{0,16},{2,18},{4,20},{6,22},{8,24},{10,26},{12,28},{14,30},{16,0},... | collective-permute-start | bytes 786440 | tf_op jit(solution)/shard_map/ppermute | solution.py:804
  419.3 19.3 %collective-permute-start.27 = (bf16[2,128,512]{2,1,0:T(8,128)(2,1)S(1)}, bf16[2,128,512]{2,1,0:T(8,128)(2,1)S(1)}, u32[]{:S(2)}, u32[]{:S(2)}) collective-permute-start(bf16[2,128,512]{2,1,0:T(8,128)(2,1)S(1)} %pad_maximum_fusion.14), channel_id=1, source_target_pairs={{0,8},{2,10},{4,12},{6,14},{8,0},{10,2},{12,4},{14,6},{16,24},{18,... | collective-permute-start | bytes 786440 | tf_op jit(solution)/shard_map/ppermute | solution.py:804
  419.3 9.3 %collective-permute-start.29 = (f32[24,512]{1,0:T(8,128)S(1)}, f32[24,512]{1,0:T(8,128)S(1)}, u32[]{:S(2)}, u32[]{:S(2)}) collective-permute-start(f32[24,512]{1,0:T(8,128)S(1)} %add.330), channel_id=1, source_target_pairs={{0,8},{2,10},{4,12},{6,14},{8,0},{10,2},{12,4},{14,6},{16,24},{18,... | collective-permute-start | bytes 147464 | tf_op jit(solution)/shard_map/ppermute | solution.py:804
  438.8 14.8 %collective-permute-start.31 = (bf16[4,128,512]{2,1,0:T(8,128)(2,1)S(1)}, bf16[4,128,512]{2,1,0:T(8,128)(2,1)S(1)}, u32[]{:S(2)}, u32[]{:S(2)}) collective-permute-start(bf16[4,128,512]{2,1,0:T(8,128)(2,1)S(1)} %pad_maximum_fusion.13), channel_id=1, source_target_pairs={{0,8},{2,10},{4,12},{6,14},{8,0},{10,2},{12,4},{14,6},{16,24},{18,... | collective-permute-start | bytes 1572872 | tf_op jit(solution)/shard_map/ppermute | solution.py:804
  439.3 14.3 %collective-permute-start.30 = (bf16[4,128,512]{2,1,0:T(8,128)(2,1)S(1)}, bf16[4,128,512]{2,1,0:T(8,128)(2,1)S(1)}, u32[]{:S(2)}, u32[]{:S(2)}) collective-permute-start(bf16[4,128,512]{2,1,0:T(8,128)(2,1)S(1)} %pad_maximum_fusion.12), channel_id=1, source_target_pairs={{0,4},{2,6},{4,0},{6,2},{8,12},{10,14},{12,8},{14,10},{16,20},{18,... | collective-permute-start | bytes 1572872 | tf_op jit(solution)/shard_map/ppermute | solution.py:804
  440.1 7.3 %collective-permute-start.32 = (f32[24,512]{1,0:T(8,128)S(1)}, f32[24,512]{1,0:T(8,128)S(1)}, u32[]{:S(2)}, u32[]{:S(2)}) collective-permute-start(f32[24,512]{1,0:T(8,128)S(1)} %add.331), channel_id=1, source_target_pairs={{0,16},{2,18},{4,20},{6,22},{8,24},{10,26},{12,28},{14,30},{16,0},... | collective-permute-start | bytes 147464 | tf_op jit(solution)/shard_map/ppermute | solution.py:804
  453.8 6.5 %collective-permute-start.35 = (bf16[8,128,512]{2,1,0:T(8,128)(2,1)S(1)}, bf16[8,128,512]{2,1,0:T(8,128)(2,1)S(1)}, u32[]{:S(2)}, u32[]{:S(2)}) collective-permute-start(bf16[8,128,512]{2,1,0:T(8,128)(2,1)S(1)} %pad_maximum_fusion.10.refs_8_.refs_9_.refs_10_.refs_11_), channel_id=1, source_target_pairs={{0,2},{2,0},{4,6},{6,4},{8,10},{10,8},{12,14},{14,12},{16,18},{18,... | collective-permute-start | bytes 3145736 | tf_op jit(solution)/shard_map/ppermute | solution.py:804
  453.9 6.4 %collective-permute-start.34 = (bf16[8,128,512]{2,1,0:T(8,128)(2,1)S(1)}, bf16[8,128,512]{2,1,0:T(8,128)(2,1)}, u32[]{:S(2)}, u32[]{:S(2)}) collective-permute-start(bf16[8,128,512]{2,1,0:T(8,128)(2,1)S(1)} %pad_maximum_fusion.9.refs_0_.refs_1_.refs_2_.refs_3_), channel_id=1, source_target_pairs={{0,2},{2,0},{4,6},{6,4},{8,10},{10,8},{12,14},{14,12},{16,18},{18,... | collective-permute-start | bytes 3145736 | tf_op jit(solution)/shard_map/ppermute | solution.py:804
  454.4 4.1 collective-permute-start.33
  (46 other events, 280.8 us)
Sparse Core Ops, SparseCore 0:
  45.7 40.9 all-gather.4
  181.0 104.8 reduce-scatter.1
  304.0 88.2 all-gather.6

commit v3 on v2

--- a/solution.py
+++ b/solution.py
@@ -137,14 +137,14 @@
     return pltpu.roll(x, (w - 8) if left else 8, 1)
 
 
-def attn_kernel(S, PD, CL, QB, HG, adding, me_ref, *refs):
+def attn_kernel(S, PD, CL, QB, HG, adding, back, me_ref, *refs):
     it = iter(refs)
     take = lambda n: [next(it) for _ in range(n)]
     stacked = S > 2
     per = 1 if stacked else S
     xs = take(per)
     dys = take(per)
-    far = 1 if stacked else S - 1
+    far = back * (1 if stacked else S - 1)
     yps = take(far * adding)
     g2s = take(far * adding)
     wq, wk, wv = take(3)
@@ -153,8 +153,14 @@
     cr, s1r, s2r = take(3)
     ys = take(far)
     gs = take(far)
-    dl, ctx, h1, ln, db = take(5)
-    yacc, dacc, q_s, k_s, v_s, dc_s, kT, vT, dk_s, dv_s = take(10)
+    dl, ctx, h1 = take(3)
+    ln = take(back)
+    (db,) = take(1)
+    sums = take(2 * back)
+    if back:
+        (ln,) = ln
+        yacc, dacc = sums
+    q_s, k_s, v_s, dc_s, kT, vT, dk_s, dv_s = take(8)
     g = pl.program_id(0)
     last = pl.num_programs(0) - 1
     me = me_ref[0]
@@ -234,7 +240,7 @@
         away(gs)[r, :] = away(g2s)[...]
 
     every_slot(proj)
-    if adding:
+    if adding and back:
         every_slot(bring, 1)
     lane = lax.broadcasted_iota(jnp.int32, (1, 128), 1)
     row_i = lax.broadcasted_iota(jnp.int32, (QB, QB), 0)
@@ -315,6 +321,8 @@
 
     for c in range(3):
         db[c : c + 1, :] = jnp.sum(dl[c].astype(F32), axis=0, keepdims=True)
+    if not back:
+        return
 
     @pl.loop(1, S)
     def _(j):
@@ -359,7 +367,7 @@
         every_slot(store, 1)
 
 
-def attn_group(S, PD, CL, me, xs, dys, yps, g2s, wqkv, bqkv, wo, gb, tabs):
+def attn_group(S, PD, CL, me, xs, dys, yps, g2s, wqkv, bqkv, wo, gb, tabs, back):
     N, D = xs[0].shape
     CW = wo.shape[0]
     T = N * S
@@ -374,17 +382,19 @@
     others = (yps, g2s)
     if not adding:
         yps, g2s = [], []
+    if not back:
+        yps, g2s, far = [], [], 0
     out_tok = SD((N, D), BF)
     part = pl.BlockSpec((N // G, D), lambda g, m: (g, 0))
     if S > 2:
         xs, dys, yps, g2s = [[jnp.stack(v, axis=0)] if v else v for v in (xs, dys, yps, g2s)]
-        tok, tok_out, per, far = full((S, N, D)), keep((S - 1, N, D)), 1, 1
+        tok, tok_out, per, far = full((S, N, D)), keep((S - 1, N, D)), 1, back
         out_tok = SD((S - 1, N, D), BF)
         part = pl.BlockSpec((S - 1, N // G, D), lambda g, m: (0, g, 0))
     wspec = lambda c: pl.BlockSpec((D, W), lambda g, m: (0, c * G + g))
     bspec = lambda c: pl.BlockSpec((1, W), lambda g, m: (0, c * G + g))
     outs = pl.pallas_call(
-        functools.partial(attn_kernel, S, PD, CL, QB, HG, adding),
+        functools.partial(attn_kernel, S, PD, CL, QB, HG, adding, back),
         grid_spec=pltpu.PrefetchScalarGridSpec(
             num_scalar_prefetch=1,
             grid=(G,),
@@ -398,19 +408,22 @@
                 pl.BlockSpec((3, T, W), lambda g, m: (0, 0, g)),
                 pl.BlockSpec((T, W), lambda g, m: (0, g)),
                 keep((T, D)),
-                keep((2, D)),
-                pl.BlockSpec((3, W), lambda g, m: (0, g)),
-            ],
-            scratch_shapes=[pltpu.VMEM((T - N, D), F32)] * 2
+            ]
+            + [keep((2, D))] * back
+            + [pl.BlockSpec((3, W), lambda g, m: (0, g))],
+            scratch_shapes=[pltpu.VMEM((T - N, D), F32)] * (2 * back)
             + [pltpu.VMEM((T, W), BF)] * 4
             + [pltpu.VMEM((128, T), BF)] * 2
             + [pltpu.VMEM((T, 128), F32)] * 2,
         ),
         out_shape=[out_tok] * (2 * far)
-        + [SD((3, T, CW), BF), SD((T, CW), BF), SD((T, D), BF), SD((2, D), F32), SD((3, CW), F32)],
+        + [SD((3, T, CW), BF), SD((T, CW), BF), SD((T, D), BF)] + [SD((2, D), F32)] * back + [SD((3, CW), F32)],
         compiler_params=pltpu.CompilerParams(vmem_limit_bytes=62 * MIB),
         cost_estimate=SMALL,
     )(me, *xs, *dys, *yps, *g2s, wqkv, wqkv, wqkv, bqkv, bqkv, bqkv, wo, gb, *tabs)
+    if not back:
+        dl, ctx, h1, db = outs
+        return [], [], [dl, ctx, h1, 0.0, db]
     ys, gs = outs[:far], outs[far : 2 * far]
     if S > 2:
         ys, gs = [[v[0][j] for j in range(S - 1)] for v in (ys, gs)]
@@ -709,7 +722,7 @@
             ln[3:4, :] += jnp.sum(b, axis=0, keepdims=True)
 
 
-def own_both_rows(x, act, dpre, wu, wd, dl, ctx, wqkv, wo, gb):
+def own_both_rows(j, x, act, dpre, wu, wd, dl, ctx, wqkv, wo, gb):
     N, D = x.shape
     FL = wu.shape[1]
     CW = wo.shape[0]
@@ -721,7 +734,11 @@
         own_both_kernel,
         grid=(FL // fb,),
         in_specs=[rows, rows, pl.BlockSpec((D, fb), lambda f: (0, f)), pl.BlockSpec((fb, D), lambda f: (f, 0))]
-        + [full((3, N, CW)), full((N, CW)), full((D, 3 * CW)), full((CW, D)), full((N, D)), full((4, D))],
+        + [
+            pl.BlockSpec((3, N, CW), lambda f: (0, j, 0), pipeline_mode=pl.Buffered(1)),
+            pl.BlockSpec((N, CW), lambda f: (j, 0), pipeline_mode=pl.Buffered(1)),
+        ]
+        + [full((D, 3 * CW)), full((CW, D)), full((N, D)), full((4, D))],
         out_specs=[keep((N, D)), keep((N, D)), keep((4, D))],
         out_shape=[SD((N, D), BF), SD((N, D), BF), SD((4, D), F32)],
         scratch_shapes=[pltpu.VMEM((N, D), F32)] * 3,
@@ -1003,10 +1020,11 @@
             X[m].append(shifted(src[m][0], S, S - j))
             DY[m].append(shifted(src[m][1], S, S - j))
 
+    chunked = (D // S // R) % 16 == 0 and R & (R - 1) == 0
     ff = [[None] * S for _ in range(MB)]
 
     def mlp(m, j):
-        ff[m][j] = mlp_rows(X[m][j], DY[m][j], w_up, bup, down_weight, gb2, int((m, j) != (MB - 1, 0)))
+        ff[m][j] = mlp_rows(X[m][j], DY[m][j], w_up, bup, down_weight, gb2, int((m, j) != (MB - 1, 0) and not (chunked and m == MB - 1)))
 
     for m in range(MB):
         mlp(m, 0)
@@ -1015,19 +1033,22 @@
 
     def attend(m):
         ys, gs, more = attn_group(
-            S, PD, CL, me_arr, X[m], DY[m], [f[4] for f in ff[m][1:]], [f[5] for f in ff[m][1:]], w_qkv, bqkv, out_weight, gb1, tabs
+            S, PD, CL, me_arr, X[m], DY[m], [f[4] for f in ff[m][1:] if len(f) > 4], [f[5] for f in ff[m][1:] if len(f) > 4], w_qkv, bqkv, out_weight, gb1, tabs, int(m < MB - 1 or not chunked)
         )
         rest.append(list(more))
-        y_got.append([shifted(ys[j - 1], S, j) for j in range(1, S)])
-        g_got.append([shifted(gs[j - 1], S, j) for j in range(1, S)])
+        y_got.append([shifted(v, S, j + 1) for j, v in enumerate(ys)])
+        g_got.append([shifted(v, S, j + 1) for j, v in enumerate(gs)])
+
+    def both_rows(m, j):
+        f = ff[m][j]
+        return own_both_rows(j, X[m][j], f[0], f[1], w_up, down_weight, rest[m][0], rest[m][1], w_qkv, out_weight, gb)
 
     def own(m):
         f = ff[m][0]
         if len(f) == 4:
-            return own_both_rows(X[m][0], f[0], f[1], w_up, down_weight, rest[m][0], rest[m][1], w_qkv, out_weight, gb)
+            return both_rows(m, 0)
         return own_rows(X[m][0], f[4], f[5], rest[m][0], rest[m][1], w_qkv, out_weight, gb1)
 
-    chunked = (D // S // R) % 16 == 0 and R & (R - 1) == 0
     rep = lax.axis_index("rep")
     late = [(MB - 1, j) for j in range(1, S)]
     early = [(m, j) for m in range(MB) for j in range(S) if (m, j) not in late]
@@ -1070,11 +1091,17 @@
         dls_own, _ = lax.optimization_barrier(([r[0] for r in rest], gatt))
         for m in range(MB):
             rest[m][0] = dls_own[m]
+        far = [both_rows(MB - 1, j) for j in range(1, S)]
+        y_got[-1], g_got[-1] = [[shifted(r[i], S, j + 1) for j, r in enumerate(far)] for i in range(2)]
+        dls_own, far_sums = lax.optimization_barrier(([r[0] for r in rest], [r[2] for r in far]))
+        for m in range(MB):
+            rest[m][0] = dls_own[m]
         mine = [own(m) for m in range(MB)]
-        beside = {1: mine[:-1]}
+        beside = {1: [far_sums] + mine[:-1]}
         beside[2] = mine[-1:]
         levels = R.bit_length() - 1
-        path = hops(vectors(mine), R)
+        beside[levels - 1] = beside.get(levels - 1, []) + [y_got[-1], g_got[-1]]
+        path = hops(vectors(mine + far), R)
         late_hops = {}
         for n, v in enumerate(path):
             at = 3 + n
@@ -1083,7 +1110,6 @@
         for m in range(MB - 1):
             outs = finals(m, mine[m], outs)
         whole_outs = finals(MB - 1, mine[-1], outs)
-        beside[levels - 1] = beside.get(levels - 1, []) + [y_got[-1], g_got[-1]]
         half = halving([(g[: R // 2], g[R // 2 :]) for g in gatt], R, beside)
         k = D // CW * (D // S // R)
         finished = mlp_finish(S, gmlp_all, FL)

time: 479 us -> 483 us (level)
  waiting for transfers between devices: 54.6 us -> 61.6 us
  starting transfers between devices: 39.7 us -> 34.5 us
    pallas_call x1 -> x2, Pallas kernels: 18 us -> 36.5 us  [own_both_rows(): pl.pallas_call(own_both_kernel, grid=(FL // fb,), in_specs=[rows, rows, p...]
    ppermute x14, waiting for transfers between devices: 18.3 us -> 34.3 us  [shifted(): return lax.ppermute(value, 'shard', [(i, (i + j) % S) for i in range(S)])]
    pallas_call x4, Pallas kernels: 72.5 us -> 63.4 us  [mlp_rows(): pl.pallas_call(functools.partial(mlp_kernel, rows_tile(rows, 640)), grid=...]
    ppermute x22, waiting for transfers between devices: 36.3 us -> 27.2 us  [exchanged(): return lax.ppermute(value, 'rep', [(i, i ^ bit) for i in range(R)])]
    pallas_call x2, Pallas kernels: 112 us -> 105 us  [attn_group(): pl.pallas_call(functools.partial(attn_kernel, S, PD, CL, QB, HG, adding,...]
  transfers between devices with their start and end apart: 39 -> 39, of which waited for: 16 -> 15; matrix products, arithmetic and copies ran while one was open for 10% -> 10% of each run, Pallas kernels for 55% -> 57%
where the time goes in v3:
time: 483 us; the launch traced here: 477 us
  Pallas kernels  306 us (63%)
  waiting for transfers between devices  61.6 us (13%)
  starting transfers between devices  34.5 us (7%)
  other arithmetic  32.9 us (7%)
  local copies, waits for them, and re-layouts  26.7 us (6%)
  between operations  15 us (3%)
    pallas_call x2, Pallas kernels, attn_group(): pl.pallas_call(functools.partial(attn_kernel, S, PD, CL, QB, HG, adding,...  105 us
    pallas_call x4, Pallas kernels, mlp_rows(): pl.pallas_call(functools.partial(mlp_kernel, rows_tile(rows, 640)), grid=...  63.4 us
    pallas_call x4, Pallas kernels, call(): pl.pallas_call(functools.partial(kernel, n, more), grid=(a[0].shape[1] //...  46.2 us
    pallas_call x2, Pallas kernels, own_both_rows(): pl.pallas_call(own_both_kernel, grid=(FL // fb,), in_specs=[rows, rows, p...  36.5 us
    ppermute x14, waiting for transfers between devices, shifted(): return lax.ppermute(value, 'shard', [(i, (i + j) % S) for i in range(S)])  34.3 us
    ppermute x22, waiting for transfers between devices, exchanged(): return lax.ppermute(value, 'rep', [(i, i ^ bit) for i in range(R)])  27.2 us
    pallas_call x1, Pallas kernels, attn_grads(): pl.pallas_call(functools.partial(attn_grads_kernel, n, S, R), grid_spec=p...  19.5 us
    ppermute x22, starting transfers between devices, exchanged(): return lax.ppermute(value, 'rep', [(i, i ^ bit) for i in range(R)])  19.4 us
  transfers between devices with their start and end apart: 39, of which 15 were waited for; matrix products, arithmetic and copies ran while one was open for 10% of the time, Pallas kernels for 57%

profile of v3, /device:TPU:0, one launch (start us, length us, event | category | flops | bytes accessed | tf_op | source)
XLA Modules:
  0.0 476.7 jit_solution(1539327127095993902)
XLA Ops:
  7.3 2.0 dynamic_slice.80
  9.3 2.9 collective-permute-start.2
  12.3 1.8 slice_bitcast_fusion.6
  20.3 6.5 %collective-permute-done.3 = bf16[105,512]{1,0:T(8,128)(2,1)S(1)} collective-permute-done((bf16[105,512]{1,0:T(8,128)(2,1)S(1)}, bf16[105,512]{1,0:T(8,128)(2,1)S(1)}, u32[]{:S(2)}, u32[]{:S(2)}) %collective-permute-start.3) | collective-permute-done | bytes 107552 | tf_op jit(solution)/shard_map/ppermute | solution.py:805
  26.9 1.8 collective-permute-start.4
  30.7 2.2 pad_maximum_fusion.6.x_ref.refs_0_.x
  32.9 2.6 constant_dynamic-slice_fusion.9
  35.5 4.7 collective-permute-done.4
  49.0 1.8 broadcast_select_fusion.5
  52.0 2.6 pad_maximum_fusion.wu_ref.wu
  54.6 11.6 %shard_map.308 = (bf16[640,2048]{1,0:T(8,128)(2,1)}, bf16[640,2048]{1,0:T(8,128)(2,1)}, bf16[640,1024]{1,0:T(8,128)(2,1)}, f32[1,2048]{1,0:T(1,128)}) custom-call(bf16[640,1024]{1,0:T(8,128)(2,1)} %pad_maximum_fusion.6.x_ref.refs_0_.x, bf16[640,1024]{1,0:T(8,128)(2,1)} %copy-done, bf16[1024,2048]{1,0:T(8,128)(2,1)} %pad_maximum_fusion.wu_ref.wu, ...), custom_call_target="tpu_custom_call" | custom-call | flops 5368709120 | bytes 17563648 | tf_op jit(solution)/shard_map/pallas_call | solution.py:109
  66.2 20.2 %shard_map.307 = (bf16[640,2048]{1,0:T(8,128)(2,1)}, bf16[640,2048]{1,0:T(8,128)(2,1)}, bf16[640,1024]{1,0:T(8,128)(2,1)}, f32[1,2048]{1,0:T(1,128)}, bf16[640,1...) custom-call(bf16[640,1024]{1,0:T(8,128)(2,1)} %pad_maximum_fusion.4.x_ref.refs_0_.x, ...), custom_call_target="tpu_custom_call" | custom-call | flops 5368709120 | bytes 17563648 | tf_op jit(solution)/shard_map/pallas_call | solution.py:109
  86.4 2.3 collective-permute-done.1.dy_ref.refs_4_.refs_3_.refs_7_
  88.7 20.1 %shard_map.306 = (bf16[640,2048]{1,0:T(8,128)(2,1)}, bf16[640,2048]{1,0:T(8,128)(2,1)}, bf16[640,1024]{1,0:T(8,128)(2,1)}, f32[1,2048]{1,0:T(1,128)}, bf16[640,1...) custom-call(bf16[640,1024]{1,0:T(8,128)(2,1)} %collective-permute-done.x_ref.refs_1_, ...), custom_call_target="tpu_custom_call" | custom-call | flops 5368709120 | bytes 17563648 | tf_op jit(solution)/shard_map/pallas_call | solution.py:109
  108.9 14.0 %shard_map.309.refs_6_ = bf16[16,256,1024]{2,1,0:T(8,128)(2,1)} custom-call(bf16[640,2048]{1,0:T(8,128)(2,1)} %get-tuple-element.133.refs_0_, bf16[640,2048]{1,0:T(8,128)(2,1)} %get-tuple-element.134.refs_1_, bf16[640,2048]{1,0:T(8,128)(2,1)} %get-tuple-element.135.refs_2_.act, bf16[640,1024]{1,0:T(8,128)(2,1)} %copy-done.2, ...), custom_call_target="tpu_custom_call" | custom-call | flops 1000000 | bytes 100000 | tf_op jit(solution)/shard_map/pallas_call | solution.py:504
  122.9 14.5 %shard_map.310.refs_2_ = bf16[16,256,1024]{2,1,0:T(8,128)(2,1)} custom-call(bf16[640,1024]{1,0:T(8,128)(2,1)} %get-tuple-element.127.refs_0_, bf16[640,1024]{1,0:T(8,128)(2,1)} %get-tuple-element.128.refs_1_, bf16[640,1024]{1,0:T(8,128)(2,1)} %get-tuple-element.129.refs_2_, ...), custom_call_target="tpu_custom_call", output_to_operand_aliasing={{}: (6, {})} | custom-call | flops 1000000 | bytes 100000 | tf_op jit(solution)/shard_map/pallas_call | solution.py:504
  137.4 2.0 broadcast_select_fusion.3
  139.4 2.0 pad_maximum_fusion.1.refs_6_.refs_7_.refs_8_.refs_4_.refs_5_.wqkv
  142.6 11.4 %shard_map.311 = (bf16[640,2048]{1,0:T(8,128)(2,1)}, bf16[640,2048]{1,0:T(8,128)(2,1)}, bf16[640,1024]{1,0:T(8,128)(2,1)}, f32[1,2048]{1,0:T(1,128)}) custom-call(bf16[640,1024]{1,0:T(8,128)(2,1)} %collective-permute-done.6.x_ref.refs_1_.x, bf16[640,1024]{1,0:T(8,128)(2,1)} %collective-permute-done.7.dy_ref.refs_1_.refs_3_.refs_9_, ...), custom_call_target="tpu_custom_call" | custom-call | flops 5368709120 | bytes 17563648 | tf_op jit(solution)/shard_map/pallas_call | solution.py:109
  154.0 9.6 %shard_map.312.refs_2_ = bf16[16,256,1024]{2,1,0:T(8,128)(2,1)} custom-call(bf16[640,2048]{1,0:T(8,128)(2,1)} %get-tuple-element.142.refs_0_.act, bf16[640,1024]{1,0:T(8,128)(2,1)} %collective-permute-done.7.dy_ref.refs_1_.refs_3_.refs_9_, bf16[16,256,1024]{2,1,0:T(8,128)(2,1)} %shard_map.310.refs_2_), custom_call_target="tpu_custom_call", output_to_operand_aliasing={{}: (2, {})} | custom-call | flops 1000000 | bytes 100000 | tf_op jit(solution)/shard_map/pallas_call | solution.py:504
  163.6 8.1 %shard_map.313 = bf16[16,256,1024]{2,1,0:T(8,128)(2,1)} custom-call(bf16[640,1024]{1,0:T(8,128)(2,1)} %get-tuple-element.140.refs_0_, bf16[640,2048]{1,0:T(8,128)(2,1)} %get-tuple-element.141.refs_1_.dpre, bf16[16,256,1024]{2,1,0:T(8,128)(2,1)} %shard_map.312.refs_2_), custom_call_target="tpu_custom_call", output_to_operand_aliasing={{}: (2, {})} | custom-call | flops 1000000 | bytes 100000 | tf_op jit(solution)/shard_map/pallas_call | solution.py:504
  172.4 56.6 %shard_map.314 = (bf16[640,1024]{1,0:T(8,128)(2,1)}, bf16[640,1024]{1,0:T(8,128)(2,1)}, bf16[3,1280,512]{2,1,0:T(8,128)(2,1)}, bf16[1280,512]{1,0:T(8,128)(2,1)}...) custom-call(s32[1]{0:T(128)} %bitcast.2.me_ref, ...), custom_call_target="tpu_custom_call" | custom-call | flops 1000000 | bytes 100000 | tf_op jit(solution)/shard_map/pallas_call | solution.py:396
  231.1 48.6 %shard_map.315 = (bf16[3,1280,512]{2,1,0:T(8,128)(2,1)}, bf16[1280,512]{1,0:T(8,128)(2,1)}, bf16[1280,1024]{1,0:T(8,128)(2,1)}, f32[3,512]{1,0:T(4,128)}) custom-call(s32[1]{0:T(128)} %bitcast.2.me_ref, bf16[640,1024]{1,0:T(8,128)(2,1)} %pad_maximum_fusion.6.x_ref.refs_0_.x, bf16[640,1024]{1,0:T(8,128)(2,1)} %collective-permute-done.6.x_ref.refs_1_.x, ...), custom_call_target="tpu_custom_call" | custom-call | flops 1000000 | bytes 100000 | tf_op jit(solution)/shard_map/pallas_call | solution.py:396
  280.6 1.6 collective-permute-start.10
  283.2 5.4 %collective-permute-done.10 = bf16[64,1024]{1,0:T(8,128)(2,1)S(1)} collective-permute-done((bf16[64,1024]{1,0:T(8,128)(2,1)S(1)}, bf16[64,1024]{1,0:T(8,128)(2,1)S(1)}, u32[]{:S(2)}, u32[]{:S(2)}) %collective-permute-start.10) | collective-permute-done | bytes 131104 | tf_op jit(solution)/shard_map/ppermute | solution.py:805
  291.2 19.5 %shard_map.316 = (bf16[16,128,512]{2,1,0:T(8,128)(2,1)}, bf16[16,128,512]{2,1,0:T(8,128)(2,1)}) custom-call(s32[2]{0:T(128)} %pad_add_fusion.q_ref, bf16[1280,1024]{1,0:T(8,128)(2,1)} %get-tuple-element.151.refs_0_, bf16[1280,1024]{1,0:T(8,128)(2,1)} %get-tuple-element.152.refs_1_, bf16[3,1280,512]{2,1,0:T(8,128)(2,1)} %get-tuple-element.162.refs_2_.dl, ...), custom_call_target="tpu_custom_call" | custom-call | flops 1000000 | bytes 100000 | tf_op jit(solution)/shard_map/pallas_call | solution.py:595
  313.0 2.0 collective-permute-done.13
  316.1 1.6 collective-permute-start.14
  321.0 17.9 %shard_map.317 = (bf16[640,1024]{1,0:T(8,128)(2,1)}, bf16[640,1024]{1,0:T(8,128)(2,1)}, f32[4,1024]{1,0:T(4,128)}) custom-call(bf16[640,2048]{1,0:T(8,128)(2,1)} %get-tuple-element.142.refs_0_.act, bf16[640,2048]{1,0:T(8,128)(2,1)} %get-tuple-element.141.refs_1_.dpre, bf16[1024,2048]{1,0:T(8,128)(2,1)} %pad_maximum_fusion.wu_ref.wu, bf16[2048,1024]{1,0:T(8,128)(2,1)} %wd.3, ...), custom_call_target="tpu_custom_call" | custom-call | flops 1000000 | bytes 100000 | tf_op jit(solution)/shard_map/pallas_call | solution.py:733
  341.0 9.9 %shard_map.318 = (bf16[640,1024]{1,0:T(8,128)(2,1)}, bf16[640,1024]{1,0:T(8,128)(2,1)}, f32[2,1024]{1,0:T(2,128)}) custom-call(bf16[3,1280,512]{2,1,0:T(8,128)(2,1)} %get-tuple-element.162.refs_2_.dl, bf16[1280,512]{1,0:T(8,128)(2,1)} %get-tuple-element.155.refs_4_.ctx, bf16[1024,1536]{1,0:T(8,128)(2,1)} %pad_maximum_fusion.1.refs_6_.refs_7_.refs_8_.refs_4_.refs_5_.wqkv, ...), custom_call_target="tpu_custom_call" | custom-call | flops 1000000 | bytes 100000 | tf_op jit(solution)/shard_map/pallas_call | solution.py:680
  350.9 1.9 add_convert_fusion.4
  352.8 2.5 collective-permute-start.16
  355.3 1.9 add_convert_fusion.6
  357.9 18.5 %shard_map.319 = (bf16[640,1024]{1,0:T(8,128)(2,1)}, bf16[640,1024]{1,0:T(8,128)(2,1)}, f32[4,1024]{1,0:T(4,128)}) custom-call(bf16[640,2048]{1,0:T(8,128)(2,1)} %get-tuple-element.135.refs_2_.act, bf16[640,2048]{1,0:T(8,128)(2,1)} %get-tuple-element.132.refs_5_.dpre, bf16[1024,2048]{1,0:T(8,128)(2,1)} %pad_maximum_fusion.wu_ref.wu, bf16[2048,1024]{1,0:T(8,128)(2,1)} %wd.3, ...), custom_call_target="tpu_custom_call" | custom-call | flops 1000000 | bytes 100000 | tf_op jit(solution)/shard_map/pallas_call | solution.py:733
  376.4 2.5 collective-permute-done.16
  379.8 1.6 add_convert_fusion.11
  385.1 12.5 %collective-permute-done.20.refs_5_ = bf16[640,1024]{1,0:T(8,128)(2,1)} collective-permute-done((bf16[640,1024]{1,0:T(8,128)(2,1)}, bf16[640,1024]{1,0:T(8,128)(2,1)}, u32[]{:S(2)}, u32[]{:S(2)}) %collective-permute-start.20) | collective-permute-done | bytes 1310752 | tf_op jit(solution)/shard_map/ppermute | solution.py:805
  403.0 1.6 collective-permute-start.25
  405.6 2.7 collective-permute-start.23
  412.4 6.4 %shard_map.320 = (bf16[2,512,1024]{2,1,0:T(8,128)(2,1)}, bf16[2,128,1024]{2,1,0:T(8,128)(2,1)}, f32[2,512,1024]{2,1,0:T(8,128)}, f32[2,128,1024]{2,1,0:T(8,128)}) custom-call(bf16[640,1024]{1,0:T(8,128)(2,1)} %pad_maximum_fusion.4.x_ref.refs_0_.x, bf16[640,1024]{1,0:T(8,128)(2,1)S(1)} %copy-done.3, bf16[640,1024]{1,0:T(8,128)(2,1)S(1)} %copy-done.10, ...), custom_call_target="tpu_custom_call" | custom-call | flops 1000000 | bytes 100000 | tf_op jit(solution)/shard_map/pallas_call | solution.py:792
  421.4 9.9 %collective-permute-done.29 = f32[24,512]{1,0:T(8,128)S(1)} collective-permute-done((f32[24,512]{1,0:T(8,128)S(1)}, f32[24,512]{1,0:T(8,128)S(1)}, u32[]{:S(2)}, u32[]{:S(2)}) %collective-permute-start.29) | collective-permute-done | bytes 49184 | tf_op jit(solution)/shard_map/ppermute | solution.py:821
  431.4 3.4 copy-done.5
  434.7 6.5 %shard_map.321 = (f32[2048,1024]{1,0:T(8,128)}, f32[512,4096]{1,0:T(8,128)}) custom-call(bf16[16,256,1024]{2,1,0:T(8,128)(2,1)S(1)} %bitcast.75), custom_call_target="tpu_custom_call" | custom-call | flops 1000000 | bytes 100000 | tf_op jit(solution)/shard_map/pallas_call | solution.py:537
  442.1 2.1 collective-permute-start.32
  444.1 5.9 %collective-permute-done.32 = f32[24,512]{1,0:T(8,128)S(1)} collective-permute-done((f32[24,512]{1,0:T(8,128)S(1)}, f32[24,512]{1,0:T(8,128)S(1)}, u32[]{:S(2)}, u32[]{:S(2)}) %collective-permute-start.32) | collective-permute-done | bytes 49184 | tf_op jit(solution)/shard_map/ppermute | solution.py:821
  450.1 6.1 %shard_map.322 = (bf16[2,512,1024]{2,1,0:T(8,128)(2,1)}, bf16[2,128,1024]{2,1,0:T(8,128)(2,1)}, f32[2,512,1024]{2,1,0:T(8,128)}, f32[2,128,1024]{2,1,0:T(8,128)}) custom-call(bf16[640,1024]{1,0:T(8,128)(2,1)S(1)} %copy-done.4, bf16[640,1024]{1,0:T(8,128)(2,1)S(1)} %copy-done.1, ...), custom_call_target="tpu_custom_call", output_to_operand_aliasing={{0}: (7, {}), {1}: (8, {}), {2}: (9, {}), {3}: (10, {})} | custom-call | flops 1000000 | bytes 100000 | tf_op jit(solution)/shard_map/pallas_call | solution.py:792
  457.1 4.1 collective-permute-done.33
  463.0 6.3 %shard_map.323 = (f32[512,1024]{1,0:T(8,128)}, f32[512,3072]{1,0:T(8,128)}) custom-call(s32[2]{0:T(128)S(1)} %copy-done.12, bf16[8,128,512]{2,1,0:T(8,128)(2,1)S(1)} %pad_maximum_fusion.9.refs_0_.refs_1_.refs_2_.refs_3_, bf16[8,128,512]{2,1,0:T(8,128)(2,1)S(1)} %pad_maximum_fusion.9.refs_0_.refs_1_.refs_2_.refs_3_, ...), custom_call_target="tpu_custom_call" | custom-call | flops 1000000 | bytes 100000 | tf_op jit(solution)/shard_map/pallas_call | solution.py:645
  (256 shorter events, 57.4 us)
Async XLA Ops:
  7.2 130.2 %all-gather.5.cloned.1.call-start = ((), (), s32[]{:S(2)}) async-start(), calls=%async_computation.2 | async-start | bytes 1671168 | tf_op jit(solution)/shard_map/all_gather | solution.py:854
  9.3 17.5 %collective-permute-start.2 = (bf16[128,2048]{1,0:T(8,128)(2,1)}, bf16[128,2048]{1,0:T(8,128)(2,1)}, u32[]{:S(2)}, u32[]{:S(2)}) collective-permute-start(bf16[128,2048]{1,0:T(8,128)(2,1)} %dynamic_slice.80), channel_id=1, source_target_pairs={{0,1},{1,0},{2,3},{3,2},{4,5},{5,4},{6,7},{7,6},{8,9},{9,8},{10,11... | collective-permute-start | bytes 1572872 | tf_op jit(solution)/shard_map/ppermute | solution.py:805
  20.3 6.6 %collective-permute-start.3 = (bf16[105,512]{1,0:T(8,128)(2,1)S(1)}, bf16[105,512]{1,0:T(8,128)(2,1)S(1)}, u32[]{:S(2)}, u32[]{:S(2)}) collective-permute-start(bf16[105,512]{1,0:T(8,128)(2,1)S(1)} %concatenate.73), channel_id=1, source_target_pairs={{0,1},{1,0},{2,3},{3,2},{4,5},{5,4},{6,7},{7,6},{8,9},{9,8},{10,11... | collective-permute-start | bytes 322568 | tf_op jit(solution)/shard_map/ppermute | solution.py:805
  26.8 18.0 %copy-start.31 = (bf16[105,512]{1,0:T(8,128)(2,1)}, bf16[105,512]{1,0:T(8,128)(2,1)S(1)}, u32[]{:S(2)}) copy-start(bf16[105,512]{1,0:T(8,128)(2,1)S(1)} %collective-permute-done.3) | copy-start | bytes 322564
  26.9 13.3 %collective-permute-start.4 = (bf16[128,2048]{1,0:T(8,128)(2,1)}, bf16[128,2048]{1,0:T(8,128)(2,1)S(1)}, u32[]{:S(2)}, u32[]{:S(2)}) collective-permute-start(bf16[128,2048]{1,0:T(8,128)(2,1)} %collective-permute-done.2), channel_id=1, source_target_pairs={{0,4},{2,6},{4,0},{6,2},{8,12},{10,14},{12,8},{14,10},{16,20},{18,... | collective-permute-start | bytes 1572872 | tf_op jit(solution)/shard_map/ppermute | solution.py:821
  28.6 57.8 %collective-permute-start = (bf16[640,1024]{1,0:T(8,128)(2,1)}, bf16[640,1024]{1,0:T(8,128)(2,1)}, u32[]{:S(2)}, u32[]{:S(2)}) collective-permute-start(bf16[640,1024]{1,0:T(8,128)(2,1)} %pad_maximum_fusion.4.x_ref.refs_0_.x), channel_id=1, source_target_pairs={{0,1},{1,0},{2,3},{3,2},{4,5},{5,4},{6,7},{7,6},{8,9},{9,8},{10,11... | collective-permute-start | bytes 3932168 | tf_op jit(solution)/shard_map/ppermute | solution.py:805
  30.1 58.6 %collective-permute-start.1 = (bf16[640,1024]{1,0:T(8,128)(2,1)S(1)}, bf16[640,1024]{1,0:T(8,128)(2,1)}, u32[]{:S(2)}, u32[]{:S(2)}) collective-permute-start(bf16[640,1024]{1,0:T(8,128)(2,1)S(1)} %pad_maximum_fusion.5.dy_ref.refs_3_.refs_2_.refs_6_.refs_1_), channel_id=1, source_target_pairs={{0,1},{1,0},{2,3},{3,2},{4,5},{5,4},{6,7},{7,6},{8,9},{9,8},{10,11... | collective-permute-start | bytes 3932168 | tf_op jit(solution)/shard_map/ppermute | solution.py:805
  42.5 6.5 %collective-permute-start.5 = (bf16[256,2048]{1,0:T(8,128)(2,1)}, bf16[256,2048]{1,0:T(8,128)(2,1)}, u32[]{:S(2)}, u32[]{:S(2)}) collective-permute-start(bf16[256,2048]{1,0:T(8,128)(2,1)} %pad_maximum_fusion.8), channel_id=1, source_target_pairs={{0,2},{2,0},{4,6},{6,4},{8,10},{10,8},{12,14},{14,12},{16,18},{18,... | collective-permute-start | bytes 3145736 | tf_op jit(solution)/shard_map/ppermute | solution.py:821
  45.6 234.1 %reduce-scatter.2.cloned.1.call-start = ((), (), s32[]{:S(2)}) async-start(), calls=%async_computation.1 | async-start | bytes 8912896 | tf_op jit(solution)/shard_map/reduce_scatter | solution.py:1067
  47.0 94.4 %collective-permute-start.6 = (bf16[640,1024]{1,0:T(8,128)(2,1)}, bf16[640,1024]{1,0:T(8,128)(2,1)}, u32[]{:S(2)}, u32[]{:S(2)}) collective-permute-start(bf16[640,1024]{1,0:T(8,128)(2,1)} %pad_maximum_fusion.6.x_ref.refs_0_.x), channel_id=1, source_target_pairs={{0,1},{1,0},{2,3},{3,2},{4,5},{5,4},{6,7},{7,6},{8,9},{9,8},{10,11... | collective-permute-start | bytes 3932168 | tf_op jit(solution)/shard_map/ppermute | solution.py:805
  48.4 94.2 %collective-permute-start.7 = (bf16[640,1024]{1,0:T(8,128)(2,1)S(1)}, bf16[640,1024]{1,0:T(8,128)(2,1)}, u32[]{:S(2)}, u32[]{:S(2)}) collective-permute-start(bf16[640,1024]{1,0:T(8,128)(2,1)S(1)} %pad_maximum_fusion.7.dy_ref.refs_5_.refs_2_.refs_8_.refs_1_), channel_id=1, source_target_pairs={{0,1},{1,0},{2,3},{3,2},{4,5},{5,4},{6,7},{7,6},{8,9},{9,8},{10,11... | collective-permute-start | bytes 3932168 | tf_op jit(solution)/shard_map/ppermute | solution.py:805
  171.7 259.6 %all-gather.7.cloned.1.call-start = ((), (), s32[]{:S(2)}) async-start(), calls=%async_computation.3 | async-start | bytes 8912896 | tf_op jit(solution)/shard_map/all_gather | solution.py:1089
  229.0 61.4 %collective-permute-start.8 = (bf16[640,1024]{1,0:T(8,128)(2,1)}, bf16[640,1024]{1,0:T(8,128)(2,1)S(1)}, u32[]{:S(2)}, u32[]{:S(2)}) collective-permute-start(bf16[640,1024]{1,0:T(8,128)(2,1)} %get-tuple-element.149), channel_id=1, source_target_pairs={{0,1},{1,0},{2,3},{3,2},{4,5},{5,4},{6,7},{7,6},{8,9},{9,8},{10,11... | collective-permute-start | bytes 3932168 | tf_op jit(solution)/shard_map/ppermute | solution.py:805
  230.6 59.9 %collective-permute-start.9 = (bf16[640,1024]{1,0:T(8,128)(2,1)}, bf16[640,1024]{1,0:T(8,128)(2,1)}, u32[]{:S(2)}, u32[]{:S(2)}) collective-permute-start(bf16[640,1024]{1,0:T(8,128)(2,1)} %get-tuple-element.150), channel_id=1, source_target_pairs={{0,1},{1,0},{2,3},{3,2},{4,5},{5,4},{6,7},{7,6},{8,9},{9,8},{10,11... | collective-permute-start | bytes 3932168 | tf_op jit(solution)/shard_map/ppermute | solution.py:805
  280.6 8.0 %collective-permute-start.10 = (bf16[64,1024]{1,0:T(8,128)(2,1)S(1)}, bf16[64,1024]{1,0:T(8,128)(2,1)S(1)}, u32[]{:S(2)}, u32[]{:S(2)}) collective-permute-start(bf16[64,1024]{1,0:T(8,128)(2,1)S(1)} %dynamic-slice_bitcast_fusion), channel_id=1, source_target_pairs={{0,1},{1,0},{2,3},{3,2},{4,5},{5,4},{6,7},{7,6},{8,9},{9,8},{10,11... | collective-permute-start | bytes 393224 | tf_op jit(solution)/shard_map/ppermute | solution.py:805
  290.4 20.3 %copy-start.8 = (bf16[640,1024]{1,0:T(8,128)(2,1)}, bf16[640,1024]{1,0:T(8,128)(2,1)S(1)}, u32[]{:S(2)}) copy-start(bf16[640,1024]{1,0:T(8,128)(2,1)S(1)} %collective-permute-done.8.refs_3_) | copy-start | bytes 3932164
  312.2 2.7 collective-permute-start.13
  312.7 5.0 %collective-permute-start.11 = (bf16[8,128,512]{2,1,0:T(8,128)(2,1)S(1)}, bf16[8,128,512]{2,1,0:T(8,128)(2,1)S(1)}, u32[]{:S(2)}, u32[]{:S(2)}) collective-permute-start(bf16[8,128,512]{2,1,0:T(8,128)(2,1)S(1)} %slice.195), channel_id=1, source_target_pairs={{0,2},{2,0},{4,6},{6,4},{8,10},{10,8},{12,14},{14,12},{16,18},{18,... | collective-permute-start | bytes 3145736 | tf_op jit(solution)/shard_map/ppermute | solution.py:821
  316.1 34.8 %collective-permute-start.14 = (bf16[4,128,512]{2,1,0:T(8,128)(2,1)}, bf16[4,128,512]{2,1,0:T(8,128)(2,1)}, u32[]{:S(2)}, u32[]{:S(2)}) collective-permute-start(bf16[4,128,512]{2,1,0:T(8,128)(2,1)} %get-tuple-element.251), channel_id=1, source_target_pairs={{0,8},{2,10},{4,12},{6,14},{8,0},{10,2},{12,4},{14,6},{16,24},{18,... | collective-permute-start | bytes 1572872 | tf_op jit(solution)/shard_map/ppermute | solution.py:821
  319.0 31.9 %collective-permute-start.12 = (bf16[4,128,512]{2,1,0:T(8,128)(2,1)}, bf16[4,128,512]{2,1,0:T(8,128)(2,1)}, u32[]{:S(2)}, u32[]{:S(2)}) collective-permute-start(bf16[4,128,512]{2,1,0:T(8,128)(2,1)} %get-tuple-element.252), channel_id=1, source_target_pairs={{0,4},{2,6},{4,0},{6,2},{8,12},{10,14},{12,8},{14,10},{16,20},{18,... | collective-permute-start | bytes 1572872 | tf_op jit(solution)/shard_map/ppermute | solution.py:821
  338.9 46.1 %collective-permute-start.19 = (bf16[640,1024]{1,0:T(8,128)(2,1)}, bf16[640,1024]{1,0:T(8,128)(2,1)S(1)}, u32[]{:S(2)}, u32[]{:S(2)}) collective-permute-start(bf16[640,1024]{1,0:T(8,128)(2,1)} %get-tuple-element.176), channel_id=1, source_target_pairs={{0,1},{1,0},{2,3},{3,2},{4,5},{5,4},{6,7},{7,6},{8,9},{9,8},{10,11... | collective-permute-start | bytes 3932168 | tf_op jit(solution)/shard_map/ppermute | solution.py:805
  340.4 57.2 %collective-permute-start.20 = (bf16[640,1024]{1,0:T(8,128)(2,1)}, bf16[640,1024]{1,0:T(8,128)(2,1)}, u32[]{:S(2)}, u32[]{:S(2)}) collective-permute-start(bf16[640,1024]{1,0:T(8,128)(2,1)} %get-tuple-element.177), channel_id=1, source_target_pairs={{0,1},{1,0},{2,3},{3,2},{4,5},{5,4},{6,7},{7,6},{8,9},{9,8},{10,11... | collective-permute-start | bytes 3932168 | tf_op jit(solution)/shard_map/ppermute | solution.py:805
  352.8 26.1 %collective-permute-start.16 = (bf16[2,128,512]{2,1,0:T(8,128)(2,1)}, bf16[2,128,512]{2,1,0:T(8,128)(2,1)}, u32[]{:S(2)}, u32[]{:S(2)}) collective-permute-start(bf16[2,128,512]{2,1,0:T(8,128)(2,1)} %get-tuple-element.269), channel_id=1, source_target_pairs={{0,16},{2,18},{4,20},{6,22},{8,24},{10,26},{12,28},{14,30},{16,0},... | collective-permute-start | bytes 786440 | tf_op jit(solution)/shard_map/ppermute | solution.py:821
  357.2 22.6 %collective-permute-start.15 = (bf16[2,128,512]{2,1,0:T(8,128)(2,1)}, bf16[2,128,512]{2,1,0:T(8,128)(2,1)S(1)}, u32[]{:S(2)}, u32[]{:S(2)}) collective-permute-start(bf16[2,128,512]{2,1,0:T(8,128)(2,1)} %get-tuple-element.270), channel_id=1, source_target_pairs={{0,8},{2,10},{4,12},{6,14},{8,0},{10,2},{12,4},{14,6},{16,24},{18,... | collective-permute-start | bytes 786440 | tf_op jit(solution)/shard_map/ppermute | solution.py:821
  357.8 25.0 %copy-start.35 = (f32[4,1024]{1,0:T(4,128)S(1)}, f32[4,1024]{1,0:T(4,128)}, u32[]{:S(2)}) copy-start(f32[4,1024]{1,0:T(4,128)} %get-tuple-element.161) | copy-start | bytes 49156
  357.8 25.0 %copy-start.36 = (f32[2,1024]{1,0:T(2,128)S(1)}, f32[2,1024]{1,0:T(2,128)}, u32[]{:S(2)}) copy-start(f32[2,1024]{1,0:T(2,128)} %get-tuple-element.179) | copy-start | bytes 24580
  357.8 25.0 %copy-start.37 = (f32[2,1024]{1,0:T(2,128)S(1)}, f32[2,1024]{1,0:T(2,128)}, u32[]{:S(2)}) copy-start(f32[2,1024]{1,0:T(2,128)} %get-tuple-element.180) | copy-start | bytes 24580
  357.8 25.0 %copy-start.38 = (f32[2,1024]{1,0:T(2,128)S(1)}, f32[2,1024]{1,0:T(2,128)}, u32[]{:S(2)}) copy-start(f32[2,1024]{1,0:T(2,128)} %get-tuple-element.178) | copy-start | bytes 24580
  357.8 25.0 %copy-start.45 = (f32[2,1024]{1,0:T(2,128)S(1)}, f32[2,1024]{1,0:T(2,128)}, u32[]{:S(2)}) copy-start(f32[2,1024]{1,0:T(2,128)} %get-tuple-element.167) | copy-start | bytes 24580
  376.4 33.4 %copy-start.3 = (bf16[640,1024]{1,0:T(8,128)(2,1)S(1)}, bf16[640,1024]{1,0:T(8,128)(2,1)}, u32[]{:S(2)}) copy-start(bf16[640,1024]{1,0:T(8,128)(2,1)} %copy-done.2) | copy-start | bytes 3932164
  381.4 16.2 %collective-permute-start.18 = (bf16[1,128,512]{2,1,0:T(8,128)(2,1)}, bf16[1,128,512]{2,1,0:T(8,128)(2,1)}, u32[]{:S(2)}, u32[]{:S(2)}) collective-permute-start(bf16[1,128,512]{2,1,0:T(8,128)(2,1)} %add_convert_fusion.11), channel_id=1, source_target_pairs={{0,4},{2,6},{4,0},{6,2},{8,12},{10,14},{12,8},{14,10},{16,20},{18,... | collective-permute-start | bytes 393224 | tf_op jit(solution)/shard_map/ppermute | solution.py:821
  382.8 14.8 %collective-permute-start.17 = (bf16[1,128,512]{2,1,0:T(8,128)(2,1)}, bf16[1,128,512]{2,1,0:T(8,128)(2,1)}, u32[]{:S(2)}, u32[]{:S(2)}) collective-permute-start(bf16[1,128,512]{2,1,0:T(8,128)(2,1)} %add_convert_fusion.12), channel_id=1, source_target_pairs={{0,16},{2,18},{4,20},{6,22},{8,24},{10,26},{12,28},{14,30},{16,0},... | collective-permute-start | bytes 393224 | tf_op jit(solution)/shard_map/ppermute | solution.py:821
  383.8 1.3 collective-permute-start.21
  383.9 25.9 %copy-start.9 = (bf16[640,1024]{1,0:T(8,128)(2,1)S(1)}, bf16[640,1024]{1,0:T(8,128)(2,1)}, u32[]{:S(2)}) copy-start(bf16[640,1024]{1,0:T(8,128)(2,1)} %copy-done.8) | copy-start | bytes 3932164
  398.7 4.3 collective-permute-start.24
  401.2 4.3 collective-permute-start.22
  403.0 15.8 %collective-permute-start.25 = (bf16[1,128,512]{2,1,0:T(8,128)(2,1)S(1)}, bf16[1,128,512]{2,1,0:T(8,128)(2,1)S(1)}, u32[]{:S(2)}, u32[]{:S(2)}) collective-permute-start(bf16[1,128,512]{2,1,0:T(8,128)(2,1)S(1)} %maximum_bitcast_fusion.1), channel_id=1, source_target_pairs={{0,4},{2,6},{4,0},{6,2},{8,12},{10,14},{12,8},{14,10},{16,20},{18,... | collective-permute-start | bytes 393224 | tf_op jit(solution)/shard_map/ppermute | solution.py:821
  405.6 13.3 %collective-permute-start.23 = (bf16[1,128,512]{2,1,0:T(8,128)(2,1)S(1)}, bf16[1,128,512]{2,1,0:T(8,128)(2,1)S(1)}, u32[]{:S(2)}, u32[]{:S(2)}) collective-permute-start(bf16[1,128,512]{2,1,0:T(8,128)(2,1)S(1)} %maximum_bitcast_fusion), channel_id=1, source_target_pairs={{0,16},{2,18},{4,20},{6,22},{8,24},{10,26},{12,28},{14,30},{16,0},... | collective-permute-start | bytes 393224 | tf_op jit(solution)/shard_map/ppermute | solution.py:821
  408.3 10.6 %collective-permute-start.26 = (f32[24,512]{1,0:T(8,128)S(1)}, f32[24,512]{1,0:T(8,128)S(1)}, u32[]{:S(2)}, u32[]{:S(2)}) collective-permute-start(f32[24,512]{1,0:T(8,128)S(1)} %add.322), channel_id=1, source_target_pairs={{0,4},{2,6},{4,0},{6,2},{8,12},{10,14},{12,8},{14,10},{16,20},{18,... | collective-permute-start | bytes 147464 | tf_op jit(solution)/shard_map/ppermute | solution.py:821
  419.0 22.3 %collective-permute-start.28 = (bf16[2,128,512]{2,1,0:T(8,128)(2,1)S(1)}, bf16[2,128,512]{2,1,0:T(8,128)(2,1)S(1)}, u32[]{:S(2)}, u32[]{:S(2)}) collective-permute-start(bf16[2,128,512]{2,1,0:T(8,128)(2,1)S(1)} %pad_maximum_fusion.15), channel_id=1, source_target_pairs={{0,16},{2,18},{4,20},{6,22},{8,24},{10,26},{12,28},{14,30},{16,0},... | collective-permute-start | bytes 786440 | tf_op jit(solution)/shard_map/ppermute | solution.py:821
  419.4 21.9 %collective-permute-start.27 = (bf16[2,128,512]{2,1,0:T(8,128)(2,1)S(1)}, bf16[2,128,512]{2,1,0:T(8,128)(2,1)S(1)}, u32[]{:S(2)}, u32[]{:S(2)}) collective-permute-start(bf16[2,128,512]{2,1,0:T(8,128)(2,1)S(1)} %pad_maximum_fusion.14), channel_id=1, source_target_pairs={{0,8},{2,10},{4,12},{6,14},{8,0},{10,2},{12,4},{14,6},{16,24},{18,... | collective-permute-start | bytes 786440 | tf_op jit(solution)/shard_map/ppermute | solution.py:821
  420.0 11.3 %collective-permute-start.29 = (f32[24,512]{1,0:T(8,128)S(1)}, f32[24,512]{1,0:T(8,128)S(1)}, u32[]{:S(2)}, u32[]{:S(2)}) collective-permute-start(f32[24,512]{1,0:T(8,128)S(1)} %add.330), channel_id=1, source_target_pairs={{0,8},{2,10},{4,12},{6,14},{8,0},{10,2},{12,4},{14,6},{16,24},{18,... | collective-permute-start | bytes 147464 | tf_op jit(solution)/shard_map/ppermute | solution.py:821
  441.4 14.9 %collective-permute-start.31 = (bf16[4,128,512]{2,1,0:T(8,128)(2,1)S(1)}, bf16[4,128,512]{2,1,0:T(8,128)(2,1)S(1)}, u32[]{:S(2)}, u32[]{:S(2)}) collective-permute-start(bf16[4,128,512]{2,1,0:T(8,128)(2,1)S(1)} %pad_maximum_fusion.13), channel_id=1, source_target_pairs={{0,8},{2,10},{4,12},{6,14},{8,0},{10,2},{12,4},{14,6},{16,24},{18,... | collective-permute-start | bytes 1572872 | tf_op jit(solution)/shard_map/ppermute | solution.py:821
  441.5 14.8 %collective-permute-start.30 = (bf16[4,128,512]{2,1,0:T(8,128)(2,1)S(1)}, bf16[4,128,512]{2,1,0:T(8,128)(2,1)S(1)}, u32[]{:S(2)}, u32[]{:S(2)}) collective-permute-start(bf16[4,128,512]{2,1,0:T(8,128)(2,1)S(1)} %pad_maximum_fusion.12), channel_id=1, source_target_pairs={{0,4},{2,6},{4,0},{6,2},{8,12},{10,14},{12,8},{14,10},{16,20},{18,... | collective-permute-start | bytes 1572872 | tf_op jit(solution)/shard_map/ppermute | solution.py:821
  442.1 8.0 %collective-permute-start.32 = (f32[24,512]{1,0:T(8,128)S(1)}, f32[24,512]{1,0:T(8,128)S(1)}, u32[]{:S(2)}, u32[]{:S(2)}) collective-permute-start(f32[24,512]{1,0:T(8,128)S(1)} %add.331), channel_id=1, source_target_pairs={{0,16},{2,18},{4,20},{6,22},{8,24},{10,26},{12,28},{14,30},{16,0},... | collective-permute-start | bytes 147464 | tf_op jit(solution)/shard_map/ppermute | solution.py:821
  456.5 6.5 %collective-permute-start.35 = (bf16[8,128,512]{2,1,0:T(8,128)(2,1)S(1)}, bf16[8,128,512]{2,1,0:T(8,128)(2,1)S(1)}, u32[]{:S(2)}, u32[]{:S(2)}) collective-permute-start(bf16[8,128,512]{2,1,0:T(8,128)(2,1)S(1)} %pad_maximum_fusion.10.refs_8_.refs_9_.refs_10_.refs_11_), channel_id=1, source_target_pairs={{0,2},{2,0},{4,6},{6,4},{8,10},{10,8},{12,14},{14,12},{16,18},{18,... | collective-permute-start | bytes 3145736 | tf_op jit(solution)/shard_map/ppermute | solution.py:821
  456.6 6.4 %collective-permute-start.34 = (bf16[8,128,512]{2,1,0:T(8,128)(2,1)S(1)}, bf16[8,128,512]{2,1,0:T(8,128)(2,1)}, u32[]{:S(2)}, u32[]{:S(2)}) collective-permute-start(bf16[8,128,512]{2,1,0:T(8,128)(2,1)S(1)} %pad_maximum_fusion.9.refs_0_.refs_1_.refs_2_.refs_3_), channel_id=1, source_target_pairs={{0,2},{2,0},{4,6},{6,4},{8,10},{10,8},{12,14},{14,12},{16,18},{18,... | collective-permute-start | bytes 3145736 | tf_op jit(solution)/shard_map/ppermute | solution.py:821
  457.1 4.1 collective-permute-start.33
  (45 other events, 239.9 us)
Sparse Core Ops, SparseCore 0:
  45.7 40.9 all-gather.4
  171.8 104.8 reduce-scatter.1
  290.6 90.4 all-gather.6
